TPU v7x, 32 devices: a whole 2x2x4 slice. The times are simulated.
32 devices in a mesh: seq: 16 (over z, y, x), fsdp: 2 (over core).
Axes of the slice: x: 2, y: 2, z: 4, core: 2. Of those that a mesh axis runs over, the one named last changes fastest.
Arguments:
- tokens: bfloat16 [2, 2, 2048, 1024], P(None, 'fsdp', 'seq'), may hold values from -6 to 6
- lengths: int32 [2, 2], replicated, may hold values from 1024 to 2048, as said below
- first_gain: bfloat16 [1024], P('fsdp'), may hold values from 0.099609375 to 1.8984375
- query_weight: bfloat16 [1024, 512], P('fsdp'), may hold values from -0.1875 to 0.1875
- key_weight: bfloat16 [1024, 512], P('fsdp'), may hold values from -0.1875 to 0.1875
- value_weight: bfloat16 [1024, 1024], P('fsdp'), may hold values from -0.1875 to 0.1875
- outgate_weight: bfloat16 [1024, 1024], P('fsdp'), may hold values from -0.1875 to 0.1875
- lowrank_in: bfloat16 [1024, 16], P('fsdp'), may hold values from -0.1875 to 0.1875
- lowrank_out: bfloat16 [16, 512], P(None, 'fsdp'), may hold values from -1.5 to 1.5
- decay_bias: bfloat16 [512], P('fsdp'), may hold values from 0 to 12
- head_gain: bfloat16 [256], P('fsdp'), may hold values from 0.099609375 to 1.8984375
- output_weight: bfloat16 [1024, 1024], P('fsdp'), may hold values from -0.1875 to 0.1875
- second_gain: bfloat16 [1024], P('fsdp'), may hold values from 0.099609375 to 1.8984375
- gate_weight: bfloat16 [1024, 2816], P('fsdp'), may hold values from -0.1875 to 0.1875
- up_weight: bfloat16 [1024, 2816], P('fsdp'), may hold values from -0.1875 to 0.1875
- down_weight: bfloat16 [2816, 1024], P('fsdp'), may hold values from -0.109375 to 0.109375
- cotangent: bfloat16 [2, 2, 2048, 1024], P(None, 'fsdp', 'seq'), may hold values from -6 to 6
Outputs:
- output: float32 [2, 2, 2048, 1024], P(None, 'fsdp', 'seq')
- tokens_grad: float32 [2, 2, 2048, 1024], P(None, 'fsdp', 'seq')
- first_gain_grad: float32 [1024], P('fsdp')
- query_weight_grad: float32 [1024, 512], P('fsdp')
- key_weight_grad: float32 [1024, 512], P('fsdp')
- value_weight_grad: float32 [1024, 1024], P('fsdp')
- outgate_weight_grad: float32 [1024, 1024], P('fsdp')
- lowrank_in_grad: float32 [1024, 16], P('fsdp')
- lowrank_out_grad: float32 [16, 512], P(None, 'fsdp')
- decay_bias_grad: float32 [512], P('fsdp')
- head_gain_grad: float32 [256], P('fsdp')
- output_weight_grad: float32 [1024, 1024], P('fsdp')
- second_gain_grad: float32 [1024], P('fsdp')
- gate_weight_grad: float32 [1024, 2816], P('fsdp')
- up_weight_grad: float32 [1024, 2816], P('fsdp')
- down_weight_grad: float32 [2816, 1024], P('fsdp')
Inputs may be any that keep to these rules, and one draw needn't show every extreme that they name: `lengths`: in every column one micro-batch's sequence has all 2048 tokens valid.
All inputs are finite; a program needn't handle non-finite values.
Results may differ from a plain program's by a relative error of at most 0.025.
Values may be sent and summed in bfloat16 or wider, within the bound.
No kernel may reach another device: no remote copies, remote signals or barrier semaphores. Data moves between devices by JAX's collectives and lax.ppermute only.
A program may use at most 576 MiB of HBM per device.

v0:
```python
from functools import partial

import jax
import jax.numpy as jnp
from jax import lax
from jax.sharding import PartitionSpec as P

HEADS = 4
SPAN = 64


HIGH = lax.Precision.HIGHEST


def carried_in(part, axis, combine, identity, reverse):
    count = lax.axis_size(axis)
    place = lax.axis_index(axis)
    ahead = count - 1 - place if reverse else place
    gathered = jax.tree.map(lambda a: lax.all_gather(a, axis), part)
    state = jax.tree.map(lambda a, e: jnp.zeros_like(a) + jnp.asarray(e, a.dtype), part, identity)

    def one(lap, state):
        source = count - 1 - lap if reverse else lap
        return combine(
            state, jax.tree.map(lambda a: lax.dynamic_index_in_dim(a, source, 0, False), gathered)
        )

    return lax.fori_loop(0, ahead, one, state)


def plain_dot(first_op, second_op):
    return jnp.dot(first_op, second_op, preferred_element_type=jnp.float32)


def left_dot(first_op, second_op):
    return lax.dot_general(
        first_op, second_op, (((0,), (0,)), ((), ())), preferred_element_type=jnp.float32
    )


def right_dot(first_op, second_op):
    return lax.dot_general(
        first_op, second_op, (((1,), (1,)), ((), ())), preferred_element_type=jnp.float32
    )


def rms_norm(value_in, gain_in, epsilon):
    return (
        value_in
        * lax.rsqrt(jnp.mean(value_in * value_in, axis=-1, keepdims=True) + epsilon)
        * gain_in
    )


def gate_norm(mixture, outgate, gain_in):
    return rms_norm(mixture, gain_in, 1e-05) * jax.nn.silu(outgate)


def block_step(carried, pieces):
    queries, key_rows, values, decays = pieces
    factor = queries.shape[-1] ** (-0.5)
    length_block = queries.shape[1]
    cumulative = jnp.cumsum(decays, axis=1)
    last_cum = cumulative[:, -1]
    row_pos = jnp.arange(length_block, dtype=jnp.int32)
    causal = (row_pos[:, None] >= row_pos[None, :]).astype(jnp.float32)[None, :, :, None, None]
    gaps = cumulative[:, :, None] - cumulative[:, None, :]
    decay_weights = jnp.exp(jnp.where(causal > 0, gaps, 0.0)) * causal
    scores = jnp.sum(queries[:, :, None] * key_rows[:, None] * decay_weights, axis=-1)
    within = jnp.einsum("pijh,pjhv->pihv", scores, values, precision=HIGH)
    cross = jnp.einsum("pihk,phkv->pihv", queries * jnp.exp(cumulative), carried, precision=HIGH)
    updated = jnp.exp(last_cum)[..., None] * carried + jnp.einsum(
        "pjhk,pjhv->phkv",
        key_rows * jnp.exp(last_cum[:, None] - cumulative),
        values,
        precision=HIGH,
    )
    return (updated, (within + cross) * factor)


def local_mix(queries, key_rows, values, decays):
    pair_count, tok_count = (queries.shape[0], queries.shape[1])

    def to_blocks(array):
        return jnp.moveaxis(
            array.reshape((pair_count, tok_count // SPAN, SPAN) + array.shape[2:]), 1, 0
        )

    start_state = jnp.zeros(
        (pair_count, queries.shape[2], queries.shape[3], values.shape[3]), jnp.float32
    )
    closing, outputs = lax.scan(
        block_step,
        start_state,
        (to_blocks(queries), to_blocks(key_rows), to_blocks(values), to_blocks(decays)),
    )
    mixture = jnp.moveaxis(outputs, 0, 1).reshape(values.shape)
    return (mixture, jnp.exp(jnp.sum(decays, axis=1)), closing)


def lift_states(queries, decays, entering):
    factor = queries.shape[-1] ** (-0.5)
    lifted = queries * jnp.exp(jnp.cumsum(decays, axis=1))
    return jnp.einsum("pthk,phkv->pthv", lifted, entering, precision=HIGH) * factor


def forward_combine(earlier, later):
    return (earlier[0] * later[0], later[0][..., None] * earlier[1] + later[1])


def backward_combine(earlier, later):
    return (earlier[0] * later[0], later[1] + later[0][..., None] * earlier[1])


def shards(
    tokens,
    lengths,
    first_gain,
    query_weight,
    key_weight,
    value_weight,
    outgate_weight,
    lowrank_in,
    lowrank_out,
    decay_bias,
    head_gain,
    output_weight,
    second_gain,
    gate_weight,
    up_weight,
    down_weight,
    cotangent,
):
    micro_count, pair_count, tok_count, model_width = tokens.shape
    row_count = pair_count * tok_count
    group_index = lax.axis_index("fsdp")
    place_index = lax.axis_index("seq")
    own_lengths = lax.dynamic_slice_in_dim(lengths, group_index * pair_count, pair_count, 1)
    positions = place_index * tok_count + jnp.arange(tok_count, dtype=jnp.int32)
    norm_model = partial(rms_norm, epsilon=1e-06)
    heads_shape = (pair_count, tok_count, HEADS, -1)
    results = []
    input_grads = []
    gradients = []
    for micro_step in range(micro_count):
        fetched = (
            lax.all_gather(first_gain, "fsdp", axis=0, tiled=True),
            lax.all_gather(query_weight, "fsdp", axis=0, tiled=True),
            lax.all_gather(key_weight, "fsdp", axis=0, tiled=True),
            lax.all_gather(value_weight, "fsdp", axis=0, tiled=True),
            lax.all_gather(outgate_weight, "fsdp", axis=0, tiled=True),
            lax.all_gather(lowrank_in, "fsdp", axis=0, tiled=True),
            lax.all_gather(lowrank_out, "fsdp", axis=1, tiled=True),
            lax.all_gather(decay_bias, "fsdp", axis=0, tiled=True),
            lax.all_gather(head_gain, "fsdp", axis=0, tiled=True),
            lax.all_gather(output_weight, "fsdp", axis=0, tiled=True),
            lax.all_gather(second_gain, "fsdp", axis=0, tiled=True),
            lax.all_gather(gate_weight, "fsdp", axis=0, tiled=True),
            lax.all_gather(up_weight, "fsdp", axis=0, tiled=True),
            lax.all_gather(down_weight, "fsdp", axis=0, tiled=True),
        )
        if micro_step == 0:
            gradients = [jnp.zeros(array.shape, jnp.float32) for array in fetched]
        inputs = tokens[micro_step].reshape(row_count, model_width).astype(jnp.float32)
        normed, first_back = jax.vjp(norm_model, inputs, fetched[0].astype(jnp.float32))
        normed_low = normed.astype(jnp.bfloat16)
        queries = plain_dot(normed_low, fetched[1]).astype(jnp.bfloat16)
        key_rows = plain_dot(normed_low, fetched[2]).astype(jnp.bfloat16)
        value_rows = plain_dot(normed_low, fetched[3]).astype(jnp.bfloat16)
        outgate = plain_dot(normed_low, fetched[4])
        lowrank = plain_dot(normed_low, fetched[5]).astype(jnp.bfloat16)
        logits = plain_dot(lowrank, fetched[6]) + fetched[7].astype(jnp.float32)
        decays = jax.nn.log_sigmoid(logits) / 16.0
        query_heads = queries.astype(jnp.float32).reshape(heads_shape)
        key_heads = key_rows.astype(jnp.float32).reshape(heads_shape)
        value_heads = value_rows.astype(jnp.float32).reshape(heads_shape)
        decay_heads = decays.reshape(heads_shape)
        (mix_local, decay_total, state_total), mix_back = jax.vjp(
            local_mix, query_heads, key_heads, value_heads, decay_heads
        )
        entering = carried_in(
            (decay_total, state_total),
            "seq",
            forward_combine,
            (jnp.ones_like(decay_total), jnp.zeros_like(state_total)),
            False,
        )[1]
        correction, lift_back = jax.vjp(lift_states, query_heads, decay_heads, entering)
        mixture = mix_local + correction
        gated_out, gate_back = jax.vjp(
            gate_norm, mixture, outgate.reshape(heads_shape), fetched[8].astype(jnp.float32)
        )
        gated_low = gated_out.reshape(row_count, -1).astype(jnp.bfloat16)
        hidden = inputs + plain_dot(gated_low, fetched[9])
        second_normed, second_back = jax.vjp(norm_model, hidden, fetched[10].astype(jnp.float32))
        second_low = second_normed.astype(jnp.bfloat16)
        gate_proj = plain_dot(second_low, fetched[11])
        up_proj = plain_dot(second_low, fetched[12])
        hidden_act = (jax.nn.silu(gate_proj) * up_proj).astype(jnp.bfloat16)
        valid_mask = (positions[None, :] < own_lengths[micro_step][:, None]).astype(jnp.float32)
        valid_rows = valid_mask.reshape(row_count, 1)
        result = (hidden + plain_dot(hidden_act, fetched[13])) * valid_rows
        results.append(result.reshape(pair_count, tok_count, model_width))
        back_weights = (
            lax.all_gather(first_gain, "fsdp", axis=0, tiled=True),
            lax.all_gather(query_weight, "fsdp", axis=0, tiled=True),
            lax.all_gather(key_weight, "fsdp", axis=0, tiled=True),
            lax.all_gather(value_weight, "fsdp", axis=0, tiled=True),
            lax.all_gather(outgate_weight, "fsdp", axis=0, tiled=True),
            lax.all_gather(lowrank_in, "fsdp", axis=0, tiled=True),
            lax.all_gather(lowrank_out, "fsdp", axis=1, tiled=True),
            lax.all_gather(decay_bias, "fsdp", axis=0, tiled=True),
            lax.all_gather(head_gain, "fsdp", axis=0, tiled=True),
            lax.all_gather(output_weight, "fsdp", axis=0, tiled=True),
            lax.all_gather(second_gain, "fsdp", axis=0, tiled=True),
            lax.all_gather(gate_weight, "fsdp", axis=0, tiled=True),
            lax.all_gather(up_weight, "fsdp", axis=0, tiled=True),
            lax.all_gather(down_weight, "fsdp", axis=0, tiled=True),
        )
        cot_rows = (
            cotangent[micro_step].reshape(row_count, model_width).astype(jnp.float32) * valid_rows
        )
        cot_low = cot_rows.astype(jnp.bfloat16)
        gradients[13] = gradients[13] + left_dot(hidden_act, cot_low)
        act_grad = right_dot(cot_low, back_weights[13])
        gate_sig = jax.nn.sigmoid(gate_proj)
        gate_grad = (act_grad * up_proj * gate_sig * (1.0 + gate_proj * (1.0 - gate_sig))).astype(
            jnp.bfloat16
        )
        up_grad = (act_grad * jax.nn.silu(gate_proj)).astype(jnp.bfloat16)
        gradients[11] = gradients[11] + left_dot(second_low, gate_grad)
        gradients[12] = gradients[12] + left_dot(second_low, up_grad)
        second_grad = right_dot(gate_grad, back_weights[11]) + right_dot(up_grad, back_weights[12])
        hidden_part, gain_two_grad = second_back(second_grad)
        gradients[10] = gradients[10] + gain_two_grad
        hidden_grad = cot_rows + hidden_part
        hidden_low = hidden_grad.astype(jnp.bfloat16)
        gradients[9] = gradients[9] + left_dot(gated_low, hidden_low)
        gated_grad = right_dot(hidden_low, back_weights[9]).reshape(gated_out.shape)
        mixture_grad, outgate_grad, headgain_grad = gate_back(gated_grad)
        gradients[8] = gradients[8] + headgain_grad
        lift_query, lift_decay, local_states = lift_back(mixture_grad)
        leaving = carried_in(
            (decay_total, local_states),
            "seq",
            backward_combine,
            (jnp.ones_like(decay_total), jnp.zeros_like(local_states)),
            True,
        )[1]
        total_grad = jnp.sum(leaving * entering, axis=-1)
        mix_query, mix_key, mix_value, mix_decay = mix_back((mixture_grad, total_grad, leaving))
        query_grad = (mix_query + lift_query).reshape(row_count, -1).astype(jnp.bfloat16)
        key_grad = mix_key.reshape(row_count, -1).astype(jnp.bfloat16)
        value_grad = mix_value.reshape(row_count, -1).astype(jnp.bfloat16)
        outgate_low = outgate_grad.reshape(row_count, -1).astype(jnp.bfloat16)
        logit_grad = (
            (mix_decay + lift_decay).reshape(row_count, -1) * jax.nn.sigmoid(-logits) / 16.0
        )
        gradients[7] = gradients[7] + jnp.sum(logit_grad, axis=0)
        logit_low = logit_grad.astype(jnp.bfloat16)
        gradients[6] = gradients[6] + left_dot(lowrank, logit_low)
        lowrank_grad = right_dot(logit_low, back_weights[6]).astype(jnp.bfloat16)
        gradients[5] = gradients[5] + left_dot(normed_low, lowrank_grad)
        gradients[1] = gradients[1] + left_dot(normed_low, query_grad)
        gradients[2] = gradients[2] + left_dot(normed_low, key_grad)
        gradients[3] = gradients[3] + left_dot(normed_low, value_grad)
        gradients[4] = gradients[4] + left_dot(normed_low, outgate_low)
        normed_total = (
            right_dot(query_grad, back_weights[1])
            + right_dot(key_grad, back_weights[2])
            + right_dot(value_grad, back_weights[3])
            + right_dot(outgate_low, back_weights[4])
            + right_dot(lowrank_grad, back_weights[5])
        )
        input_part, gain_one_grad = first_back(normed_total)
        gradients[0] = gradients[0] + gain_one_grad
        input_grads.append((hidden_grad + input_part).reshape(pair_count, tok_count, model_width))
    halves = (
        lax.psum_scatter(gradients[0], "fsdp", scatter_dimension=0, tiled=True),
        lax.psum_scatter(gradients[1], "fsdp", scatter_dimension=0, tiled=True),
        lax.psum_scatter(gradients[2], "fsdp", scatter_dimension=0, tiled=True),
        lax.psum_scatter(gradients[3], "fsdp", scatter_dimension=0, tiled=True),
        lax.psum_scatter(gradients[4], "fsdp", scatter_dimension=0, tiled=True),
        lax.psum_scatter(gradients[5], "fsdp", scatter_dimension=0, tiled=True),
        lax.psum_scatter(gradients[6], "fsdp", scatter_dimension=1, tiled=True),
        lax.psum_scatter(gradients[7], "fsdp", scatter_dimension=0, tiled=True),
        lax.psum_scatter(gradients[8], "fsdp", scatter_dimension=0, tiled=True),
        lax.psum_scatter(gradients[9], "fsdp", scatter_dimension=0, tiled=True),
        lax.psum_scatter(gradients[10], "fsdp", scatter_dimension=0, tiled=True),
        lax.psum_scatter(gradients[11], "fsdp", scatter_dimension=0, tiled=True),
        lax.psum_scatter(gradients[12], "fsdp", scatter_dimension=0, tiled=True),
        lax.psum_scatter(gradients[13], "fsdp", scatter_dimension=0, tiled=True),
    )
    totals = lax.psum(
        (
            halves[0],
            halves[1],
            halves[2],
            halves[3],
            halves[4],
            halves[5],
            halves[6],
            halves[7],
            halves[8],
            halves[9],
            halves[10],
            halves[11],
            halves[12],
            halves[13],
        ),
        "seq",
    )
    return (
        jnp.stack(results),
        jnp.stack(input_grads),
        totals[0],
        totals[1],
        totals[2],
        totals[3],
        totals[4],
        totals[5],
        totals[6],
        totals[7],
        totals[8],
        totals[9],
        totals[10],
        totals[11],
        totals[12],
        totals[13],
    )


def solution(mesh):
    return jax.shard_map(
        shards,
        mesh=mesh,
        in_specs=(
            P(None, "fsdp", "seq", None),
            P(),
            P("fsdp"),
            P("fsdp", None),
            P("fsdp", None),
            P("fsdp", None),
            P("fsdp", None),
            P("fsdp", None),
            P(None, "fsdp"),
            P("fsdp"),
            P("fsdp"),
            P("fsdp", None),
            P("fsdp"),
            P("fsdp", None),
            P("fsdp", None),
            P("fsdp", None),
            P(None, "fsdp", "seq", None),
        ),
        out_specs=(
            P(None, "fsdp", "seq", None),
            P(None, "fsdp", "seq", None),
            P("fsdp"),
            P("fsdp", None),
            P("fsdp", None),
            P("fsdp", None),
            P("fsdp", None),
            P("fsdp", None),
            P(None, "fsdp"),
            P("fsdp"),
            P("fsdp"),
            P("fsdp", None),
            P("fsdp"),
            P("fsdp", None),
            P("fsdp", None),
            P("fsdp", None),
        ),
        check_vma=False,
    )
```

profile of v0, /device:TPU:0, one launch (start us, length us, event | category | flops | bytes accessed | tf_op | source)
XLA Modules:
  0.0 1887.4 jit_solution(17586470216942298816)
XLA Ops:
  27.2 5.9 all-gather.21.cloned.1.call-done
  34.8 11.6 all-gather.23.cloned.1.call-done
  49.0 6.3 broadcast.1091.clone.3
  55.3 6.3 broadcast.1091.clone.4
  61.6 6.3 broadcast.1091.clone.5
  76.2 103.2 %while.187 = (s32[]{:T(128)}, f32[1,4,128,256]{3,2,1,0:T(8,128)S(1)}, f32[2,1,64,4,256]{4,2,0,3,1:T(8,128)}, f32[2,1,64,64,4,128]{5,4,3,2,1,0:T(4,128)}, f32[2,1...) while((s32[]{:T(128)}, ...), condition=%wide.region_15.16_spmd.clone.clone, body=%wide.region_12.15_spmd.clone.clone.sunk | while | flops 275668992 | bytes 42143784 | solution.py:92
  77.7 5.4 multiply_dynamic-update-slice_fusion.18
  83.8 15.7 multiply_reduce_fusion.27
  112.8 13.9 multiply_dynamic-update-slice_fusion.17
  129.2 5.5 multiply_dynamic-update-slice_fusion.18
  135.4 15.7 multiply_reduce_fusion.27
  164.5 13.9 multiply_dynamic-update-slice_fusion.17
  193.2 6.2 broadcast.1091.clone
  199.4 6.2 broadcast.1091.clone.1
  205.6 6.2 broadcast.1091.clone.2
  220.1 94.8 %while.186 = (s32[]{:T(128)}, f32[1,4,128,256]{3,2,1,0:T(8,128)S(1)}, f32[2,1,64,4,256]{4,2,0,3,1:T(8,128)}, f32[2,1,64,64,4,128]{5,4,3,2,1,0:T(4,128)}, f32[2,1...) while((s32[]{:T(128)}, ...), condition=%wide.region_4.5_spmd.clone.clone, body=%wide.region_1.4_spmd.clone.clone.sunk | while | flops 275668992 | bytes 44241020 | solution.py:92
  221.7 5.4 multiply_dynamic-update-slice_fusion.15
  227.2 15.7 multiply_reduce_fusion.26
  254.0 12.6 multiply_dynamic-update-slice_fusion.14
  269.1 5.5 multiply_dynamic-update-slice_fusion.15
  274.6 15.7 multiply_reduce_fusion.26
  301.4 12.6 multiply_dynamic-update-slice_fusion.14
  321.3 41.8 %all_gather.129 = f32[16,1,4,128]{3,2,1,0:T(4,128)S(1)} all-gather(f32[1,1,4,128]{3,2,1,0:T(4,128)S(1)} %exponential_bitcast_fusion), channel_id=1, replica_groups=mesh['seq'=16,'fsdp'=2] {'seq'}, dimensions={0}, use_global_device_ids=true | all-gather | bytes 34816 | tf_op jit(solution)/shard_map/all_gather | solution.py:19
  365.9 36.6 %all_gather.55 = f32[16,1,4,128]{3,2,1,0:T(4,128)S(1)} all-gather(f32[1,1,4,128]{3,2,1,0:T(4,128)S(1)} %exponential_bitcast_fusion.1), channel_id=1, replica_groups=mesh['seq'=16,'fsdp'=2] {'seq'}, dimensions={0}, use_global_device_ids=true | all-gather | bytes 34816 | tf_op jit(solution)/shard_map/all_gather | solution.py:19
  418.1 12.2 all-gather.37.cloned.1.call-done
  433.8 3.5 multiply_convert_fusion.9
  437.3 3.4 all-gather.29.cloned.1.call-done
  445.5 14.0 all-gather.31.cloned.1.call-done
  459.5 4.7 fusion.335
  464.1 14.1 all-gather.33.cloned.1.call-done
  478.2 4.7 fusion.336
  482.9 13.9 all-gather.35.cloned.1.call-done
  496.8 6.6 multiply_convert_fusion.2
  503.4 5.2 fusion.339
  514.7 3.4 multiply_convert_fusion
  543.0 3.5 convolution_add_fusion.6
  546.6 98.8 %all-gather.41.cloned.1.call-done = f32[16,4,128,256]{3,2,1,0:T(8,128)} async-done(((f32[1,4,128,256]{3,2,1,0:T(8,128)}), f32[16,4,128,256]{3,2,1,0:T(8,128)}) %all-gather.41.cloned.1.call-update) | async-done | bytes 8388624 | tf_op jit(solution)/shard_map/all_gather | solution.py:19
  645.4 19.2 %while.182 = (s32[]{:T(128)}, f32[1,4,128,256]{3,2,1,0:T(8,128)S(1)}, s32[]{:T(128)}, f32[16,1,4,128,256]{4,3,2,1,0:T(8,128)}, f32[16,1,4,128]{3,2,1,0:T(4,128)S...) while((s32[]{:T(128)}, f32[1,4,128,256]{3,2,1,0:T(8,128)S(1)}, s32[]{:T(128)}, ...), condition=%wide.region_25.26_spmd, body=%wide.region_24.25_spmd.sunk | while | flops 262150 | bytes 1579155 | solution.py:28
  667.7 78.4 %while.184 = (s32[]{:T(128)}, f32[1,4,128,256]{2,3,1,0:T(8,128)S(1)}, f32[2,1,64,4,128]{4,2,0,3,1:T(8,128)}, bf16[2,1,64,4,128]{4,2,3,1,0:T(8,128)(2,1)}, bf16[2...) while((s32[]{:T(128)}, ...), condition=%wide.region_34.35_spmd.clone, body=%wide.region_26.34_spmd.clone.sunk | while | flops 529735680 | bytes 72808056 | solution.py:92
  671.6 19.6 %multiply_reduce_fusion.24 = (f32[64,4,128]{2,1,0:T(4,128)S(1)}, f32[64,4,128]{2,1,0:T(4,128)}, f32[1,64,64,4,128]{4,3,2,1,0:T(4,128)}) fusion(f32[2,1,64,64,4,128]{5,4,3,2,1,0:T(4,128)} %get-tuple-element.3894, s32[]{:T(128)S(6)} %sub.344, f32[64,4,128]{2,1,0:T(4,128)S(1)} %dynamic-slice_bitcast_fusion.28, f32[64,64,4]{2,1,0:T(8,128)S(1)} %copy.562, ...), kind=kLoop, calls=%fused_computation.21.clone.1 | loop fusion | flops 18808832 | bytes 34164740 | tf_op jit(solution)/shard_map/transpose(jvp())/while/body/eval_jaxpr/reduce_sum | solution.py:69
  697.6 6.0 fusion.502
  710.8 19.6 %multiply_reduce_fusion.24 = (f32[64,4,128]{2,1,0:T(4,128)S(1)}, f32[64,4,128]{2,1,0:T(4,128)}, f32[1,64,64,4,128]{4,3,2,1,0:T(4,128)}) fusion(f32[2,1,64,64,4,128]{5,4,3,2,1,0:T(4,128)} %get-tuple-element.3894, s32[]{:T(128)S(6)} %sub.344, f32[64,4,128]{2,1,0:T(4,128)S(1)} %dynamic-slice_bitcast_fusion.28, f32[64,64,4]{2,1,0:T(8,128)S(1)} %copy.562, ...), kind=kLoop, calls=%fused_computation.21.clone.1 | loop fusion | flops 18808832 | bytes 34164740 | tf_op jit(solution)/shard_map/transpose(jvp())/while/body/eval_jaxpr/reduce_sum | solution.py:69
  736.8 6.0 fusion.502
  746.1 13.4 all-gather.43.cloned.1.call-done
  759.6 29.3 %while.183 = (s32[]{:T(128)}, f32[1,4,128,256]{3,2,1,0:T(8,128)S(1)}, s32[]{:T(128)}, f32[16,1,4,128,256]{4,3,2,1,0:T(8,128)}, f32[16,1,4,128]{3,2,1,0:T(4,128)}...) while((s32[]{:T(128)}, f32[1,4,128,256]{3,2,1,0:T(8,128)S(1)}, s32[]{:T(128)}, ...), condition=%wide.region_41.42_spmd, body=%wide.region_40.41_spmd.sunk | while | flops 262150 | bytes 1579155 | solution.py:28
  792.8 75.4 %while.185 = (s32[]{:T(128)}, f32[1,4,128,256]{2,3,1,0:T(8,128)S(1)}, f32[2,1,64,4,128]{4,2,0,3,1:T(8,128)}, bf16[2,1,64,4,128]{4,2,3,1,0:T(8,128)(2,1)}, bf16[2...) while((s32[]{:T(128)}, ...), condition=%wide.region_50.51_spmd.clone, body=%wide.region_42.50_spmd.clone.sunk | while | flops 529735680 | bytes 70710880 | solution.py:92
  795.8 18.9 %multiply_reduce_fusion.25 = (f32[64,4,128]{2,1,0:T(4,128)S(1)}, f32[64,4,128]{2,1,0:T(4,128)S(1)}, f32[1,64,64,4,128]{4,3,2,1,0:T(4,128)}) fusion(f32[2,1,64,64,4,128]{5,4,3,2,1,0:T(4,128)} %get-tuple-element.3792, s32[]{:T(128)S(6)} %sub.345, f32[64,4,128]{2,1,0:T(4,128)S(1)} %dynamic-slice_bitcast_fusion.30, f32[64,64,4]{2,1,0:T(8,128)S(1)} %copy.579, ...), kind=kLoop, calls=%fused_computation.103.clone.1 | loop fusion | flops 18808832 | bytes 34164740 | tf_op jit(solution)/shard_map/transpose(jvp())/while/body/eval_jaxpr/reduce_sum | solution.py:69
  821.2 6.0 fusion.516
  833.5 18.9 %multiply_reduce_fusion.25 = (f32[64,4,128]{2,1,0:T(4,128)S(1)}, f32[64,4,128]{2,1,0:T(4,128)S(1)}, f32[1,64,64,4,128]{4,3,2,1,0:T(4,128)}) fusion(f32[2,1,64,64,4,128]{5,4,3,2,1,0:T(4,128)} %get-tuple-element.3792, s32[]{:T(128)S(6)} %sub.345, f32[64,4,128]{2,1,0:T(4,128)S(1)} %dynamic-slice_bitcast_fusion.30, f32[64,64,4]{2,1,0:T(8,128)S(1)} %copy.579, ...), kind=kLoop, calls=%fused_computation.103.clone.1 | loop fusion | flops 18808832 | bytes 34164740 | tf_op jit(solution)/shard_map/transpose(jvp())/while/body/eval_jaxpr/reduce_sum | solution.py:69
  858.8 6.0 fusion.516
  889.5 6.0 convolution_add_fusion.2
  899.3 8.1 convolution_add_fusion.3
  910.7 6.5 convolution_add_fusion.4
  921.3 3.6 convolution_add_fusion.7
  929.0 6.2 reduce_window_sum.91
  935.2 6.2 reduce_window_sum.93
  948.0 16.1 reduce-scatter.25.cloned.1.call-done
  964.1 16.0 reduce-scatter.15.cloned.1.call-done
  984.0 3.6 fusion.181
  987.6 3.8 fusion.179
  999.6 3.4 all-reduce.8
  1005.5 82.2 %all-reduce.6 = (f32[512]{0:T(512)}, f32[512,16]{0,1:T(8,128)}, f32[16,256]{1,0:T(8,128)}, f32[256]{0:T(256)}, f32[128]{0:T(128)}, /*index=5*/f32[512]{0:T(512)}) all-reduce(f32[512]{0:T(512)S(1)} %dynamic-slice.1, f32[512,16]{0,1:T(8,128)} %reduce-scatter.19.cloned.1.call-done, ...), channel_id=1, replica_groups=mesh['seq'=16,'fsdp'=2] {'seq'}, use_global_device_ids=true, to_apply=%region_57.58 | all-reduce | flops 13696 | bytes 109568 | tf_op jit(solution)/shard_map/psum | solution.py:294
  1087.7 772.8 %all-reduce.11.cloned.1.call-done = (f32[512,512]{1,0:T(8,128)}, f32[512,512]{1,0:T(8,128)}, f32[512,1024]{1,0:T(8,128)}, f32[512,1024]{1,0:T(8,128)}, f32[512,1...) async-done(((f32[512,512]{1,0:T(8,128)}, f32[512,512]{1,0:T(8,128)}, f32[512,1024]{1,0:T(8,128)}, f32[512,1024]{1,0:T(8,128)}, ...) | async-done | bytes 25690128 | tf_op jit(solution)/shard_map/psum | solution.py:294
  1865.3 3.3 copy.794
  (972 shorter events, 354.4 us)
Async XLA Ops:
  7.2 400.8 %copy-start = (s32[2,2]{1,0:T(2,128)S(1)}, s32[2,2]{1,0:T(2,128)}, u32[]{:S(2)}) copy-start(s32[2,2]{1,0:T(2,128)} %param.34) | copy-start | bytes 52
  7.2 18.3 all-gather.25.cloned.1.call-start
  7.9 25.2 %all-gather.21.cloned.1.call-start = ((), (), s32[]{:S(2)}) async-start(), calls=%async_computation.10 | async-start | bytes 1572864 | tf_op jit(solution)/shard_map/all_gather | solution.py:149
  8.7 37.8 %all-gather.23.cloned.1.call-start = ((), (), s32[]{:S(2)}) async-start(), calls=%async_computation.11 | async-start | bytes 3145728 | tf_op jit(solution)/shard_map/all_gather | solution.py:150
  9.4 403.5 %all-gather.27.cloned.1.call-start = ((), (), s32[]{:S(2)}) async-start(), calls=%async_computation.13 | async-start | bytes 3145728 | tf_op jit(solution)/shard_map/all_gather | solution.py:151
  10.0 405.6 %all-gather.39.cloned.1.call-start = ((), (), s32[]{:S(2)}) async-start(), calls=%async_computation.29 | async-start | bytes 8912896 | tf_op jit(solution)/shard_map/all_gather | solution.py:19
  15.1 33.5 %copy-start.163 = (f32[128]{0:T(128)}, f32[128]{0:T(128)S(1)}, u32[]{:S(2)}) copy-start(f32[128]{0:T(128)S(1)} %fusion.290) | copy-start | bytes 1540
  22.0 26.6 %copy-start.190 = (f32[2,1,256]{2,1,0:T(1,128)}, f32[2,1,256]{2,1,0:T(1,128)S(1)}, u32[]{:S(2)}) copy-start(f32[2,1,256]{2,1,0:T(1,128)S(1)} %convert_element_type.353) | copy-start | bytes 6148
  23.2 25.4 %copy-start.183 = (bf16[128,16]{0,1:T(8,128)(2,1)}, bf16[128,16]{0,1:T(8,128)(2,1)S(1)}, u32[]{:S(2)}) copy-start(bf16[128,16]{0,1:T(8,128)(2,1)S(1)} %convolution_convert_fusion.8) | copy-start | bytes 12292
  180.2 250.1 %all-gather.37.cloned.1.call-start = ((), (), s32[]{:S(2)}) async-start(), calls=%async_computation.28 | async-start | bytes 8912896 | tf_op jit(solution)/shard_map/all_gather | solution.py:19
  314.9 49.9 %copy-start.37 = (f32[2,1,64,4,128]{4,3,2,1,0:T(4,128)}, f32[2,1,64,4,128]{4,3,2,1,0:T(4,128)S(1)}, u32[]{:S(2)}) copy-start(f32[2,1,64,4,128]{4,3,2,1,0:T(4,128)S(1)} %get-tuple-element.4006) | copy-start | bytes 786436
  314.9 49.9 %copy-start.41 = (f32[2,1,64,4,128]{4,3,2,1,0:T(4,128)}, f32[2,1,64,4,128]{4,3,2,1,0:T(4,128)S(1)}, u32[]{:S(2)}) copy-start(f32[2,1,64,4,128]{4,3,2,1,0:T(4,128)S(1)} %get-tuple-element.4007) | copy-start | bytes 786436
  315.7 50.2 %copy-start.175 = (f32[512]{0:T(512)S(1)}, f32[512]{0:T(512)}, u32[]{:S(2)}) copy-start(f32[512]{0:T(512)} %get-tuple-element.2644) | copy-start | bytes 6148
  315.7 125.0 %all-gather.29.cloned.1.call-start = ((), (), s32[]{:S(2)}) async-start(), calls=%async_computation.14 | async-start | bytes 3145728 | tf_op jit(solution)/shard_map/all_gather | solution.py:156
  316.5 88.0 %copy-start.195 = (bf16[128]{0:T(256)(128)(2,1)S(1)}, bf16[128]{0:T(256)(128)(2,1)}, u32[]{:S(2)}) copy-start(bf16[128]{0:T(256)(128)(2,1)} %param.43) | copy-start | bytes 772
  316.5 89.7 %copy-start.191 = (bf16[512]{0:T(512)(128)(2,1)S(1)}, bf16[512]{0:T(512)(128)(2,1)}, u32[]{:S(2)}) copy-start(bf16[512]{0:T(512)(128)(2,1)} %param.45) | copy-start | bytes 3076
  316.5 93.4 %copy-start.113 = (f32[128,512]{1,0:T(8,128)S(1)}, f32[128,512]{1,0:T(8,128)}, u32[]{:S(2)}) copy-start(f32[128,512]{1,0:T(8,128)} %copy-done.112) | copy-start | bytes 786436
  316.5 93.6 %copy-start.115 = (f32[128,512]{1,0:T(8,128)S(1)}, f32[128,512]{1,0:T(8,128)}, u32[]{:S(2)}) copy-start(f32[128,512]{1,0:T(8,128)} %copy-done.114) | copy-start | bytes 786436
  316.5 142.9 %all-gather.31.cloned.1.call-start = ((), (), s32[]{:S(2)}) async-start(), calls=%async_computation.15 | async-start | bytes 8650752 | tf_op jit(solution)/shard_map/all_gather | solution.py:158
  317.3 93.7 %copy-start.131 = (f32[2,1,64,4,256]{4,2,0,3,1:T(8,128)S(1)}, f32[2,1,64,4,256]{4,2,0,3,1:T(8,128)}, u32[]{:S(2)}) copy-start(f32[2,1,64,4,256]{4,2,0,3,1:T(8,128)} %get-tuple-element.1653) | copy-start | bytes 1572868
  317.3 94.7 %copy-start.132 = (f32[2,1,64,4,256]{4,2,0,3,1:T(8,128)S(1)}, f32[2,1,64,4,256]{4,2,0,3,1:T(8,128)}, u32[]{:S(2)}) copy-start(f32[2,1,64,4,256]{4,2,0,3,1:T(8,128)} %get-tuple-element.1650) | copy-start | bytes 1572868
  317.3 95.7 %copy-start.10 = (bf16[2,1,128,1024]{3,2,1,0:T(8,128)(2,1)S(1)}, bf16[2,1,128,1024]{3,2,1,0:T(8,128)(2,1)}, u32[]{:S(2)}) copy-start(bf16[2,1,128,1024]{3,2,1,0:T(8,128)(2,1)} %param.33) | copy-start | bytes 1572868
  317.3 95.6 %copy-start.164 = (f32[128]{0:T(128)S(1)}, f32[128]{0:T(128)}, u32[]{:S(2)}) copy-start(f32[128]{0:T(128)} %copy-done.163) | copy-start | bytes 1540
  317.3 160.9 %all-gather.33.cloned.1.call-start = ((), (), s32[]{:S(2)}) async-start(), calls=%async_computation.16 | async-start | bytes 8650752 | tf_op jit(solution)/shard_map/all_gather | solution.py:159
  318.1 178.7 %all-gather.35.cloned.1.call-start = ((), (), s32[]{:S(2)}) async-start(), calls=%async_computation.17 | async-start | bytes 8650752 | tf_op jit(solution)/shard_map/all_gather | solution.py:160
  318.6 326.7 %all-gather.41.cloned.1.call-start = ((), (), s32[]{:S(2)}) async-start(), calls=%async_computation.30 | async-start | bytes 8912896 | tf_op jit(solution)/shard_map/all_gather | solution.py:19
  365.9 165.3 %copy-start.76 = (f32[1,128,4,128]{1,3,2,0:T(8,128)}, f32[1,128,4,128]{1,3,2,0:T(8,128)S(1)}, u32[]{:S(2)}) copy-start(f32[1,128,4,128]{1,3,2,0:T(8,128)S(1)} %copy.237) | copy-start | bytes 786436
  409.3 113.5 %copy-start.177 = (f32[128]{0:T(128)}, f32[128]{0:T(128)S(1)}, u32[]{:S(2)}) copy-start(f32[128]{0:T(128)S(1)} %compare_convert_fusion.1) | copy-start | bytes 1540
  410.0 112.9 %copy-start.179 = (f32[128]{0:T(128)}, f32[128]{0:T(128)S(1)}, u32[]{:S(2)}) copy-start(f32[128]{0:T(128)S(1)} %compare_convert_fusion) | copy-start | bytes 1540
  442.9 65.7 %copy-start.52 = (f32[128,1024]{1,0:T(8,128)}, f32[128,1024]{1,0:T(8,128)S(1)}, u32[]{:S(2)}) copy-start(f32[128,1024]{1,0:T(8,128)S(1)} %get-tuple-element.2725) | copy-start | bytes 1572868
  445.3 63.2 %copy-start.49 = (f32[128,1024]{1,0:T(8,128)}, f32[128,1024]{1,0:T(8,128)S(1)}, u32[]{:S(2)}) copy-start(f32[128,1024]{1,0:T(8,128)S(1)} %get-tuple-element.2727) | copy-start | bytes 1572868
  445.5 32.7 %copy-start.55 = (bf16[128,1024]{1,0:T(8,128)(2,1)}, bf16[128,1024]{1,0:T(8,128)(2,1)S(1)}, u32[]{:S(2)}) copy-start(bf16[128,1024]{1,0:T(8,128)(2,1)S(1)} %multiply_convert_fusion.8) | copy-start | bytes 786436
  464.1 32.7 %copy-start.128 = (bf16[2,1,128,1024]{3,2,1,0:T(8,128)(2,1)S(1)}, bf16[2,1,128,1024]{3,2,1,0:T(8,128)(2,1)}, u32[]{:S(2)}) copy-start(bf16[2,1,128,1024]{3,2,1,0:T(8,128)(2,1)} %param.49) | copy-start | bytes 1572868
  531.2 228.4 %all-gather.43.cloned.1.call-start = ((), (), s32[]{:S(2)}) async-start(), calls=%async_computation.31 | async-start | bytes 8912896 | tf_op jit(solution)/shard_map/all_gather | solution.py:19
  535.7 412.2 %reduce-scatter.23.cloned.1.call-start = ((), (), s32[]{:S(2)}) async-start(), calls=%async_computation.24 | async-start | bytes 6291456 | tf_op jit(solution)/shard_map/reduce_scatter | solution.py:288
  540.2 407.7 %reduce-scatter.17.cloned.1.call-start = ((), (), s32[]{:S(2)}) async-start(), calls=%async_computation.21 | async-start | bytes 6291456 | tf_op jit(solution)/shard_map/reduce_scatter | solution.py:283
  546.5 121.2 %copy-start.38 = (f32[2,1,64,4,128]{4,3,2,1,0:T(4,128)S(1)}, f32[2,1,64,4,128]{4,3,2,1,0:T(4,128)}, u32[]{:S(2)}) copy-start(f32[2,1,64,4,128]{4,3,2,1,0:T(4,128)} %copy-done.37) | copy-start | bytes 786436
  546.5 121.2 %copy-start.162 = (f32[2,1,4,128,1]{3,2,4,1,0:T(4,128)S(1)}, f32[2,1,4,128,1]{3,2,4,1,0:T(4,128)}, u32[]{:S(2)}) copy-start(f32[2,1,4,128,1]{3,2,4,1,0:T(4,128)} %get-tuple-element.3838) | copy-start | bytes 12292
  546.5 401.4 %reduce-scatter.13.cloned.1.call-start = ((), (), s32[]{:S(2)}) async-start(), calls=%async_computation.19 | async-start | bytes 3145728 | tf_op jit(solution)/shard_map/reduce_scatter | solution.py:281
  671.5 20.3 %copy-start.147 = (bf16[2,1,64,4,128]{4,2,3,1,0:T(8,128)(2,1)S(1)}, bf16[2,1,64,4,128]{4,2,3,1,0:T(8,128)(2,1)}, u32[]{:S(2)}) copy-start(bf16[2,1,64,4,128]{4,2,3,1,0:T(8,128)(2,1)} %get-tuple-element.3860) | copy-start | bytes 393220 | tf_op jit(solution)/shard_map/transpose(jvp())/while
  671.6 20.7 %copy-start.42 = (f32[2,1,64,4,128]{4,3,2,0,1:T(4,128)S(1)}, f32[2,1,64,4,128]{4,3,2,0,1:T(4,128)}, u32[]{:S(2)}) copy-start(f32[2,1,64,4,128]{4,3,2,0,1:T(4,128)} %get-tuple-element.3900) | copy-start | bytes 786436 | tf_op jit(solution)/shard_map/transpose(jvp())/while
  671.6 21.5 %copy-start.21 = (f32[2,1,4,128,256]{4,3,2,1,0:T(8,128)S(1)}, f32[2,1,4,128,256]{4,3,2,1,0:T(8,128)}, u32[]{:S(2)}) copy-start(f32[2,1,4,128,256]{4,3,2,1,0:T(8,128)} %get-tuple-element.3891) | copy-start | bytes 3145732 | tf_op jit(solution)/shard_map/transpose(jvp())/while
  710.8 20.3 %copy-start.147 = (bf16[2,1,64,4,128]{4,2,3,1,0:T(8,128)(2,1)S(1)}, bf16[2,1,64,4,128]{4,2,3,1,0:T(8,128)(2,1)}, u32[]{:S(2)}) copy-start(bf16[2,1,64,4,128]{4,2,3,1,0:T(8,128)(2,1)} %get-tuple-element.3860) | copy-start | bytes 393220 | tf_op jit(solution)/shard_map/transpose(jvp())/while
  710.8 20.7 %copy-start.42 = (f32[2,1,64,4,128]{4,3,2,0,1:T(4,128)S(1)}, f32[2,1,64,4,128]{4,3,2,0,1:T(4,128)}, u32[]{:S(2)}) copy-start(f32[2,1,64,4,128]{4,3,2,0,1:T(4,128)} %get-tuple-element.3900) | copy-start | bytes 786436 | tf_op jit(solution)/shard_map/transpose(jvp())/while
  710.8 21.5 %copy-start.21 = (f32[2,1,4,128,256]{4,3,2,1,0:T(8,128)S(1)}, f32[2,1,4,128,256]{4,3,2,1,0:T(8,128)}, u32[]{:S(2)}) copy-start(f32[2,1,4,128,256]{4,3,2,1,0:T(8,128)} %get-tuple-element.3891) | copy-start | bytes 3145732 | tf_op jit(solution)/shard_map/transpose(jvp())/while
  746.1 43.0 %copy-start.149 = (bf16[2,1,64,4,128]{4,2,3,1,0:T(8,128)(2,1)S(1)}, bf16[2,1,64,4,128]{4,2,3,1,0:T(8,128)(2,1)}, u32[]{:S(2)}) copy-start(bf16[2,1,64,4,128]{4,2,3,1,0:T(8,128)(2,1)} %get-tuple-element.1671) | copy-start | bytes 393220
  746.1 46.6 %copy-start.6 = (f32[2,1,64,4,256]{4,2,3,1,0:T(8,128)S(1)}, f32[2,1,64,4,256]{4,2,3,1,0:T(8,128)}, u32[]{:S(2)}) copy-start(f32[2,1,64,4,256]{4,2,3,1,0:T(8,128)} %copy-done.5) | copy-start | bytes 1572868
  746.1 46.6 %copy-start.12 = (f32[1,128,4,256]{3,1,2,0:T(8,128)S(1)}, f32[1,128,4,256]{3,1,2,0:T(8,128)}, u32[]{:S(2)}) copy-start(f32[1,128,4,256]{3,1,2,0:T(8,128)} %copy.272) | copy-start | bytes 1572868
  746.1 46.6 %copy-start.30 = (f32[2,1,64,4,128]{4,3,2,1,0:T(4,128)S(1)}, f32[2,1,64,4,128]{4,3,2,1,0:T(4,128)}, u32[]{:S(2)}) copy-start(f32[2,1,64,4,128]{4,3,2,1,0:T(4,128)} %copy-done.29) | copy-start | bytes 786436
  746.1 46.6 %copy-start.159 = (f32[2,1,4,128,1]{3,2,4,1,0:T(4,128)S(1)}, f32[2,1,4,128,1]{3,2,4,1,0:T(4,128)}, u32[]{:S(2)}) copy-start(f32[2,1,4,128,1]{3,2,4,1,0:T(4,128)} %get-tuple-element.3736) | copy-start | bytes 12292
  795.8 20.2 %copy-start.34 = (f32[2,1,64,4,128]{4,3,2,0,1:T(4,128)S(1)}, f32[2,1,64,4,128]{4,3,2,0,1:T(4,128)}, u32[]{:S(2)}) copy-start(f32[2,1,64,4,128]{4,3,2,0,1:T(4,128)} %get-tuple-element.3798) | copy-start | bytes 786436 | tf_op jit(solution)/shard_map/transpose(jvp())/while
  795.8 20.9 %copy-start.20 = (f32[2,1,4,128,256]{4,3,2,1,0:T(8,128)S(1)}, f32[2,1,4,128,256]{4,3,2,1,0:T(8,128)}, u32[]{:S(2)}) copy-start(f32[2,1,4,128,256]{4,3,2,1,0:T(8,128)} %get-tuple-element.3789) | copy-start | bytes 3145732 | tf_op jit(solution)/shard_map/transpose(jvp())/while
  833.5 20.2 %copy-start.34 = (f32[2,1,64,4,128]{4,3,2,0,1:T(4,128)S(1)}, f32[2,1,64,4,128]{4,3,2,0,1:T(4,128)}, u32[]{:S(2)}) copy-start(f32[2,1,64,4,128]{4,3,2,0,1:T(4,128)} %get-tuple-element.3798) | copy-start | bytes 786436 | tf_op jit(solution)/shard_map/transpose(jvp())/while
  833.5 20.9 %copy-start.20 = (f32[2,1,4,128,256]{4,3,2,1,0:T(8,128)S(1)}, f32[2,1,4,128,256]{4,3,2,1,0:T(8,128)}, u32[]{:S(2)}) copy-start(f32[2,1,4,128,256]{4,3,2,1,0:T(8,128)} %get-tuple-element.3789) | copy-start | bytes 3145732 | tf_op jit(solution)/shard_map/transpose(jvp())/while
  873.9 74.1 %reduce-scatter.11.cloned.1.call-start = ((), (), s32[]{:S(2)}) async-start(), calls=%async_computation.18 | async-start | bytes 3145728 | tf_op jit(solution)/shard_map/reduce_scatter | solution.py:280
  886.3 61.7 %reduce-scatter.29.cloned.1.call-start = ((), (), s32[]{:S(2)}) async-start(), calls=%async_computation.27 | async-start | bytes 17301504 | tf_op jit(solution)/shard_map/reduce_scatter | solution.py:292
  895.6 52.4 %reduce-scatter.27.cloned.1.call-start = ((), (), s32[]{:S(2)}) async-start(), calls=%async_computation.26 | async-start | bytes 17301504 | tf_op jit(solution)/shard_map/reduce_scatter | solution.py:291
  907.5 56.6 %reduce-scatter.25.cloned.1.call-start = ((), (), s32[]{:S(2)}) async-start(), calls=%async_computation.25 | async-start | bytes 17301504 | tf_op jit(solution)/shard_map/reduce_scatter | solution.py:290
  917.2 62.9 %reduce-scatter.15.cloned.1.call-start = ((), (), s32[]{:S(2)}) async-start(), calls=%async_computation.20 | async-start | bytes 6291456 | tf_op jit(solution)/shard_map/reduce_scatter | solution.py:282
  921.3 20.1 %copy-start.23 = (f32[1,4,128,256]{3,2,1,0:T(8,128)S(1)}, f32[1,4,128,256]{3,2,1,0:T(8,128)}, u32[]{:S(2)}) copy-start(f32[1,4,128,256]{3,2,1,0:T(8,128)} %copy-done.22) | copy-start | bytes 1572868
  924.9 80.5 %reduce-scatter.21.cloned.1.call-start = ((), (), s32[]{:S(2)}) async-start(), calls=%async_computation.23 | async-start | bytes 49152 | tf_op jit(solution)/shard_map/reduce_scatter | solution.py:285
  944.0 36.2 %copy-start.185 = (bf16[128,16]{0,1:T(8,128)(2,1)}, bf16[128,16]{0,1:T(8,128)(2,1)S(1)}, u32[]{:S(2)}) copy-start(bf16[128,16]{0,1:T(8,128)(2,1)S(1)} %convolution_convert_fusion.7) | copy-start | bytes 12292
  946.0 59.4 %reduce-scatter.19.cloned.1.call-start = ((), (), s32[]{:S(2)}) async-start(), calls=%async_computation.22 | async-start | bytes 98304 | tf_op jit(solution)/shard_map/reduce_scatter | solution.py:284
  947.6 912.8 %all-reduce.11.cloned.1.call-start = ((), (), s32[]{:S(2)}) async-start(), calls=%async_computation.32 | async-start | bytes 51380224 | tf_op jit(solution)/shard_map/psum | solution.py:294
  (216 other events, 1622.2 us)
Sparse Core Ops, SparseCore 0:
  9.6 11.7 all-gather.24
  22.9 10.1 all-gather.20
  34.7 11.7 all-gather.22
  47.9 11.7 all-gather.26
  180.3 113.9 all-gather.38
  315.8 114.4 all-gather.36
  431.8 8.8 all-gather.28
  442.3 17.1 all-gather.30
  461.0 17.1 all-gather.32
  479.6 17.1 all-gather.34
  531.3 113.9 all-gather.40
  648.5 111.0 all-gather.42
  762.4 10.2 reduce-scatter.22
  775.5 13.3 reduce-scatter.16
  874.0 5.4 reduce-scatter.12
  886.4 6.6 reduce-scatter.10
  895.7 20.9 reduce-scatter.28
  918.8 21.4 reduce-scatter.26
  942.6 21.4 reduce-scatter.24
  966.8 13.2 reduce-scatter.14
  983.0 8.6 reduce-scatter.20
  994.6 8.5 reduce-scatter.18
  1010.8 849.6 all-reduce.10
where the time goes:
time: 1900 us; the launch traced here: 1890 us
  waiting for transfers between devices  998 us (53%)
  other arithmetic  323 us (17%)
  matrix products  192 us (10%)
  blocking collectives  176 us (9%)
  local copies, waits for them, and re-layouts  174 us (9%)
    psum x1, waiting for transfers between devices, shards(): lax.psum((halves[0], halves[1], halves[2], halves[3], halves[4], halves[5...  773 us
    all_gather x4, waiting for transfers between devices, carried_in(): gathered = jax.tree.map(lambda a: lax.all_gather(a, axis), part)  124 us
    dynamic_update_slice x16, other arithmetic, local_mix(): lax.scan(block_step, start_state, (to_blocks(queries), to_blocks(key_rows...  85.5 us
    psum x1, blocking collectives, shards(): lax.psum((halves[0], halves[1], halves[2], halves[3], halves[4], halves[5...  82.2 us
    all_gather x2, blocking collectives, carried_in(): gathered = jax.tree.map(lambda a: lax.all_gather(a, axis), part)  78.4 us
    reduce_sum x4, other arithmetic, block_step(): queries[:, :, None] * key_rows[:, None] * decay_weights  76.9 us
    reduce_sum x4, other arithmetic, block_step(): jnp.sum(queries[:, :, None] * key_rows[:, None] * decay_weights, axis=-1)  62.9 us
    another operation x40, local copies, waits for them, and re-layouts  59.9 us
  transfers between devices with their start and end apart: 23, of which 12 were waited for; matrix products, arithmetic and copies ran while one was open for 33% of the time, Pallas kernels for 0%

commit v1 on v0

v1 whole, which is shorter than its diff:
```python
from functools import partial

import jax
import jax.numpy as jnp
from jax import lax
from jax.experimental import pallas as pl
from jax.experimental.pallas import tpu as pltpu
from jax.sharding import PartitionSpec as P

HEADS = 4
F32 = jnp.float32
BF16 = jnp.bfloat16
MIB = 1024 * 1024


def dot(first_op, second_op):
    return jnp.dot(first_op, second_op, preferred_element_type=F32)


def dot_t(first_op, second_op):
    return lax.dot_general(
        first_op, second_op, (((1,), (1,)), ((), ())), preferred_element_type=F32
    )


def t_dot(first_op, second_op):
    return lax.dot_general(
        first_op, second_op, (((0,), (0,)), ((), ())), preferred_element_type=F32
    )


def two_part(value):
    high = value.astype(BF16)
    return high, (value - high.astype(F32)).astype(BF16)


def mask_dot(mask, value):
    high, rest = two_part(value)
    return dot(mask, high) + dot(mask, rest)


def sigmoid(value):
    return 1.0 / (1.0 + jnp.exp(-value))


def pair_iota(size):
    return (
        lax.broadcasted_iota(jnp.int32, (size, size), 0),
        lax.broadcasted_iota(jnp.int32, (size, size), 1),
    )


def level_masks(size):
    row, col = pair_iota(size)
    out = []
    half = size // 2
    while half >= 1:
        block = 2 * half
        row_block = row // block
        middle = row_block * block + half - 1
        upper = row > middle
        sums = (upper & (col > middle) & (col <= row)) | (
            jnp.logical_not(upper) & (col > row) & (col <= middle)
        )
        same = row_block == col // block
        pairs = same & upper & (col <= middle)
        both = same & (upper != (col > middle))
        out.append((sums.astype(F32).astype(BF16), pairs, both, half))
        half //= 2
    return out


def upper_rows(half, width, size):
    row = lax.broadcasted_iota(jnp.int32, (size, width), 0)
    return row % (2 * half) >= half


def seat(idx_ref):
    return idx_ref[0], idx_ref[1]


def mine_at(idx_ref, width):
    return pl.ds(pl.multiple_of(idx_ref[0] * width, 128), width)


def theirs_at(idx_ref, width):
    return pl.ds(pl.multiple_of((1 - idx_ref[0]) * width, 128), width)


SMEM = pl.BlockSpec(memory_space=pltpu.SMEM)
VMEM = pl.BlockSpec(memory_space=pltpu.VMEM)


def call(name, body, idx, inputs, outs, scratch=(), flops=0, limit=32):
    shapes = [jax.ShapeDtypeStruct(s, d) for s, d in outs]
    moved = sum(a.size * a.dtype.itemsize for a in inputs) + sum(
        s.size * s.dtype.itemsize for s in shapes
    )
    result = pl.pallas_call(
        body,
        name=name,
        out_shape=shapes,
        in_specs=[SMEM] + [VMEM] * len(inputs),
        out_specs=[VMEM] * len(shapes),
        scratch_shapes=[pltpu.VMEM(s, d) for s, d in scratch],
        compiler_params=pltpu.CompilerParams(vmem_limit_bytes=limit * MIB),
        cost_estimate=pl.CostEstimate(
            flops=int(flops), bytes_accessed=int(moved), transcendentals=0
        ),
    )(idx, *inputs)
    return result


def put_message(ref, rows, total):
    count = rows.shape[0]
    ref[pl.ds(0, count), :] = rows.astype(BF16)
    high = total.astype(BF16)
    rest = total - high.astype(F32)
    middle = rest.astype(BF16)
    low = (rest - middle.astype(F32)).astype(BF16)
    tail = jnp.concatenate(
        [high, middle, low, jnp.zeros((13,) + total.shape[1:], BF16)], axis=0
    )
    ref[pl.ds(count, 16), :] = tail


def get_message(ref):
    count = ref.shape[0] - 16
    tail = ref[pl.ds(count, 16), :].astype(F32)
    return ref[pl.ds(0, count), :].astype(F32), tail[0:1] + tail[1:2] + tail[2:3]


def write_quarters(idx_ref, state, totals, messages, seq_count):
    low = lax.rem(idx_ref[1], 4)
    for other in range(4):
        quarter = low ^ other
        total = totals[0]
        for one in range(1, seq_count):
            total = jnp.where(quarter * seq_count // 4 >= one, totals[one], total)
        put_message(messages[other], state[quarter], total)


def group_total(reverse, idx_ref, *refs):
    out_ref, kept, held = refs[4], refs[5], refs[6]
    low = lax.rem(idx_ref[1], 4)
    for other in range(4):
        rows, total = get_message(refs[other])
        kept[low ^ other] = rows
        held[low ^ other] = total
    order = (3, 2, 1, 0) if reverse else (0, 1, 2, 3)
    rows, total = kept[order[0]], held[order[0]]
    for one in order[1:]:
        rows = held[one] * rows + kept[one]
        total = total * held[one]
    put_message(out_ref, rows, total)


def group_entering(reverse, far_count, idx_ref, *refs):
    far, near = refs[:far_count], refs[far_count : far_count + 4]
    outs = refs[far_count + 4 : far_count + 8]
    kept, held, entering = refs[far_count + 8 :]
    low = lax.rem(idx_ref[1], 4)
    for other in range(4):
        rows, total = get_message(near[other])
        kept[low ^ other] = rows
        held[low ^ other] = total
    rows = jnp.zeros(kept.shape[1:], F32)
    for one in far[::-1]:
        part, total = get_message(one)
        rows = total * rows + part
    for one in (3, 2, 1, 0) if reverse else (0, 1, 2, 3):
        entering[one] = rows
        rows = held[one] * rows + kept[one]
    for other in range(4):
        outs[other][...] = entering[low ^ other].astype(BF16)


def load_state(idx_ref, pieces, state):
    low = lax.rem(idx_ref[1], 4)
    for other in range(4):
        state[low ^ other] = pieces[other][...]


def keys_kernel(dims, idx_ref, x_ref, g1_own, g1_oth, wk_own, wk_oth, wv_own, wv_oth, li_own, li_oth,
                lo_own, lo_oth, b_own, b_oth, nm_ref, no_ref, k_ref, v_ref, lr_ref, lg_ref, kd_ref, tot_ref,
                m0, m1, m2, m3, state):
    seqs, span = dims
    half = g1_own.shape[1]
    xm = x_ref[:, mine_at(idx_ref, half)].astype(F32)
    xo = x_ref[:, theirs_at(idx_ref, half)].astype(F32)
    square = jnp.sum(xm * xm, axis=1, keepdims=True) + jnp.sum(xo * xo, axis=1, keepdims=True)
    root = lax.rsqrt(square / (2 * half) + 1e-6)
    nm = (xm * root * g1_own[...].astype(F32)).astype(BF16)
    no = (xo * root * g1_oth[...].astype(F32)).astype(BF16)
    nm_ref[...] = nm
    no_ref[...] = no
    lr = (dot(nm, li_own[...]) + dot(no, li_oth[...])).astype(BF16)
    lr_ref[...] = lr
    part = lo_own.shape[1]
    lg_ref[:, mine_at(idx_ref, part)] = dot(lr, lo_own[...]) + b_own[...].astype(F32)
    lg_ref[:, theirs_at(idx_ref, part)] = dot(lr, lo_oth[...]) + b_oth[...].astype(F32)
    keys = (dot(nm, wk_own[...]) + dot(no, wk_oth[...])).astype(BF16)
    k_ref[...] = keys
    values = (dot(nm, wv_own[...]) + dot(no, wv_oth[...])).astype(BF16)
    v_ref[...] = values
    row, col = pair_iota(span)
    later = (col > row).astype(F32).astype(BF16)
    wide = keys.shape[1] // HEADS
    tall = values.shape[1] // HEADS
    quarter = state.shape[1]
    totals = []
    for s in range(seqs):
        at = slice(s * span, (s + 1) * span)
        logits = lg_ref[at, :]
        decays = (jnp.minimum(logits, 0.0) - jnp.log1p(jnp.exp(-jnp.abs(logits)))) / 16.0
        ahead = mask_dot(later, decays)
        totals.append(jnp.exp(jnp.sum(decays, axis=0, keepdims=True)))
        tot_ref[pl.ds(s, 1), :] = totals[s]
        faded = (keys[at].astype(F32) * jnp.exp(ahead)).astype(BF16)
        kd_ref[at, :] = faded
        for h in range(HEADS):
            part = t_dot(values[at, h * tall : (h + 1) * tall], faded[:, h * wide : (h + 1) * wide])
            per = tall // quarter
            for q in range(per):
                state[s * per + q, :, h * wide : (h + 1) * wide] = part[q * quarter : (q + 1) * quarter]
    write_quarters(idx_ref, state, totals, (m0, m1, m2, m3), seqs)


def inner_kernel(dims, idx_ref, nm_ref, no_ref, wq_own, wq_oth, wg_own, wg_oth, k_ref, v_ref, lg_ref,
                 q_ref, og_ref, mix_ref, a_ref, qb_ref):
    seqs, span = dims
    nm, no = nm_ref[...], no_ref[...]
    queries = (dot(nm, wq_own[...]) + dot(no, wq_oth[...])).astype(BF16)
    q_ref[...] = queries
    og_ref[...] = dot(nm, wg_own[...]) + dot(no, wg_oth[...])
    row, col = pair_iota(span)
    upto = (col <= row).astype(F32).astype(BF16)
    diagonal = row == col
    levels = level_masks(span)
    wide = queries.shape[1] // HEADS
    tall = v_ref.shape[1] // HEADS
    for s in range(seqs):
        at = slice(s * span, (s + 1) * span)
        logits = lg_ref[at, :]
        decays = (jnp.minimum(logits, 0.0) - jnp.log1p(jnp.exp(-jnp.abs(logits)))) / 16.0
        high, rest = two_part(decays)
        qs, ks = queries[at], k_ref[at, :]
        qs32, ks32 = qs.astype(F32), ks.astype(F32)
        qb_ref[at, :] = (qs32 * jnp.exp(dot(upto, high) + dot(upto, rest))).astype(BF16)
        scores = []
        for h in range(HEADS):
            hs = slice(h * wide, (h + 1) * wide)
            scores.append(jnp.where(diagonal, dot_t(qs[:, hs], ks[:, hs]), 0.0))
        for sums, pairs, _, half in levels:
            fade = jnp.exp(dot(sums, high) + dot(sums, rest))
            side = (jnp.where(upper_rows(half, qs.shape[1], span), qs32, ks32) * fade).astype(BF16)
            for h in range(HEADS):
                part = side[:, h * wide : (h + 1) * wide]
                scores[h] = scores[h] + jnp.where(pairs, dot_t(part, part), 0.0)
        for h in range(HEADS):
            low = scores[h].astype(BF16)
            a_ref[s * HEADS + h] = low
            vs = slice(h * tall, (h + 1) * tall)
            mix_ref[at, vs] = dot(low, v_ref[at, vs])


def hidden_kernel(dims, idx_ref, mix_ref, qb_ref, e0, e1, e2, e3, og_ref, hg_own, hg_oth, x_ref, wo_own, wo_oth,
                  g2_own, g2_oth, mixture_ref, gm_ref, go_ref, hid_ref, sm_ref, so_ref, st_ref,
                  gain, gated):
    seqs, span = dims
    load_state(idx_ref, (e0, e1, e2, e3), st_ref)
    gain[:, mine_at(idx_ref, hg_own.shape[1])] = hg_own[...].astype(F32)
    gain[:, theirs_at(idx_ref, hg_own.shape[1])] = hg_oth[...].astype(F32)
    wide = qb_ref.shape[1] // HEADS
    tall = mix_ref.shape[1] // HEADS
    factor = wide ** (-0.5)
    quarter = st_ref.shape[1]
    per = tall // quarter
    head_gain = gain[...]
    for s in range(seqs):
        at = slice(s * span, (s + 1) * span)
        for h in range(HEADS):
            hs = slice(h * wide, (h + 1) * wide)
            for q in range(per):
                vs = slice(h * tall + q * quarter, h * tall + (q + 1) * quarter)
                carried = dot_t(qb_ref[at, hs], st_ref[s * per + q, :, hs])
                mixture_ref[at, vs] = (mix_ref[at, vs] + carried) * factor
            vs = slice(h * tall, (h + 1) * tall)
            mixture = mixture_ref[at, vs]
            root = lax.rsqrt(jnp.mean(mixture * mixture, axis=1, keepdims=True) + 1e-5)
            opened = og_ref[at, vs]
            gated[at, vs] = (mixture * root * head_gain * (opened * sigmoid(opened))).astype(BF16)
    half = wo_own.shape[0]
    gm = gated[:, mine_at(idx_ref, half)]
    go = gated[:, theirs_at(idx_ref, half)]
    gm_ref[...] = gm
    go_ref[...] = go
    hid_ref[...] = x_ref[...].astype(F32) + dot(gm, wo_own[...]) + dot(go, wo_oth[...])
    half = g2_own.shape[1]
    hm = hid_ref[:, mine_at(idx_ref, half)]
    ho = hid_ref[:, theirs_at(idx_ref, half)]
    square = jnp.sum(hm * hm, axis=1, keepdims=True) + jnp.sum(ho * ho, axis=1, keepdims=True)
    root = lax.rsqrt(square / (2 * half) + 1e-6)
    sm_ref[...] = (hm * root * g2_own[...].astype(F32)).astype(BF16)
    so_ref[...] = (ho * root * g2_oth[...].astype(F32)).astype(BF16)


def ffn_kernel(dims, idx_ref, sm_ref, so_ref, hid_ref, cot_ref, wg_own, wg_oth, wu_own, wu_oth, wd_own, wd_oth,
               out_ref, e_ref, am_ref, ao_ref, gg_ref, ug_ref, dm_ref, do_ref):
    seqs, span = dims
    rows, width = hid_ref.shape
    for s in range(seqs):
        at = slice(s * span, (s + 1) * span)
        places = lax.broadcasted_iota(jnp.int32, (span, width), 0) + idx_ref[1] * span
        valid = places < idx_ref[2 + s]
        e_ref[at, :] = jnp.where(valid, cot_ref[at, :].astype(F32), 0.0).astype(BF16)
    sm, so, cots = sm_ref[...], so_ref[...], e_ref[...]
    half = wd_own.shape[0]
    out_ref[...] = hid_ref[...]
    for step in range(2):
        at = (mine_at, theirs_at)[step](idx_ref, half)
        down = (wd_own, wd_oth)[step]
        act_ref = (am_ref, ao_ref)[step]
        gates = dot(sm, wg_own[:, at]) + dot(so, wg_oth[:, at])
        ups = dot(sm, wu_own[:, at]) + dot(so, wu_oth[:, at])
        sig = sigmoid(gates)
        opened = gates * sig
        act = (opened * ups).astype(BF16)
        act_ref[...] = act
        grads = dot_t(cots, down[...])
        gate_grad = (grads * ups * sig * (1.0 + gates * (1.0 - sig))).astype(BF16)
        up_grad = (grads * opened).astype(BF16)
        gg_ref[:, at] = gate_grad
        ug_ref[:, at] = up_grad
        out_ref[...] += dot(act, down[...])
        dm = dot_t(gate_grad, wg_own[:, at]) + dot_t(up_grad, wu_own[:, at])
        do = dot_t(gate_grad, wg_oth[:, at]) + dot_t(up_grad, wu_oth[:, at])
        if step == 0:
            dm_ref[...] = dm
            do_ref[...] = do
        else:
            dm_ref[...] += dm
            do_ref[...] += do
    for s in range(seqs):
        at = slice(s * span, (s + 1) * span)
        places = lax.broadcasted_iota(jnp.int32, (span, width), 0) + idx_ref[1] * span
        out_ref[at, :] = jnp.where(places < idx_ref[2 + s], out_ref[at, :], 0.0)


def gate_back_kernel(dims, idx_ref, hid_ref, dm_ref, do_ref, g2_own, g2_oth, e_ref, wo_own, wo_oth, mixture_ref,
                     og_ref, hg_own, hg_oth, qb_ref, tot_ref,
                     hg_ref, hl_ref, mg_ref, ol_ref, g2m_ref, g2o_ref, hgm_ref, hgo_ref, m0, m1, m2, m3,
                     gain, gated, gain_sum, state):
    seqs, span = dims
    half = g2_own.shape[1]
    mine, theirs = mine_at(idx_ref, half), theirs_at(idx_ref, half)
    hm, ho = hid_ref[:, mine], hid_ref[:, theirs]
    square = jnp.sum(hm * hm, axis=1, keepdims=True) + jnp.sum(ho * ho, axis=1, keepdims=True)
    root = lax.rsqrt(square / (2 * half) + 1e-6)
    dm, do = dm_ref[...], do_ref[...]
    g2m_ref[...] = jnp.sum(dm * hm * root, axis=0, keepdims=True)
    g2o_ref[...] = jnp.sum(do * ho * root, axis=0, keepdims=True)
    dm = dm * g2_own[...].astype(F32)
    do = do * g2_oth[...].astype(F32)
    along = jnp.sum(dm * hm, axis=1, keepdims=True) + jnp.sum(do * ho, axis=1, keepdims=True)
    along = along * (root * root * root) / (2 * half)
    hg_ref[:, mine] = e_ref[:, mine].astype(F32) + dm * root - hm * along
    hg_ref[:, theirs] = e_ref[:, theirs].astype(F32) + do * root - ho * along
    low = hg_ref[...].astype(BF16)
    hl_ref[...] = low
    half = wo_own.shape[0]
    gated[:, mine_at(idx_ref, half)] = dot_t(low, wo_own[...])
    gated[:, theirs_at(idx_ref, half)] = dot_t(low, wo_oth[...])
    gain[:, mine_at(idx_ref, hg_own.shape[1])] = hg_own[...].astype(F32)
    gain[:, theirs_at(idx_ref, hg_own.shape[1])] = hg_oth[...].astype(F32)
    head_gain = gain[...]
    wide = qb_ref.shape[1] // HEADS
    tall = mixture_ref.shape[1] // HEADS
    factor = wide ** (-0.5)
    quarter = state.shape[1]
    per = tall // quarter
    gain_grad = jnp.zeros((1, tall), F32)
    for s in range(seqs):
        at = slice(s * span, (s + 1) * span)
        for h in range(HEADS):
            vs = slice(h * tall, (h + 1) * tall)
            hs = slice(h * wide, (h + 1) * wide)
            mixture, opened, grad = mixture_ref[at, vs], og_ref[at, vs], gated[at, vs]
            root = lax.rsqrt(jnp.mean(mixture * mixture, axis=1, keepdims=True) + 1e-5)
            sig = sigmoid(opened)
            flat = mixture * root
            ol_ref[at, vs] = (grad * flat * head_gain * sig * (1.0 + opened * (1.0 - sig))).astype(BF16)
            grad = grad * (opened * sig)
            gain_grad += jnp.sum(grad * flat, axis=0, keepdims=True)
            grad = grad * head_gain
            along = jnp.mean(grad * flat, axis=1, keepdims=True)
            mixed = (grad - flat * along) * (root * factor)
            mg_ref[at, vs] = mixed
            part = t_dot(mixed.astype(BF16), qb_ref[at, hs])
            for q in range(per):
                state[s * per + q, :, hs] = part[q * quarter : (q + 1) * quarter]
    gain_sum[...] = gain_grad
    hgm_ref[...] = gain_sum[:, mine_at(idx_ref, hg_own.shape[1])]
    hgo_ref[...] = gain_sum[:, theirs_at(idx_ref, hg_own.shape[1])]
    totals = [tot_ref[pl.ds(s, 1), :] for s in range(seqs)]
    write_quarters(idx_ref, state, totals, (m0, m1, m2, m3), seqs)


def inner_back_kernel(dims, idx_ref, q_ref, k_ref, v_ref, lg_ref, a_ref, mg_ref, qb_ref, st_ref,
                      dq_ref, dk_ref, dv_ref, dc_ref):
    seqs, span = dims
    row, col = pair_iota(span)
    upto = (col <= row).astype(F32).astype(BF16)
    diagonal = row == col
    levels = level_masks(span)
    wide = q_ref.shape[1] // HEADS
    tall = v_ref.shape[1] // HEADS
    quarter = st_ref.shape[1]
    per = tall // quarter
    for s in range(seqs):
        at = slice(s * span, (s + 1) * span)
        logits = lg_ref[at, :]
        decays = (jnp.minimum(logits, 0.0) - jnp.log1p(jnp.exp(-jnp.abs(logits)))) / 16.0
        high, rest = two_part(decays)
        qs32, ks32 = q_ref[at, :].astype(F32), k_ref[at, :].astype(F32)
        begun = jnp.exp(dot(upto, high) + dot(upto, rest))
        pair_grads = []
        for h in range(HEADS):
            hs = slice(h * wide, (h + 1) * wide)
            vs = slice(h * tall, (h + 1) * tall)
            mixed, more = two_part(mg_ref[at, vs])
            values = v_ref[at, vs]
            full = dot_t(mixed, values) + dot_t(more, values)
            back = dot_t(values, mixed) + dot_t(values, more)
            pair_grads.append(jnp.where(row >= col, full, back))
            dv_ref[at, vs] = t_dot(a_ref[s * HEADS + h], mixed)
            own = jnp.sum(jnp.where(diagonal, full, 0.0), axis=1, keepdims=True)
            crossed = jnp.zeros((span, wide), F32)
            for q in range(per):
                part = slice(h * tall + q * quarter, h * tall + (q + 1) * quarter)
                crossed += dot(mg_ref[at, part].astype(BF16), st_ref[s * per + q, :, hs])
            dq_ref[at, hs] = own * ks32[:, hs] + begun[:, hs] * crossed
            dk_ref[at, hs] = own * qs32[:, hs]
            dc_ref[at, hs] = qb_ref[at, hs].astype(F32) * crossed
        for sums, _, both, half in levels:
            fade = jnp.exp(dot(sums, high) + dot(sums, rest))
            upper = upper_rows(half, qs32.shape[1], span)
            side = (jnp.where(upper, qs32, ks32) * fade).astype(BF16)
            for h in range(HEADS):
                hs = slice(h * wide, (h + 1) * wide)
                grads = dot(jnp.where(both, pair_grads[h], 0.0).astype(BF16), side[:, hs])
                moved = side[:, hs].astype(F32) * grads
                faded = fade[:, hs] * grads
                over = upper[:, hs]
                dc_ref[at, hs] += jnp.where(over, moved, -moved)
                dq_ref[at, hs] += jnp.where(over, faded, 0.0)
                dk_ref[at, hs] += jnp.where(over, 0.0, faded)


def inputs_back_kernel(dims, idx_ref, dq_ref, dk_ref, dv_ref, dc_ref, ol_ref, kd_ref, v_ref, lg_ref, tot_ref, st_ref,
                       l0, l1, l2, l3, x_ref, hg_ref, g1_own, g1_oth, wq_own, wq_oth, wk_own, wk_oth, wv_own, wv_oth,
                       wg_own, wg_oth, li_own, li_oth, lo_own, lo_oth,
                       tg_ref, ga_ref, llm_ref, llo_ref, g1m_ref, g1o_ref, bm_ref, bo_ref,
                       leaving, logit, bias):
    seqs, span = dims
    load_state(idx_ref, (l0, l1, l2, l3), leaving)
    row, col = pair_iota(span)
    later = (col > row).astype(F32).astype(BF16)
    since = (col >= row).astype(F32).astype(BF16)
    before = (col < row).astype(F32).astype(BF16)
    keys = kd_ref.shape[1]
    vals = v_ref.shape[1]
    wide, tall = keys // HEADS, vals // HEADS
    quarter = st_ref.shape[1]
    per = tall // quarter
    bias_sum = jnp.zeros((1, keys), F32)
    for s in range(seqs):
        at = slice(s * span, (s + 1) * span)
        logits = lg_ref[at, :]
        decays = (jnp.minimum(logits, 0.0) - jnp.log1p(jnp.exp(-jnp.abs(logits)))) / 16.0
        ahead = jnp.exp(mask_dot(later, decays))
        for h in range(HEADS):
            hs = slice(h * wide, (h + 1) * wide)
            faded = kd_ref[at, hs]
            grads = jnp.zeros((span, wide), F32)
            ends = jnp.zeros((1, wide), F32)
            for q in range(per):
                vs = slice(h * tall + q * quarter, h * tall + (q + 1) * quarter)
                at_v = slice(keys * 2 + vs.start, keys * 2 + vs.stop)
                part = leaving[s * per + q, :, hs]
                ga_ref[at, at_v] = (dv_ref[at, vs] + dot_t(faded, part)).astype(BF16)
                grads += dot(v_ref[at, vs], part)
                ends += jnp.sum(
                    st_ref[s * per + q, :, hs].astype(F32) * part.astype(F32), axis=0, keepdims=True
                )
            moved = faded.astype(F32) * grads
            ga_ref[at, keys + h * wide : keys + (h + 1) * wide] = (
                dk_ref[at, hs] + ahead[:, hs] * grads
            ).astype(BF16)
            decay_grad = (
                mask_dot(since, dc_ref[at, hs])
                + mask_dot(before, moved)
                + tot_ref[pl.ds(s, 1), hs] * ends
            )
            logit_grad = decay_grad * sigmoid(-logits[:, hs]) / 16.0
            bias[:, hs] = jnp.sum(logit_grad, axis=0, keepdims=True)
            logit[at, hs] = logit_grad.astype(BF16)
        bias_sum += bias[...]
    bias[...] = bias_sum
    part = lo_own.shape[1]
    bm_ref[...] = bias[:, mine_at(idx_ref, part)]
    bo_ref[...] = bias[:, theirs_at(idx_ref, part)]
    ga_ref[:, 0:keys] = dq_ref[...].astype(BF16)
    ga_ref[:, 2 * keys + vals : 2 * keys + 2 * vals] = ol_ref[...]
    llm, llo = logit[:, mine_at(idx_ref, part)], logit[:, theirs_at(idx_ref, part)]
    llm_ref[...] = llm
    llo_ref[...] = llo
    lrg = (dot_t(llm, lo_own[...]) + dot_t(llo, lo_oth[...])).astype(BF16)
    rank = lrg.shape[1]
    rest = jnp.zeros((lrg.shape[0], 128 - rank), BF16)
    ga_ref[:, 2 * keys + 2 * vals :] = jnp.concatenate([lrg, rest], axis=1)
    qg, kg = ga_ref[:, 0:keys], ga_ref[:, keys : 2 * keys]
    vg = ga_ref[:, 2 * keys : 2 * keys + vals]
    og = ga_ref[:, 2 * keys + vals : 2 * keys + 2 * vals]
    dm = dot_t(qg, wq_own[...]) + dot_t(kg, wk_own[...]) + dot_t(vg, wv_own[...])
    dm = dm + dot_t(og, wg_own[...]) + dot_t(lrg, li_own[...])
    do = dot_t(qg, wq_oth[...]) + dot_t(kg, wk_oth[...]) + dot_t(vg, wv_oth[...])
    do = do + dot_t(og, wg_oth[...]) + dot_t(lrg, li_oth[...])
    half = g1_own.shape[1]
    mine, theirs = mine_at(idx_ref, half), theirs_at(idx_ref, half)
    xm, xo = x_ref[:, mine].astype(F32), x_ref[:, theirs].astype(F32)
    square = jnp.sum(xm * xm, axis=1, keepdims=True) + jnp.sum(xo * xo, axis=1, keepdims=True)
    root = lax.rsqrt(square / (2 * half) + 1e-6)
    g1m_ref[...] = jnp.sum(dm * xm * root, axis=0, keepdims=True)
    g1o_ref[...] = jnp.sum(do * xo * root, axis=0, keepdims=True)
    dm = dm * g1_own[...].astype(F32)
    do = do * g1_oth[...].astype(F32)
    along = jnp.sum(dm * xm, axis=1, keepdims=True) + jnp.sum(do * xo, axis=1, keepdims=True)
    along = along * (root * root * root) / (2 * half)
    tg_ref[:, mine] = hg_ref[:, mine] + dm * root - xm * along
    tg_ref[:, theirs] = hg_ref[:, theirs] + do * root - xo * along


def block_of(position, order):
    block = 0
    for at, bit in enumerate(order):
        if (position >> (3 - at)) & 1:
            block |= bit
    return block


def deal(position, keep_ref, send_ref):
    return keep_ref.at[position] if position < 8 else send_ref.at[position - 8]


def wide_grad_kernel(order, idx_ref, lm_ref, lo_ref, gm_ref, go_ref, keep_ref, send_ref, full):
    place = lax.rem(idx_ref[1], 16)
    full[...] = t_dot(lm_ref[...], gm_ref[...]) + t_dot(lo_ref[...], go_ref[...])
    high = full.shape[0] // 16
    for position in range(16):
        block = block_of(position, order) ^ place
        rows = full[pl.ds(pl.multiple_of(block * high, high), high), :].astype(BF16)
        to = deal(position, keep_ref, send_ref)
        for tile in range(full.shape[1] // 128):
            to[tile * high : (tile + 1) * high, :] = rows[:, tile * 128 : (tile + 1) * 128]


def down_grad_kernel(order, idx_ref, lm_ref, lo_ref, gm_ref, go_ref, keep_ref, send_ref, full):
    place = lax.rem(idx_ref[1], 16)
    full[...] = t_dot(lm_ref[...], gm_ref[...]) + t_dot(lo_ref[...], go_ref[...])
    high = full.shape[0] // 2
    for position in range(16):
        block = block_of(position, order) ^ place
        rows = pl.ds(pl.multiple_of(lax.div(block, 8) * high, 16), high)
        cols = pl.ds(pl.multiple_of(lax.rem(block, 8) * 128, 128), 128)
        deal(position, keep_ref, send_ref)[...] = full[rows, cols].astype(BF16)


def attention_grad_kernel(orders, cuts, idx_ref, nm_ref, no_ref, gm_ref, go_ref, am_ref, ao_ref, hm_ref, ho_ref,
                          lrm_ref, lro_ref, llm_ref, llo_ref, g1_ref, g1o_ref, g2_ref, g2o_ref, b_ref, bo_ref,
                          hg_ref, hgo_ref, k0, s0, k1, s1, k2, s2, full, outer, small):
    place = lax.rem(idx_ref[1], 16)
    full[...] = t_dot(nm_ref[...], gm_ref[...]) + t_dot(no_ref[...], go_ref[...])
    outer[...] = t_dot(am_ref[...], hm_ref[...]) + t_dot(ao_ref[...], ho_ref[...])
    low_out = t_dot(lrm_ref[...], llm_ref[...]) + t_dot(lro_ref[...], llo_ref[...])
    small[...] = jnp.zeros_like(small)
    small[0] = low_out[:, 0:128]
    small[1] = low_out[:, 128:256]
    line = 0
    for first, second in ((g1_ref, g1o_ref), (g2_ref, g2o_ref), (b_ref, bo_ref), (hg_ref, hgo_ref)):
        row = first[...] + second[...]
        for tile in range(row.shape[1] // 128):
            small[2, line : line + 1, :] = row[:, tile * 128 : (tile + 1) * 128]
            line += 1
    high = full.shape[0] // 16
    tiles = full.shape[1] // 128
    for which, refs in enumerate(((k0, s0), (k1, s1), (k2, s2))):
        first, last = cuts[which], cuts[which + 1]
        for position in range(16):
            block = block_of(position, orders[which]) ^ place
            at = pl.ds(pl.multiple_of(block * high, high), high)
            to = deal(position, *refs)
            for tile in range(first, last):
                if tile < tiles:
                    rows = full[at, tile * 128 : (tile + 1) * 128]
                else:
                    rows = outer[at, (tile - tiles) * 128 : (tile - tiles + 1) * 128]
                to[(tile - first) * high : (tile - first + 1) * high, :] = rows.astype(BF16)
            if which == 2:
                to[(last - first) * high :, :] = small[block].astype(BF16)


def wide_open_kernel(order, idx_ref, own_ref, got_ref, out_ref):
    place = lax.rem(idx_ref[1], 16)
    high = out_ref.shape[0] // 16
    for position in range(16):
        block = block_of(position, order) ^ place
        held = deal(position, own_ref, got_ref)
        at = pl.ds(pl.multiple_of(block * high, high), high)
        for tile in range(out_ref.shape[1] // 128):
            out_ref[at, tile * 128 : (tile + 1) * 128] = held[tile * high : (tile + 1) * high, :].astype(F32)


def down_open_kernel(order, idx_ref, own_ref, got_ref, out_ref):
    place = lax.rem(idx_ref[1], 16)
    high = out_ref.shape[0] // 2
    for position in range(16):
        block = block_of(position, order) ^ place
        rows = pl.ds(pl.multiple_of(lax.div(block, 8) * high, 16), high)
        cols = pl.ds(pl.multiple_of(lax.rem(block, 8) * 128, 128), 128)
        out_ref[rows, cols] = deal(position, own_ref, got_ref)[...].astype(F32)


def attention_open_kernel(orders, cuts, idx_ref, o0, r0, o1, r1, o2, r2, q_ref, k_ref, v_ref, og_ref, li_ref, w_ref,
                          lo_ref, g1_ref, g2_ref, b_ref, hg_ref, small):
    place = lax.rem(idx_ref[1], 16)
    high = q_ref.shape[0] // 16
    homes = []
    for ref in (q_ref, k_ref, v_ref, og_ref):
        homes += [(ref, tile) for tile in range(ref.shape[1] // 128)]
    homes.append((li_ref, None))
    homes += [(w_ref, tile) for tile in range(w_ref.shape[1] // 128)]
    for which, refs in enumerate(((o0, r0), (o1, r1), (o2, r2))):
        first, last = cuts[which], cuts[which + 1]
        for position in range(16):
            block = block_of(position, orders[which]) ^ place
            at = pl.ds(pl.multiple_of(block * high, high), high)
            held = deal(position, *refs)
            for tile in range(first, last):
                rows = held[(tile - first) * high : (tile - first + 1) * high, :].astype(F32)
                ref, column = homes[tile]
                if column is None:
                    ref[at, :] = rows[:, : ref.shape[1]]
                else:
                    ref[at, column * 128 : (column + 1) * 128] = rows
            if which == 2:
                small[block] = held[(last - first) * high :, :].astype(F32)
    lo_ref[:, 0:128] = small[0]
    lo_ref[:, 128:256] = small[1]
    line = 0
    for ref in (g1_ref, g2_ref, b_ref, hg_ref):
        for tile in range(ref.shape[1] // 128):
            ref[:, tile * 128 : (tile + 1) * 128] = small[2, line : line + 1, :]
            line += 1


def across(array):
    return lax.ppermute(array, "fsdp", ((0, 1), (1, 0)))


def swap(array, bit):
    count = lax.axis_size("seq")
    return lax.ppermute(array, "seq", tuple((one, one ^ bit) for one in range(count)))


def ahead(array, step):
    count = lax.axis_size("seq")
    return lax.ppermute(
        array,
        "seq",
        tuple((one, one + step) for one in range(count) if 0 <= one + step < count),
    )


def together(arrays):
    return list(lax.optimization_barrier(tuple(arrays)))


def reduce_all(parts, orders):
    count = lax.axis_size("seq")
    kept = [keep for keep, _ in parts]
    sent = [send for _, send in parts]
    for step in range(4):
        got = together([swap(s, order[step]) for s, order in zip(sent, orders)])
        for one, more in enumerate(got):
            if step < 3:
                half = more.shape[0] // 2
                sent[one] = kept[one][half:] + more[half:]
                kept[one] = kept[one][:half] + more[:half]
            else:
                kept[one] = kept[one] + more
    bit = 16
    while bit < count:
        got = together([swap(k, bit) for k in kept])
        kept = [k + more for k, more in zip(kept, got)]
        bit *= 2
    for step in (3, 2, 1, 0):
        got = together([swap(k, order[step]) for k, order in zip(kept, orders)])
        if step:
            kept = [jnp.concatenate([k, more], axis=0) for k, more in zip(kept, got)]
    return list(zip(kept, got))


def scan_states(messages, idx, reverse, mid=None):
    count = lax.axis_size("seq")
    rows, lanes = messages[0].shape
    quarter = rows - 16
    near = [messages[0]] + [swap(messages[o], o) for o in (1, 2, 3)]
    kept = [((4, quarter, lanes), F32), ((4, 1, lanes), F32)]
    total = call("group_total", partial(group_total, reverse), idx, near, [((rows, lanes), BF16)], kept)[0]
    groups = count // 4
    sign = -4 if reverse else 4
    far = [ahead(total, sign * step) for step in range(1, groups)]
    outs = call(
        "group_entering", partial(group_entering, reverse, len(far)), idx, far + near,
        [((quarter, lanes), BF16)] * 4, kept + [((4, quarter, lanes), F32)],
    )
    return [outs[0]] + [swap(outs[o], o) for o in (1, 2, 3)]


def shards(
    tokens,
    lengths,
    first_gain,
    query_weight,
    key_weight,
    value_weight,
    outgate_weight,
    lowrank_in,
    lowrank_out,
    decay_bias,
    head_gain,
    output_weight,
    second_gain,
    gate_weight,
    up_weight,
    down_weight,
    cotangent,
):
    micro_count, pair_count, span, width = tokens.shape
    seqs = micro_count * pair_count
    rows = seqs * span
    dims = (seqs, span)
    core = lax.axis_index("fsdp")
    place = lax.axis_index("seq")
    own_lengths = lax.dynamic_slice_in_dim(lengths, core * pair_count, pair_count, 1).reshape(-1)
    idx = jnp.concatenate([jnp.stack([core, place]).astype(jnp.int32), own_lengths])
    keys, vals, ff = query_weight.shape[1], value_weight.shape[1], gate_weight.shape[1]
    half = query_weight.shape[0]
    tall = vals // HEADS
    quarter = seqs * tall // 4

    x = tokens.reshape(rows, width)
    cot = cotangent.reshape(rows, width)
    first_gain, decay_bias, head_gain, second_gain = (
        a.reshape(1, -1) for a in (first_gain, decay_bias, head_gain, second_gain)
    )
    wk2, g12, li2, lo2, b2 = (across(a) for a in (key_weight, first_gain, lowrank_in, lowrank_out, decay_bias))
    wv2, wq2, wg2 = (across(a) for a in (value_weight, query_weight, outgate_weight))
    hg2, g22, wo2 = (across(a) for a in (head_gain, second_gain, output_weight))
    wgate2, wup2, wdown2 = (across(a) for a in (gate_weight, up_weight, down_weight))

    message = ((quarter + 16, keys), BF16)
    state = ((4, quarter, keys), F32)
    nm, no, k, v, lr, lg, kd, tot, *messages = call(
        "keys", partial(keys_kernel, dims), idx,
        [x, first_gain, g12, key_weight, wk2, value_weight, wv2, lowrank_in, li2, lowrank_out, lo2, decay_bias, b2],
        [((rows, half), BF16), ((rows, half), BF16), ((rows, keys), BF16), ((rows, vals), BF16),
         ((rows, lowrank_in.shape[1]), BF16), ((rows, keys), F32), ((rows, keys), BF16), ((seqs, keys), F32)]
        + [message] * 4,
        [state], flops=2 * rows * width * (keys + vals) + 4 * rows * span * keys,
    )
    pieces = scan_states(messages, idx, False)
    q, og, mix, scores, qb = call(
        "inner", partial(inner_kernel, dims), idx,
        [nm, no, query_weight, wq2, outgate_weight, wg2, k, v, lg],
        [((rows, keys), BF16), ((rows, vals), F32), ((rows, vals), F32), ((seqs * HEADS, span, span), BF16),
         ((rows, keys), BF16)],
        flops=2 * rows * width * (keys + vals) + 60 * rows * span * keys,
    )
    mixture, gm, go, hid, sm, so, st = call(
        "hidden", partial(hidden_kernel, dims), idx,
        [mix, qb, *pieces, og, head_gain, hg2, x, output_weight, wo2, second_gain, g22],
        [((rows, vals), F32), ((rows, vals // 2), BF16), ((rows, vals // 2), BF16), ((rows, width), F32),
         ((rows, half), BF16), ((rows, half), BF16), ((4, quarter, keys), BF16)],
        [((1, tall), F32), ((rows, vals), BF16)], flops=2 * rows * vals * width,
    )
    out, cots, am, ao, gate_grad, up_grad, dm, do = call(
        "ffn", partial(ffn_kernel, dims), idx,
        [sm, so, hid, cot, gate_weight, wgate2, up_weight, wup2, down_weight, wdown2],
        [((rows, width), F32), ((rows, width), BF16), ((rows, ff // 2), BF16), ((rows, ff // 2), BF16),
         ((rows, ff), BF16), ((rows, ff), BF16), ((rows, half), F32), ((rows, half), F32)],
        flops=12 * rows * width * ff, limit=52,
    )

    bits = (1, 2, 4, 8)
    orders = ((bits[0], bits[1], bits[2], bits[3]), (bits[1], bits[2], bits[0], bits[3]), (bits[2], bits[0], bits[1], bits[3]))
    cots2, ao2, so2, gate_grad2, up_grad2 = (across(a) for a in (cots, ao, so, gate_grad, up_grad))
    portion = ff // 128 * (half // 16)
    flat = [((8, portion, 128), BF16)] * 2
    down_parts = call("down_grad", partial(down_grad_kernel, orders[2]), idx, [am, ao2, cots, cots2], flat,
                      [((ff // 2, width), F32)], flops=2 * rows * ff * width)
    gate_parts = call("gate_grad", partial(wide_grad_kernel, orders[0]), idx, [sm, so2, gate_grad, gate_grad2], flat,
                      [((half, ff), F32)], flops=2 * rows * ff * width)
    up_parts = call("up_grad", partial(wide_grad_kernel, orders[1]), idx, [sm, so2, up_grad, up_grad2], flat,
                    [((half, ff), F32)], flops=2 * rows * ff * width)
    gate_halves, up_halves, down_halves = reduce_all([gate_parts, up_parts, down_parts], orders)
    gate_out = call("gate_open", partial(wide_open_kernel, orders[0]), idx, gate_halves, [((half, ff), F32)])[0]
    up_out = call("up_open", partial(wide_open_kernel, orders[1]), idx, up_halves, [((half, ff), F32)])[0]
    down_out = call("down_open", partial(down_open_kernel, orders[2]), idx, down_halves, [((ff // 2, width), F32)])[0]

    hg, hl, mg, ol, g2m, g2o, hgm, hgo, *messages = call(
        "gate_back", partial(gate_back_kernel, dims), idx,
        [hid, dm, do, second_gain, g22, cots, output_weight, wo2, mixture, og, head_gain, hg2, qb, tot],
        [((rows, width), F32), ((rows, width), BF16), ((rows, vals), F32), ((rows, vals), BF16),
         ((1, half), F32), ((1, half), F32), ((1, tall // 2), F32), ((1, tall // 2), F32)] + [message] * 4,
        [((1, tall), F32), ((rows, vals), F32), ((1, tall), F32), state],
        flops=2 * rows * width * vals + 4 * rows * span * keys,
    )
    pieces = scan_states(messages, idx, True)
    dq, dk, dv, dc = call(
        "inner_back", partial(inner_back_kernel, dims), idx, [q, k, v, lg, scores, mg, qb, st],
        [((rows, keys), F32), ((rows, keys), F32), ((rows, vals), F32), ((rows, keys), F32)],
        flops=100 * rows * span * keys,
    )
    lanes = 2 * keys + 2 * vals + 128
    tg, ga, llm, llo, g1m, g1o, bm, bo = call(
        "inputs_back", partial(inputs_back_kernel, dims), idx,
        [dq, dk, dv, dc, ol, kd, v, lg, tot, st, *pieces, x, hg, first_gain, g12, query_weight, wq2, key_weight, wk2,
         value_weight, wv2, outgate_weight, wg2, lowrank_in, li2, lowrank_out, lo2],
        [((rows, width), F32), ((rows, lanes), BF16), ((rows, keys // 2), BF16), ((rows, keys // 2), BF16),
         ((1, half), F32), ((1, half), F32), ((1, keys // 2), F32), ((1, keys // 2), F32)],
        [((4, quarter, keys), BF16), ((rows, keys), BF16), ((1, keys), F32)],
        flops=2 * rows * width * lanes + 8 * rows * span * keys, limit=40,
    )
    go2, hl2, no2, lr2 = (across(a) for a in (go, hl, no, lr))
    ga2, llo2, g1o2, g2o2, bo2, hgo2 = (across(a) for a in (ga, llo, g1o, g2o, bo, hgo))
    tiles = lanes // 128 + width // 128
    cuts = (0, tiles // 3, 2 * tiles // 3, tiles)
    high = half // 16
    shapes = []
    for which in range(3):
        size = (cuts[which + 1] - cuts[which]) * high + (16 if which == 2 else 0)
        shapes += [((8, size, 128), BF16)] * 2
    parts = call(
        "attention_grad", partial(attention_grad_kernel, orders, cuts), idx,
        [nm, no2, ga, ga2, gm, go2, hl, hl2, lr, lr2, llm, llo2, g1m, g1o2, g2m, g2o2, bm, bo2, hgm, hgo2],
        shapes, [((half, lanes), F32), ((vals // 2, width), F32), ((16, 16, 128), F32)],
        flops=2 * 2 * rows * (half * lanes + width * vals // 2),
    )
    halves = reduce_all([parts[0:2], parts[2:4], parts[4:6]], orders)
    opened = call(
        "attention_open", partial(attention_open_kernel, orders, cuts), idx, [a for pair in halves for a in pair],
        [((half, keys), F32), ((half, keys), F32), ((half, vals), F32), ((half, vals), F32),
         ((half, lowrank_in.shape[1]), F32), ((vals // 2, width), F32), ((lowrank_out.shape[0], keys // 2), F32),
         ((1, half), F32), ((1, half), F32), ((1, keys // 2), F32), ((1, tall // 2), F32)],
        [((16, 16, 128), F32)],
    )
    q_out, k_out, v_out, og_out, li_out, w_out, lo_out, g1_out, g2_out, b_out, hg_out = opened
    return (
        out.reshape(tokens.shape),
        tg.reshape(tokens.shape),
        g1_out.reshape(-1),
        q_out,
        k_out,
        v_out,
        og_out,
        li_out,
        lo_out,
        b_out.reshape(-1),
        hg_out.reshape(-1),
        w_out,
        g2_out.reshape(-1),
        gate_out,
        up_out,
        down_out,
    )


def solution(mesh):
    shard, column = P("fsdp", None), P(None, "fsdp")
    stream, line = P(None, "fsdp", "seq", None), P("fsdp")
    weights = (line, shard, shard, shard, shard, shard, column, line, line, shard, line, shard, shard, shard)
    return jax.shard_map(
        shards,
        mesh=mesh,
        in_specs=(stream, P()) + weights + (stream,),
        out_specs=(stream, stream) + weights,
        check_vma=False,
    )
```

time: 1900 us -> 460 us (0.24)
  waiting for transfers between devices: 998 us -> 263 us
  other arithmetic: 323 us -> 3.75 us
  matrix products: 192 us -> 0 us
  blocking collectives: 176 us -> 0 us
  local copies, waits for them, and re-layouts: 174 us -> 14.8 us
  starting transfers between devices: 2.18 us -> 94.7 us
  Pallas kernels: 0 us -> 78 us
    psum x1 -> x0, waiting for transfers between devices: 773 us -> none  [shards(): lax.psum((halves[0], halves[1], halves[2], halves[3], halves[4], halves[5...]
    ppermute x0 -> x95, waiting for transfers between devices: none -> 263 us  [the longest x60 215 us: swap(): lax.ppermute(array, 'seq', tuple(((one, one ^ bit) for one in range(count...]
    dot_general x102 -> x0, matrix products: 192 us -> none  [the longest x20 55.5 us: left_dot(): lax.dot_general(first_op, second_op, (((0,), (0,)), ((), ())), preferred_...]
    all_gather x12 -> x0, waiting for transfers between devices: 187 us -> none  [the longest x4 124 us: carried_in(): gathered = jax.tree.map(lambda a: lax.all_gather(a, axis), part)]
    reduce_sum x25 -> x0, other arithmetic: 170 us -> none  [the longest x4 76.9 us: block_step(): queries[:, :, None] * key_rows[:, None] * decay_weights]
    ppermute x0 -> x95, starting transfers between devices: none -> 94.7 us  [the longest x60 76.1 us: swap(): lax.ppermute(array, 'seq', tuple(((one, one ^ bit) for one in range(count...]
    all_gather x8 -> x0, blocking collectives: 90 us -> none  [the longest x2 78.4 us: carried_in(): gathered = jax.tree.map(lambda a: lax.all_gather(a, axis), part)]
    dynamic_update_slice x16 -> x0, other arithmetic: 85.5 us -> none  [local_mix(): lax.scan(block_step, start_state, (to_blocks(queries), to_blocks(key_rows...]
  transfers between devices with their start and end apart: 23 -> 95, of which waited for: 12 -> 47; matrix products, arithmetic and copies ran while one was open for 33% -> 1% of each run, Pallas kernels for 0% -> 8%
where the time goes in v1:
time: 460 us; the launch traced here: 457 us
  waiting for transfers between devices  263 us (57%)
  starting transfers between devices  94.7 us (21%)
  Pallas kernels  78 us (17%)
  local copies, waits for them, and re-layouts  14.8 us (3%)
    ppermute x60, waiting for transfers between devices, swap(): lax.ppermute(array, 'seq', tuple(((one, one ^ bit) for one in range(count...  215 us
    pallas_call x19, Pallas kernels, call(): pl.pallas_call(body, name=name, out_shape=shapes, in_specs=[SMEM] + [VMEM...  78 us
    ppermute x60, starting transfers between devices, swap(): lax.ppermute(array, 'seq', tuple(((one, one ^ bit) for one in range(count...  76.1 us
    ppermute x29, waiting for transfers between devices, across(): return lax.ppermute(array, 'fsdp', ((0, 1), (1, 0)))  27.7 us
    ppermute x6, waiting for transfers between devices, ahead(): lax.ppermute(array, 'seq', tuple(((one, one + step) for one in range(coun...  20.4 us
    unnamed x106, local copies, waits for them, and re-layouts  13.3 us
    ppermute x6, starting transfers between devices, ahead(): lax.ppermute(array, 'seq', tuple(((one, one + step) for one in range(coun...  12.2 us
  transfers between devices with their start and end apart: 95, of which 47 were waited for; matrix products, arithmetic and copies ran while one was open for 1% of the time, Pallas kernels for 8%

profile of v1, /device:TPU:0, one launch (start us, length us, event | category | flops | bytes accessed | tf_op | source)
XLA Modules:
  0.0 456.5 jit_solution(7263328755972323921)
XLA Ops:
  3.5 3.9 collective-permute-done.5.b_oth
  7.7 4.1 collective-permute-done.g1_oth
  12.9 3.1 collective-permute-done.4.lo_oth
  24.1 2.6 keys.1
  26.8 2.9 collective-permute-start.8
  29.7 4.2 collective-permute-done.8.refs_1_.refs_4_
  35.6 3.6 collective-permute-done.9.refs_2_.refs_5_
  39.3 2.5 collective-permute-start.10
  41.7 3.6 collective-permute-done.10.refs_3_.refs_6_
  46.5 5.5 %collective-permute-start.13 = (bf16[144,512]{1,0:T(8,128)(2,1)S(1)}, bf16[144,512]{1,0:T(8,128)(2,1)S(1)}, u32[]{:S(2)}, u32[]{:S(2)}) collective-permute-start(bf16[144,512]{1,0:T(8,128)(2,1)S(1)} %group_total.2), channel_id=1, source_target_pairs={{0,24},{2,26},{4,28},{6,30},{1,25},{3,27},{5,29},{7,31}} | collective-permute-start | bytes 442376 | tf_op jit(solution)/shard_map/ppermute | solution.py:678
  53.3 2.9 collective-permute-done.13.refs_2_
  59.4 2.4 collective-permute-done.11.refs_0_
  65.9 2.7 collective-permute-done.14.e1
  68.6 2.5 collective-permute-start.16
  71.1 6.0 %inner.1 = (bf16[256,512]{1,0:T(8,128)(2,1)S(1)}, f32[256,1024]{1,0:T(8,128)S(1)}, f32[256,1024]{1,0:T(8,128)S(1)}, bf16[8,128,128]{2,1,0:T(8,128)(2,1)S(1)}, bf16[256,512]{1,0:T(8,128)(2,1)S(1)}) custom-call(s32[4]{0:T(128)S(1)} %pad_add_fusion.idx_ref, bf16[256,512]{1,0:T(8,128)(2,1)S(1)} %get-tuple-element.151.nm_ref, ...), custom_call_target="tpu_custom_call" | custom-call | flops 1811939328 | bytes 7864320 | tf_op jit(solution)/shard_map/inner/pallas_call | solution.py:99
  77.9 2.3 hidden.1
  83.5 18.8 %ffn.1 = (f32[256,1024]{1,0:T(8,128)}, bf16[256,1024]{1,0:T(8,128)(2,1)S(1)}, bf16[256,1408]{1,0:T(8,128)(2,1)}, bf16[256,1408]{1,0:T(8,128)(2,1)}, bf16[256,281...) custom-call(s32[4]{0:T(128)S(1)} %pad_add_fusion.idx_ref, ...), custom_call_target="tpu_custom_call" | custom-call | flops 8858370048 | bytes 26345472 | tf_op jit(solution)/shard_map/ffn/pallas_call | solution.py:99
  103.6 3.2 gate_back.1
  107.9 2.5 collective-permute-start.25
  110.3 3.3 collective-permute-done.23.refs_1_.refs_4_
  113.6 1.9 collective-permute-done.24.refs_2_.refs_5_
  120.2 9.6 %collective-permute-done.28.refs_2_ = bf16[144,512]{1,0:T(8,128)(2,1)S(1)} collective-permute-done((bf16[144,512]{1,0:T(8,128)(2,1)S(1)}, bf16[144,512]{1,0:T(8,128)(2,1)S(1)}, u32[]{:S(2)}, u32[]{:S(2)}) %collective-permute-start.28) | collective-permute-done | bytes 147488 | tf_op jit(solution)/shard_map/ppermute | solution.py:678
  129.7 3.9 collective-permute-done.27.refs_1_
  138.2 5.8 %inner_back.1 = (f32[256,512]{1,0:T(8,128)S(1)}, f32[256,512]{1,0:T(8,128)S(1)}, f32[256,1024]{1,0:T(8,128)S(1)}, f32[256,512]{1,0:T(8,128)S(1)}) custom-call(s32[4]{0:T(128)S(1)} %pad_add_fusion.idx_ref, bf16[256,512]{1,0:T(8,128)(2,1)S(1)} %copy-done.46, bf16[256,512]{1,0:T(8,128)(2,1)S(1)} %copy-done.42, bf16[256,1024]{1,0:T(8,128)(2,1)S(1)} %copy-done.18, ...), custom_call_target="tpu_custom_call" | custom-call | flops 1677721600 | bytes 6291456 | tf_op jit(solution)/shard_map/inner_back/pallas_call | solution.py:99
  144.1 6.4 %inputs_back.1 = (f32[256,1024]{1,0:T(8,128)}, bf16[256,3200]{1,0:T(8,128)(2,1)}, bf16[256,256]{1,0:T(8,128)(2,1)S(1)}, bf16[256,256]{1,0:T(8,128)(2,1)S(1)}, f3...) custom-call(s32[4]{0:T(128)S(1)} %pad_add_fusion.idx_ref, ...), custom_call_target="tpu_custom_call" | custom-call | flops 1811939328 | bytes 16379904 | tf_op jit(solution)/shard_map/inputs_back/pallas_call | solution.py:99
  151.7 5.7 %collective-permute-done.36.lro_ref = bf16[256,16]{1,0:T(8,128)(2,1)S(1)} collective-permute-done((bf16[256,16]{1,0:T(8,128)(2,1)S(1)}, bf16[256,16]{1,0:T(8,128)(2,1)S(1)}, u32[]{:S(2)}, u32[]{:S(2)}) %collective-permute-start.36) | collective-permute-done | bytes 8224 | tf_op jit(solution)/shard_map/ppermute | solution.py:668
  157.9 3.1 collective-permute-done.34.ao_ref
  169.6 3.7 attention_grad.1
  174.2 3.0 down_grad.1
  177.3 3.5 collective-permute-start.73
  180.7 2.5 gate_grad.1
  186.2 2.5 up_grad.1
  188.7 3.6 collective-permute-done.42
  193.9 9.7 %collective-permute-done.43 = bf16[8,352,128]{2,1,0:T(8,128)(2,1)S(1)} collective-permute-done((bf16[8,352,128]{2,1,0:T(8,128)(2,1)S(1)}, bf16[8,352,128]{2,1,0:T(8,128)(2,1)S(1)}, u32[]{:S(2)}, u32[]{:S(2)}) %collective-permute-start.43) | collective-permute-done | bytes 720928 | tf_op jit(solution)/shard_map/ppermute | solution.py:673
  203.6 25.5 %collective-permute-done.44 = bf16[8,368,128]{2,1,0:T(8,128)(2,1)S(1)} collective-permute-done((bf16[8,368,128]{2,1,0:T(8,128)(2,1)S(1)}, bf16[8,368,128]{2,1,0:T(8,128)(2,1)S(1)}, u32[]{:S(2)}, u32[]{:S(2)}) %collective-permute-start.44) | collective-permute-done | bytes 753696 | tf_op jit(solution)/shard_map/ppermute | solution.py:673
  229.2 1.8 collective-permute-start.46
  235.6 4.9 %collective-permute-done.46 = bf16[4,352,128]{2,1,0:T(8,128)(2,1)S(1)} collective-permute-done((bf16[4,352,128]{2,1,0:T(8,128)(2,1)S(1)}, bf16[4,352,128]{2,1,0:T(8,128)(2,1)S(1)}, u32[]{:S(2)}, u32[]{:S(2)}) %collective-permute-start.46) | collective-permute-done | bytes 360480 | tf_op jit(solution)/shard_map/ppermute | solution.py:673
  241.2 3.3 collective-permute-done.47
  247.1 14.9 %collective-permute-done.49 = bf16[2,352,128]{2,1,0:T(8,128)(2,1)S(1)} collective-permute-done((bf16[2,352,128]{2,1,0:T(8,128)(2,1)S(1)}, bf16[2,352,128]{2,1,0:T(8,128)(2,1)S(1)}, u32[]{:S(2)}, u32[]{:S(2)}) %collective-permute-start.49) | collective-permute-done | bytes 180256 | tf_op jit(solution)/shard_map/ppermute | solution.py:673
  262.5 3.0 collective-permute-start.53
  265.5 6.4 %collective-permute-done.52 = bf16[1,352,128]{2,1,0:T(8,128)(2,1)S(1)} collective-permute-done((bf16[1,352,128]{2,1,0:T(8,128)(2,1)S(1)}, bf16[1,352,128]{2,1,0:T(8,128)(2,1)S(1)}, u32[]{:S(2)}, u32[]{:S(2)}) %collective-permute-start.52) | collective-permute-done | bytes 90144 | tf_op jit(solution)/shard_map/ppermute | solution.py:673
  271.9 5.4 %collective-permute-done.51 = bf16[1,352,128]{2,1,0:T(8,128)(2,1)S(1)} collective-permute-done((bf16[1,352,128]{2,1,0:T(8,128)(2,1)S(1)}, bf16[1,352,128]{2,1,0:T(8,128)(2,1)S(1)}, u32[]{:S(2)}, u32[]{:S(2)}) %collective-permute-start.51) | collective-permute-done | bytes 90144 | tf_op jit(solution)/shard_map/ppermute | solution.py:673
  281.2 2.0 collective-permute-start.54
  286.6 4.9 %collective-permute-done.77 = bf16[2,704,128]{2,1,0:T(8,128)(2,1)S(1)} collective-permute-done((bf16[2,704,128]{2,1,0:T(8,128)(2,1)S(1)}, bf16[2,704,128]{2,1,0:T(8,128)(2,1)S(1)}, u32[]{:S(2)}, u32[]{:S(2)}) %collective-permute-start.77) | collective-permute-done | bytes 360480 | tf_op jit(solution)/shard_map/ppermute | solution.py:673
  291.6 3.0 collective-permute-start.81
  294.7 3.0 collective-permute-start.55
  297.7 20.2 %collective-permute-done.55 = bf16[1,352,128]{2,1,0:T(8,128)(2,1)S(1)} collective-permute-done((bf16[1,352,128]{2,1,0:T(8,128)(2,1)S(1)}, bf16[1,352,128]{2,1,0:T(8,128)(2,1)S(1)}, u32[]{:S(2)}, u32[]{:S(2)}) %collective-permute-start.55) | collective-permute-done | bytes 90144 | tf_op jit(solution)/shard_map/ppermute | solution.py:673
  318.1 2.9 collective-permute-start.84
  321.9 2.6 collective-permute-start.59
  324.5 10.7 %collective-permute-done.83 = bf16[1,704,128]{2,1,0:T(8,128)(2,1)S(1)} collective-permute-done((bf16[1,704,128]{2,1,0:T(8,128)(2,1)S(1)}, bf16[1,704,128]{2,1,0:T(8,128)(2,1)S(1)}, u32[]{:S(2)}, u32[]{:S(2)}) %collective-permute-start.83) | collective-permute-done | bytes 180256 | tf_op jit(solution)/shard_map/ppermute | solution.py:673
  335.2 3.9 collective-permute-done.84
  339.1 3.8 collective-permute-done.85
  342.9 3.6 collective-permute-start.88
  347.5 2.1 collective-permute-start.57
  349.6 11.5 %collective-permute-done.57 = bf16[2,352,128]{2,1,0:T(8,128)(2,1)S(1)} collective-permute-done((bf16[2,352,128]{2,1,0:T(8,128)(2,1)S(1)}, bf16[2,352,128]{2,1,0:T(8,128)(2,1)S(1)}, u32[]{:S(2)}, u32[]{:S(2)}) %collective-permute-start.57) | collective-permute-done | bytes 180256 | tf_op jit(solution)/shard_map/ppermute | solution.py:673
  366.4 6.2 %collective-permute-done.61 = bf16[4,352,128]{2,1,0:T(8,128)(2,1)S(1)} collective-permute-done((bf16[4,352,128]{2,1,0:T(8,128)(2,1)S(1)}, bf16[4,352,128]{2,1,0:T(8,128)(2,1)S(1)}, u32[]{:S(2)}, u32[]{:S(2)}) %collective-permute-start.61) | collective-permute-done | bytes 360480 | tf_op jit(solution)/shard_map/ppermute | solution.py:673
  372.9 15.8 %collective-permute-done.60 = bf16[4,352,128]{2,1,0:T(8,128)(2,1)S(1)} collective-permute-done((bf16[4,352,128]{2,1,0:T(8,128)(2,1)S(1)}, bf16[4,352,128]{2,1,0:T(8,128)(2,1)S(1)}, u32[]{:S(2)}, u32[]{:S(2)}) %collective-permute-start.60) | collective-permute-done | bytes 360480 | tf_op jit(solution)/shard_map/ppermute | solution.py:673
  393.6 1.8 collective-permute-start.65
  395.5 12.4 %collective-permute-done.64.r1 = bf16[8,352,128]{2,1,0:T(8,128)(2,1)S(1)} collective-permute-done((bf16[8,352,128]{2,1,0:T(8,128)(2,1)S(1)}, bf16[8,352,128]{2,1,0:T(8,128)(2,1)S(1)}, u32[]{:S(2)}, u32[]{:S(2)}) %collective-permute-start.64) | collective-permute-done | bytes 720928 | tf_op jit(solution)/shard_map/ppermute | solution.py:673
  408.7 29.1 %collective-permute-done.63.r0 = bf16[8,352,128]{2,1,0:T(8,128)(2,1)S(1)} collective-permute-done((bf16[8,352,128]{2,1,0:T(8,128)(2,1)S(1)}, bf16[8,352,128]{2,1,0:T(8,128)(2,1)S(1)}, u32[]{:S(2)}, u32[]{:S(2)}) %collective-permute-start.63) | collective-permute-done | bytes 720928 | tf_op jit(solution)/shard_map/ppermute | solution.py:673
  437.8 4.0 attention_open.1
  442.5 4.3 gate_open.1
  446.8 4.3 up_open.1
  451.1 5.2 %down_open.1 = f32[1408,1024]{1,0:T(8,128)} custom-call(s32[4]{0:T(128)S(1)} %pad_add_fusion.idx_ref, bf16[8,704,128]{2,1,0:T(8,128)(2,1)} %pad_maximum_fusion.2.own_ref, bf16[8,704,128]{2,1,0:T(8,128)(2,1)} %collective-permute-done.94.got_ref), custom_call_target="tpu_custom_call" | custom-call | bytes 8650752 | tf_op jit(solution)/shard_map/down_open/pallas_call | solution.py:99
  (298 shorter events, 85.0 us)
Async XLA Ops:
  0.7 19.3 %collective-permute-start.2 = (bf16[512,1024]{1,0:T(8,128)(2,1)}, bf16[512,1024]{1,0:T(8,128)(2,1)S(1)}, u32[]{:S(2)}, u32[]{:S(2)}) collective-permute-start(bf16[512,1024]{1,0:T(8,128)(2,1)} %wv_own.3), channel_id=1, source_target_pairs={{0,1},{1,0},{2,3},{3,2},{4,5},{5,4},{6,7},{7,6},{8,9},{9,8},{10,11... | collective-permute-start | bytes 3145736 | tf_op jit(solution)/shard_map/ppermute | solution.py:668
  1.2 82.3 %collective-permute-start.20 = (bf16[512,2816]{1,0:T(8,128)(2,1)}, bf16[512,2816]{1,0:T(8,128)(2,1)}, u32[]{:S(2)}, u32[]{:S(2)}) collective-permute-start(bf16[512,2816]{1,0:T(8,128)(2,1)} %wg_own.4), channel_id=1, source_target_pairs={{0,1},{1,0},{2,3},{3,2},{4,5},{5,4},{6,7},{7,6},{8,9},{9,8},{10,11... | collective-permute-start | bytes 8650760 | tf_op jit(solution)/shard_map/ppermute | solution.py:668
  1.3 82.2 %collective-permute-start.21 = (bf16[512,2816]{1,0:T(8,128)(2,1)}, bf16[512,2816]{1,0:T(8,128)(2,1)}, u32[]{:S(2)}, u32[]{:S(2)}) collective-permute-start(bf16[512,2816]{1,0:T(8,128)(2,1)} %wu_own.1), channel_id=1, source_target_pairs={{0,1},{1,0},{2,3},{3,2},{4,5},{5,4},{6,7},{7,6},{8,9},{9,8},{10,11... | collective-permute-start | bytes 8650760 | tf_op jit(solution)/shard_map/ppermute | solution.py:668
  1.7 81.8 %collective-permute-start.22 = (bf16[1408,1024]{1,0:T(8,128)(2,1)}, bf16[1408,1024]{1,0:T(8,128)(2,1)}, u32[]{:S(2)}, u32[]{:S(2)}) collective-permute-start(bf16[1408,1024]{1,0:T(8,128)(2,1)} %wd_own.1), channel_id=1, source_target_pairs={{0,1},{1,0},{2,3},{3,2},{4,5},{5,4},{6,7},{7,6},{8,9},{9,8},{10,11... | collective-permute-start | bytes 8650760 | tf_op jit(solution)/shard_map/ppermute | solution.py:668
  19.9 32.1 %collective-permute-start.6 = (bf16[512,512]{1,0:T(8,128)(2,1)}, bf16[512,512]{1,0:T(8,128)(2,1)S(1)}, u32[]{:S(2)}, u32[]{:S(2)}) collective-permute-start(bf16[512,512]{1,0:T(8,128)(2,1)} %wq_own.3), channel_id=1, source_target_pairs={{0,1},{1,0},{2,3},{3,2},{4,5},{5,4},{6,7},{7,6},{8,9},{9,8},{10,11... | collective-permute-start | bytes 1572872 | tf_op jit(solution)/shard_map/ppermute | solution.py:668
  46.5 9.7 %collective-permute-start.13 = (bf16[144,512]{1,0:T(8,128)(2,1)S(1)}, bf16[144,512]{1,0:T(8,128)(2,1)S(1)}, u32[]{:S(2)}, u32[]{:S(2)}) collective-permute-start(bf16[144,512]{1,0:T(8,128)(2,1)S(1)} %group_total.2), channel_id=1, source_target_pairs={{0,24},{2,26},{4,28},{6,30},{1,25},{3,27},{5,29},{7,31}} | collective-permute-start | bytes 442376 | tf_op jit(solution)/shard_map/ppermute | solution.py:678
  64.4 13.5 %collective-permute-start.15 = (bf16[128,512]{1,0:T(8,128)(2,1)S(1)}, bf16[128,512]{1,0:T(8,128)(2,1)S(1)}, u32[]{:S(2)}, u32[]{:S(2)}) collective-permute-start(bf16[128,512]{1,0:T(8,128)(2,1)S(1)} %get-tuple-element.164), channel_id=1, source_target_pairs={{0,4},{2,6},{4,0},{6,2},{8,12},{10,14},{12,8},{14,10},{16,20},{18,... | collective-permute-start | bytes 393224 | tf_op jit(solution)/shard_map/ppermute | solution.py:673
  68.6 9.3 %collective-permute-start.16 = (bf16[128,512]{1,0:T(8,128)(2,1)S(1)}, bf16[128,512]{1,0:T(8,128)(2,1)S(1)}, u32[]{:S(2)}, u32[]{:S(2)}) collective-permute-start(bf16[128,512]{1,0:T(8,128)(2,1)S(1)} %get-tuple-element.165), channel_id=1, source_target_pairs={{0,6},{2,4},{4,2},{6,0},{8,14},{10,12},{12,10},{14,8},{16,22},{18,... | collective-permute-start | bytes 393224 | tf_op jit(solution)/shard_map/ppermute | solution.py:673
  107.4 8.2 %collective-permute-start.24 = (bf16[144,512]{1,0:T(8,128)(2,1)S(1)}, bf16[144,512]{1,0:T(8,128)(2,1)S(1)}, u32[]{:S(2)}, u32[]{:S(2)}) collective-permute-start(bf16[144,512]{1,0:T(8,128)(2,1)S(1)} %get-tuple-element.188), channel_id=1, source_target_pairs={{0,4},{2,6},{4,0},{6,2},{8,12},{10,14},{12,8},{14,10},{16,20},{18,... | collective-permute-start | bytes 442376 | tf_op jit(solution)/shard_map/ppermute | solution.py:673
  116.3 13.5 %collective-permute-start.28 = (bf16[144,512]{1,0:T(8,128)(2,1)S(1)}, bf16[144,512]{1,0:T(8,128)(2,1)S(1)}, u32[]{:S(2)}, u32[]{:S(2)}) collective-permute-start(bf16[144,512]{1,0:T(8,128)(2,1)S(1)} %group_total.3), channel_id=1, source_target_pairs={{24,0},{26,2},{28,4},{30,6},{25,1},{27,3},{29,5},{31,7}} | collective-permute-start | bytes 442376 | tf_op jit(solution)/shard_map/ppermute | solution.py:678
  117.6 16.1 %collective-permute-start.27 = (bf16[144,512]{1,0:T(8,128)(2,1)S(1)}, bf16[144,512]{1,0:T(8,128)(2,1)S(1)}, u32[]{:S(2)}, u32[]{:S(2)}) collective-permute-start(bf16[144,512]{1,0:T(8,128)(2,1)S(1)} %group_total.3), channel_id=1, source_target_pairs={{16,0},{18,2},{20,4},{22,6},{24,8},{26,10},{28,12},{30,14},{17,1},... | collective-permute-start | bytes 442376 | tf_op jit(solution)/shard_map/ppermute | solution.py:678
  118.9 14.8 %collective-permute-start.26 = (bf16[144,512]{1,0:T(8,128)(2,1)S(1)}, bf16[144,512]{1,0:T(8,128)(2,1)S(1)}, u32[]{:S(2)}, u32[]{:S(2)}) collective-permute-start(bf16[144,512]{1,0:T(8,128)(2,1)S(1)} %group_total.3), channel_id=1, source_target_pairs={{8,0},{10,2},{12,4},{14,6},{16,8},{18,10},{20,12},{22,14},{24,16},... | collective-permute-start | bytes 442376 | tf_op jit(solution)/shard_map/ppermute | solution.py:678
  134.6 9.4 %collective-permute-start.29 = (bf16[128,512]{1,0:T(8,128)(2,1)S(1)}, bf16[128,512]{1,0:T(8,128)(2,1)S(1)}, u32[]{:S(2)}, u32[]{:S(2)}) collective-permute-start(bf16[128,512]{1,0:T(8,128)(2,1)S(1)} %get-tuple-element.191), channel_id=1, source_target_pairs={{0,2},{2,0},{4,6},{6,4},{8,10},{10,8},{12,14},{14,12},{16,18},{18,... | collective-permute-start | bytes 393224 | tf_op jit(solution)/shard_map/ppermute | solution.py:673
  135.4 8.6 %collective-permute-start.30 = (bf16[128,512]{1,0:T(8,128)(2,1)S(1)}, bf16[128,512]{1,0:T(8,128)(2,1)S(1)}, u32[]{:S(2)}, u32[]{:S(2)}) collective-permute-start(bf16[128,512]{1,0:T(8,128)(2,1)S(1)} %get-tuple-element.192), channel_id=1, source_target_pairs={{0,4},{2,6},{4,0},{6,2},{8,12},{10,14},{12,8},{14,10},{16,20},{18,... | collective-permute-start | bytes 393224 | tf_op jit(solution)/shard_map/ppermute | solution.py:673
  150.6 16.5 %collective-permute-start.33 = (bf16[256,3200]{1,0:T(8,128)(2,1)}, bf16[256,3200]{1,0:T(8,128)(2,1)S(1)}, u32[]{:S(2)}, u32[]{:S(2)}) collective-permute-start(bf16[256,3200]{1,0:T(8,128)(2,1)} %get-tuple-element.196.gm_ref), channel_id=1, source_target_pairs={{0,1},{1,0},{2,3},{3,2},{4,5},{5,4},{6,7},{7,6},{8,9},{9,8},{10,11... | collective-permute-start | bytes 4915208 | tf_op jit(solution)/shard_map/ppermute | solution.py:668
  151.1 29.6 %collective-permute-start.67 = (bf16[256,2816]{1,0:T(8,128)(2,1)S(1)}, bf16[256,2816]{1,0:T(8,128)(2,1)S(1)}, u32[]{:S(2)}, u32[]{:S(2)}) collective-permute-start(bf16[256,2816]{1,0:T(8,128)(2,1)S(1)} %copy-done.28), channel_id=1, source_target_pairs={{0,1},{1,0},{2,3},{3,2},{4,5},{5,4},{6,7},{7,6},{8,9},{9,8},{10,11... | collective-permute-start | bytes 4325384 | tf_op jit(solution)/shard_map/ppermute | solution.py:668
  151.2 14.6 %collective-permute-start.35 = (bf16[256,1024]{1,0:T(8,128)(2,1)S(1)}, bf16[256,1024]{1,0:T(8,128)(2,1)S(1)}, u32[]{:S(2)}, u32[]{:S(2)}) collective-permute-start(bf16[256,1024]{1,0:T(8,128)(2,1)S(1)} %get-tuple-element.199.hm_ref), channel_id=1, source_target_pairs={{0,1},{1,0},{2,3},{3,2},{4,5},{5,4},{6,7},{7,6},{8,9},{9,8},{10,11... | collective-permute-start | bytes 1572872 | tf_op jit(solution)/shard_map/ppermute | solution.py:668
  157.4 28.8 %collective-permute-start.69 = (bf16[256,2816]{1,0:T(8,128)(2,1)S(1)}, bf16[256,2816]{1,0:T(8,128)(2,1)S(1)}, u32[]{:S(2)}, u32[]{:S(2)}) collective-permute-start(bf16[256,2816]{1,0:T(8,128)(2,1)S(1)} %copy-done.27), channel_id=1, source_target_pairs={{0,1},{1,0},{2,3},{3,2},{4,5},{5,4},{6,7},{7,6},{8,9},{9,8},{10,11... | collective-permute-start | bytes 4325384 | tf_op jit(solution)/shard_map/ppermute | solution.py:668
  165.8 8.4 %collective-permute-start.71 = (bf16[256,1408]{1,0:T(8,128)(2,1)S(1)}, bf16[256,1408]{1,0:T(8,128)(2,1)S(1)}, u32[]{:S(2)}, u32[]{:S(2)}) collective-permute-start(bf16[256,1408]{1,0:T(8,128)(2,1)S(1)} %copy-done.51), channel_id=1, source_target_pairs={{0,1},{1,0},{2,3},{3,2},{4,5},{5,4},{6,7},{7,6},{8,9},{9,8},{10,11... | collective-permute-start | bytes 2162696 | tf_op jit(solution)/shard_map/ppermute | solution.py:668
  173.4 19.0 %collective-permute-start.42 = (bf16[8,352,128]{2,1,0:T(8,128)(2,1)S(1)}, bf16[8,352,128]{2,1,0:T(8,128)(2,1)S(1)}, u32[]{:S(2)}, u32[]{:S(2)}) collective-permute-start(bf16[8,352,128]{2,1,0:T(8,128)(2,1)S(1)} %get-tuple-element.212), channel_id=1, source_target_pairs={{0,2},{2,0},{4,6},{6,4},{8,10},{10,8},{12,14},{14,12},{16,18},{18,... | collective-permute-start | bytes 2162696 | tf_op jit(solution)/shard_map/ppermute | solution.py:673
  177.3 55.5 %collective-permute-start.73 = (bf16[8,704,128]{2,1,0:T(8,128)(2,1)S(1)}, bf16[8,704,128]{2,1,0:T(8,128)(2,1)S(1)}, u32[]{:S(2)}, u32[]{:S(2)}) collective-permute-start(bf16[8,704,128]{2,1,0:T(8,128)(2,1)S(1)} %get-tuple-element.259), channel_id=1, source_target_pairs={{0,8},{2,10},{4,12},{6,14},{8,0},{10,2},{12,4},{14,6},{16,24},{18,... | collective-permute-start | bytes 4325384 | tf_op jit(solution)/shard_map/ppermute | solution.py:673
  183.3 50.8 %collective-permute-start.68 = (bf16[8,704,128]{2,1,0:T(8,128)(2,1)S(1)}, bf16[8,704,128]{2,1,0:T(8,128)(2,1)S(1)}, u32[]{:S(2)}, u32[]{:S(2)}) collective-permute-start(bf16[8,704,128]{2,1,0:T(8,128)(2,1)S(1)} %get-tuple-element.254), channel_id=1, source_target_pairs={{0,2},{2,0},{4,6},{6,4},{8,10},{10,8},{12,14},{14,12},{16,18},{18,... | collective-permute-start | bytes 4325384 | tf_op jit(solution)/shard_map/ppermute | solution.py:673
  184.6 19.0 %collective-permute-start.43 = (bf16[8,352,128]{2,1,0:T(8,128)(2,1)S(1)}, bf16[8,352,128]{2,1,0:T(8,128)(2,1)S(1)}, u32[]{:S(2)}, u32[]{:S(2)}) collective-permute-start(bf16[8,352,128]{2,1,0:T(8,128)(2,1)S(1)} %get-tuple-element.213), channel_id=1, source_target_pairs={{0,4},{2,6},{4,0},{6,2},{8,12},{10,14},{12,8},{14,10},{16,20},{18,... | collective-permute-start | bytes 2162696 | tf_op jit(solution)/shard_map/ppermute | solution.py:673
  186.2 42.9 %collective-permute-start.44 = (bf16[8,368,128]{2,1,0:T(8,128)(2,1)S(1)}, bf16[8,368,128]{2,1,0:T(8,128)(2,1)S(1)}, u32[]{:S(2)}, u32[]{:S(2)}) collective-permute-start(bf16[8,368,128]{2,1,0:T(8,128)(2,1)S(1)} %get-tuple-element.214), channel_id=1, source_target_pairs={{0,8},{2,10},{4,12},{6,14},{8,0},{10,2},{12,4},{14,6},{16,24},{18,... | collective-permute-start | bytes 2261000 | tf_op jit(solution)/shard_map/ppermute | solution.py:673
  192.4 41.7 %collective-permute-start.70 = (bf16[8,704,128]{2,1,0:T(8,128)(2,1)S(1)}, bf16[8,704,128]{2,1,0:T(8,128)(2,1)S(1)}, u32[]{:S(2)}, u32[]{:S(2)}) collective-permute-start(bf16[8,704,128]{2,1,0:T(8,128)(2,1)S(1)} %get-tuple-element.256), channel_id=1, source_target_pairs={{0,4},{2,6},{4,0},{6,2},{8,12},{10,14},{12,8},{14,10},{16,20},{18,... | collective-permute-start | bytes 4325384 | tf_op jit(solution)/shard_map/ppermute | solution.py:673
  229.2 11.4 %collective-permute-start.46 = (bf16[4,352,128]{2,1,0:T(8,128)(2,1)S(1)}, bf16[4,352,128]{2,1,0:T(8,128)(2,1)S(1)}, u32[]{:S(2)}, u32[]{:S(2)}) collective-permute-start(bf16[4,352,128]{2,1,0:T(8,128)(2,1)S(1)} %get-tuple-element.317), channel_id=1, source_target_pairs={{0,8},{2,10},{4,12},{6,14},{8,0},{10,2},{12,4},{14,6},{16,24},{18,... | collective-permute-start | bytes 1081352 | tf_op jit(solution)/shard_map/ppermute | solution.py:673
  231.1 10.1 %collective-permute-start.45 = (bf16[4,352,128]{2,1,0:T(8,128)(2,1)S(1)}, bf16[4,352,128]{2,1,0:T(8,128)(2,1)S(1)}, u32[]{:S(2)}, u32[]{:S(2)}) collective-permute-start(bf16[4,352,128]{2,1,0:T(8,128)(2,1)S(1)} %get-tuple-element.318), channel_id=1, source_target_pairs={{0,4},{2,6},{4,0},{6,2},{8,12},{10,14},{12,8},{14,10},{16,20},{18,... | collective-permute-start | bytes 1081352 | tf_op jit(solution)/shard_map/ppermute | solution.py:673
  232.8 11.8 %collective-permute-start.47 = (bf16[4,368,128]{2,1,0:T(8,128)(2,1)S(1)}, bf16[4,368,128]{2,1,0:T(8,128)(2,1)S(1)}, u32[]{:S(2)}, u32[]{:S(2)}) collective-permute-start(bf16[4,368,128]{2,1,0:T(8,128)(2,1)S(1)} %get-tuple-element.309), channel_id=1, source_target_pairs={{0,2},{2,0},{4,6},{6,4},{8,10},{10,8},{12,14},{14,12},{16,18},{18,... | collective-permute-start | bytes 1130504 | tf_op jit(solution)/shard_map/ppermute | solution.py:673
  234.2 43.1 %collective-permute-start.76 = (bf16[4,704,128]{2,1,0:T(8,128)(2,1)S(1)}, bf16[4,704,128]{2,1,0:T(8,128)(2,1)S(1)}, u32[]{:S(2)}, u32[]{:S(2)}) collective-permute-start(bf16[4,704,128]{2,1,0:T(8,128)(2,1)S(1)} %get-tuple-element.303), channel_id=1, source_target_pairs={{0,2},{2,0},{4,6},{6,4},{8,10},{10,8},{12,14},{14,12},{16,18},{18,... | collective-permute-start | bytes 2162696 | tf_op jit(solution)/shard_map/ppermute | solution.py:673
  235.3 42.1 %collective-permute-start.75 = (bf16[4,704,128]{2,1,0:T(8,128)(2,1)S(1)}, bf16[4,704,128]{2,1,0:T(8,128)(2,1)S(1)}, u32[]{:S(2)}, u32[]{:S(2)}) collective-permute-start(bf16[4,704,128]{2,1,0:T(8,128)(2,1)S(1)} %get-tuple-element.305), channel_id=1, source_target_pairs={{0,8},{2,10},{4,12},{6,14},{8,0},{10,2},{12,4},{14,6},{16,24},{18,... | collective-permute-start | bytes 2162696 | tf_op jit(solution)/shard_map/ppermute | solution.py:673
  244.6 17.4 %collective-permute-start.49 = (bf16[2,352,128]{2,1,0:T(8,128)(2,1)S(1)}, bf16[2,352,128]{2,1,0:T(8,128)(2,1)S(1)}, u32[]{:S(2)}, u32[]{:S(2)}) collective-permute-start(bf16[2,352,128]{2,1,0:T(8,128)(2,1)S(1)} %get-tuple-element.323), channel_id=1, source_target_pairs={{0,2},{2,0},{4,6},{6,4},{8,10},{10,8},{12,14},{14,12},{16,18},{18,... | collective-permute-start | bytes 540680 | tf_op jit(solution)/shard_map/ppermute | solution.py:673
  245.9 16.5 %collective-permute-start.48 = (bf16[2,352,128]{2,1,0:T(8,128)(2,1)S(1)}, bf16[2,352,128]{2,1,0:T(8,128)(2,1)S(1)}, u32[]{:S(2)}, u32[]{:S(2)}) collective-permute-start(bf16[2,352,128]{2,1,0:T(8,128)(2,1)S(1)} %get-tuple-element.324), channel_id=1, source_target_pairs={{0,8},{2,10},{4,12},{6,14},{8,0},{10,2},{12,4},{14,6},{16,24},{18,... | collective-permute-start | bytes 540680 | tf_op jit(solution)/shard_map/ppermute | solution.py:673
  246.3 16.1 %collective-permute-start.50 = (bf16[2,368,128]{2,1,0:T(8,128)(2,1)S(1)}, bf16[2,368,128]{2,1,0:T(8,128)(2,1)S(1)}, u32[]{:S(2)}, u32[]{:S(2)}) collective-permute-start(bf16[2,368,128]{2,1,0:T(8,128)(2,1)S(1)} %get-tuple-element.321), channel_id=1, source_target_pairs={{0,4},{2,6},{4,0},{6,2},{8,12},{10,14},{12,8},{14,10},{16,20},{18,... | collective-permute-start | bytes 565256 | tf_op jit(solution)/shard_map/ppermute | solution.py:673
  261.9 16.3 %collective-permute-start.74 = (bf16[4,704,128]{2,1,0:T(8,128)(2,1)S(1)}, bf16[4,704,128]{2,1,0:T(8,128)(2,1)S(1)}, u32[]{:S(2)}, u32[]{:S(2)}) collective-permute-start(bf16[4,704,128]{2,1,0:T(8,128)(2,1)S(1)} %get-tuple-element.306), channel_id=1, source_target_pairs={{0,4},{2,6},{4,0},{6,2},{8,12},{10,14},{12,8},{14,10},{16,20},{18,... | collective-permute-start | bytes 2162696 | tf_op jit(solution)/shard_map/ppermute | solution.py:673
  262.4 9.4 %collective-permute-start.52 = (bf16[1,352,128]{2,1,0:T(8,128)(2,1)S(1)}, bf16[1,352,128]{2,1,0:T(8,128)(2,1)S(1)}, u32[]{:S(2)}, u32[]{:S(2)}) collective-permute-start(bf16[1,352,128]{2,1,0:T(8,128)(2,1)S(1)} %slice_add_fusion.33), channel_id=1, source_target_pairs={{0,16},{2,18},{4,20},{6,22},{8,24},{10,26},{12,28},{14,30},{16,0},... | collective-permute-start | bytes 270344 | tf_op jit(solution)/shard_map/ppermute | solution.py:673
  262.5 14.8 %collective-permute-start.53 = (bf16[1,368,128]{2,1,0:T(8,128)(2,1)S(1)}, bf16[1,368,128]{2,1,0:T(8,128)(2,1)S(1)}, u32[]{:S(2)}, u32[]{:S(2)}) collective-permute-start(bf16[1,368,128]{2,1,0:T(8,128)(2,1)S(1)} %slice_add_fusion.31), channel_id=1, source_target_pairs={{0,16},{2,18},{4,20},{6,22},{8,24},{10,26},{12,28},{14,30},{16,0},... | collective-permute-start | bytes 282632 | tf_op jit(solution)/shard_map/ppermute | solution.py:673
  280.6 10.9 %collective-permute-start.77 = (bf16[2,704,128]{2,1,0:T(8,128)(2,1)S(1)}, bf16[2,704,128]{2,1,0:T(8,128)(2,1)S(1)}, u32[]{:S(2)}, u32[]{:S(2)}) collective-permute-start(bf16[2,704,128]{2,1,0:T(8,128)(2,1)S(1)} %get-tuple-element.314), channel_id=1, source_target_pairs={{0,8},{2,10},{4,12},{6,14},{8,0},{10,2},{12,4},{14,6},{16,24},{18,... | collective-permute-start | bytes 1081352 | tf_op jit(solution)/shard_map/ppermute | solution.py:673
  281.2 13.6 %collective-permute-start.54 = (bf16[1,352,128]{2,1,0:T(8,128)(2,1)S(1)}, bf16[1,352,128]{2,1,0:T(8,128)(2,1)S(1)}, u32[]{:S(2)}, u32[]{:S(2)}) collective-permute-start(bf16[1,352,128]{2,1,0:T(8,128)(2,1)S(1)} %fusion.5), channel_id=1, source_target_pairs={{0,16},{2,18},{4,20},{6,22},{8,24},{10,26},{12,28},{14,30},{16,0},... | collective-permute-start | bytes 270344 | tf_op jit(solution)/shard_map/ppermute | solution.py:673
  283.2 34.7 %collective-permute-start.56 = (bf16[1,368,128]{2,1,0:T(8,128)(2,1)S(1)}, bf16[1,368,128]{2,1,0:T(8,128)(2,1)S(1)}, u32[]{:S(2)}, u32[]{:S(2)}) collective-permute-start(bf16[1,368,128]{2,1,0:T(8,128)(2,1)S(1)} %fusion.3), channel_id=1, source_target_pairs={{0,16},{2,18},{4,20},{6,22},{8,24},{10,26},{12,28},{14,30},{16,0},... | collective-permute-start | bytes 282632 | tf_op jit(solution)/shard_map/ppermute | solution.py:673
  291.5 26.4 %collective-permute-start.82 = (bf16[1,704,128]{2,1,0:T(8,128)(2,1)S(1)}, bf16[1,704,128]{2,1,0:T(8,128)(2,1)S(1)}, u32[]{:S(2)}, u32[]{:S(2)}) collective-permute-start(bf16[1,704,128]{2,1,0:T(8,128)(2,1)S(1)} %slice_add_fusion.22), channel_id=1, source_target_pairs={{0,16},{2,18},{4,20},{6,22},{8,24},{10,26},{12,28},{14,30},{16,0},... | collective-permute-start | bytes 540680 | tf_op jit(solution)/shard_map/ppermute | solution.py:673
  291.6 26.3 %collective-permute-start.81 = (bf16[1,704,128]{2,1,0:T(8,128)(2,1)S(1)}, bf16[1,704,128]{2,1,0:T(8,128)(2,1)S(1)}, u32[]{:S(2)}, u32[]{:S(2)}) collective-permute-start(bf16[1,704,128]{2,1,0:T(8,128)(2,1)S(1)} %slice_add_fusion.23), channel_id=1, source_target_pairs={{0,16},{2,18},{4,20},{6,22},{8,24},{10,26},{12,28},{14,30},{16,0},... | collective-permute-start | bytes 540680 | tf_op jit(solution)/shard_map/ppermute | solution.py:673
  294.6 23.3 %collective-permute-start.80 = (bf16[1,704,128]{2,1,0:T(8,128)(2,1)S(1)}, bf16[1,704,128]{2,1,0:T(8,128)(2,1)S(1)}, u32[]{:S(2)}, u32[]{:S(2)}) collective-permute-start(bf16[1,704,128]{2,1,0:T(8,128)(2,1)S(1)} %slice_add_fusion.24), channel_id=1, source_target_pairs={{0,16},{2,18},{4,20},{6,22},{8,24},{10,26},{12,28},{14,30},{16,0},... | collective-permute-start | bytes 540680 | tf_op jit(solution)/shard_map/ppermute | solution.py:673
  294.7 23.1 %collective-permute-start.55 = (bf16[1,352,128]{2,1,0:T(8,128)(2,1)S(1)}, bf16[1,352,128]{2,1,0:T(8,128)(2,1)S(1)}, u32[]{:S(2)}, u32[]{:S(2)}) collective-permute-start(bf16[1,352,128]{2,1,0:T(8,128)(2,1)S(1)} %fusion.4), channel_id=1, source_target_pairs={{0,16},{2,18},{4,20},{6,22},{8,24},{10,26},{12,28},{14,30},{16,0},... | collective-permute-start | bytes 270344 | tf_op jit(solution)/shard_map/ppermute | solution.py:673
  318.0 17.2 %collective-permute-start.83 = (bf16[1,704,128]{2,1,0:T(8,128)(2,1)S(1)}, bf16[1,704,128]{2,1,0:T(8,128)(2,1)S(1)}, u32[]{:S(2)}, u32[]{:S(2)}) collective-permute-start(bf16[1,704,128]{2,1,0:T(8,128)(2,1)S(1)} %fusion.2), channel_id=1, source_target_pairs={{0,16},{2,18},{4,20},{6,22},{8,24},{10,26},{12,28},{14,30},{16,0},... | collective-permute-start | bytes 540680 | tf_op jit(solution)/shard_map/ppermute | solution.py:673
  318.1 21.0 %collective-permute-start.84 = (bf16[1,704,128]{2,1,0:T(8,128)(2,1)S(1)}, bf16[1,704,128]{2,1,0:T(8,128)(2,1)S(1)}, u32[]{:S(2)}, u32[]{:S(2)}) collective-permute-start(bf16[1,704,128]{2,1,0:T(8,128)(2,1)S(1)} %fusion.1), channel_id=1, source_target_pairs={{0,16},{2,18},{4,20},{6,22},{8,24},{10,26},{12,28},{14,30},{16,0},... | collective-permute-start | bytes 540680 | tf_op jit(solution)/shard_map/ppermute | solution.py:673
  321.0 21.8 %collective-permute-start.85 = (bf16[1,704,128]{2,1,0:T(8,128)(2,1)S(1)}, bf16[1,704,128]{2,1,0:T(8,128)(2,1)S(1)}, u32[]{:S(2)}, u32[]{:S(2)}) collective-permute-start(bf16[1,704,128]{2,1,0:T(8,128)(2,1)S(1)} %fusion), channel_id=1, source_target_pairs={{0,16},{2,18},{4,20},{6,22},{8,24},{10,26},{12,28},{14,30},{16,0},... | collective-permute-start | bytes 540680 | tf_op jit(solution)/shard_map/ppermute | solution.py:673
  321.1 26.4 %collective-permute-start.58 = (bf16[2,352,128]{2,1,0:T(8,128)(2,1)S(1)}, bf16[2,352,128]{2,1,0:T(8,128)(2,1)S(1)}, u32[]{:S(2)}, u32[]{:S(2)}) collective-permute-start(bf16[2,352,128]{2,1,0:T(8,128)(2,1)S(1)} %pad_maximum_fusion.17), channel_id=1, source_target_pairs={{0,2},{2,0},{4,6},{6,4},{8,10},{10,8},{12,14},{14,12},{16,18},{18,... | collective-permute-start | bytes 540680 | tf_op jit(solution)/shard_map/ppermute | solution.py:673
  321.9 39.2 %collective-permute-start.59 = (bf16[2,368,128]{2,1,0:T(8,128)(2,1)S(1)}, bf16[2,368,128]{2,1,0:T(8,128)(2,1)S(1)}, u32[]{:S(2)}, u32[]{:S(2)}) collective-permute-start(bf16[2,368,128]{2,1,0:T(8,128)(2,1)S(1)} %pad_maximum_fusion.15), channel_id=1, source_target_pairs={{0,4},{2,6},{4,0},{6,2},{8,12},{10,14},{12,8},{14,10},{16,20},{18,... | collective-permute-start | bytes 565256 | tf_op jit(solution)/shard_map/ppermute | solution.py:673
  342.9 18.6 %collective-permute-start.88 = (bf16[2,704,128]{2,1,0:T(8,128)(2,1)S(1)}, bf16[2,704,128]{2,1,0:T(8,128)(2,1)S(1)}, u32[]{:S(2)}, u32[]{:S(2)}) collective-permute-start(bf16[2,704,128]{2,1,0:T(8,128)(2,1)S(1)} %pad_maximum_fusion.14), channel_id=1, source_target_pairs={{0,4},{2,6},{4,0},{6,2},{8,12},{10,14},{12,8},{14,10},{16,20},{18,... | collective-permute-start | bytes 1081352 | tf_op jit(solution)/shard_map/ppermute | solution.py:673
  346.5 14.9 %collective-permute-start.87 = (bf16[2,704,128]{2,1,0:T(8,128)(2,1)S(1)}, bf16[2,704,128]{2,1,0:T(8,128)(2,1)S(1)}, u32[]{:S(2)}, u32[]{:S(2)}) collective-permute-start(bf16[2,704,128]{2,1,0:T(8,128)(2,1)S(1)} %pad_maximum_fusion.13), channel_id=1, source_target_pairs={{0,2},{2,0},{4,6},{6,4},{8,10},{10,8},{12,14},{14,12},{16,18},{18,... | collective-permute-start | bytes 1081352 | tf_op jit(solution)/shard_map/ppermute | solution.py:673
  347.4 14.1 %collective-permute-start.86 = (bf16[2,704,128]{2,1,0:T(8,128)(2,1)S(1)}, bf16[2,704,128]{2,1,0:T(8,128)(2,1)S(1)}, u32[]{:S(2)}, u32[]{:S(2)}) collective-permute-start(bf16[2,704,128]{2,1,0:T(8,128)(2,1)S(1)} %pad_maximum_fusion.12), channel_id=1, source_target_pairs={{0,8},{2,10},{4,12},{6,14},{8,0},{10,2},{12,4},{14,6},{16,24},{18,... | collective-permute-start | bytes 1081352 | tf_op jit(solution)/shard_map/ppermute | solution.py:673
  347.5 13.6 %collective-permute-start.57 = (bf16[2,352,128]{2,1,0:T(8,128)(2,1)S(1)}, bf16[2,352,128]{2,1,0:T(8,128)(2,1)S(1)}, u32[]{:S(2)}, u32[]{:S(2)}) collective-permute-start(bf16[2,352,128]{2,1,0:T(8,128)(2,1)S(1)} %pad_maximum_fusion.16), channel_id=1, source_target_pairs={{0,8},{2,10},{4,12},{6,14},{8,0},{10,2},{12,4},{14,6},{16,24},{18,... | collective-permute-start | bytes 540680 | tf_op jit(solution)/shard_map/ppermute | solution.py:673
  361.1 11.4 %collective-permute-start.61 = (bf16[4,352,128]{2,1,0:T(8,128)(2,1)S(1)}, bf16[4,352,128]{2,1,0:T(8,128)(2,1)S(1)}, u32[]{:S(2)}, u32[]{:S(2)}) collective-permute-start(bf16[4,352,128]{2,1,0:T(8,128)(2,1)S(1)} %pad_maximum_fusion.11), channel_id=1, source_target_pairs={{0,8},{2,10},{4,12},{6,14},{8,0},{10,2},{12,4},{14,6},{16,24},{18,... | collective-permute-start | bytes 1081352 | tf_op jit(solution)/shard_map/ppermute | solution.py:673
  361.6 27.6 %collective-permute-start.91 = (bf16[4,704,128]{2,1,0:T(8,128)(2,1)S(1)}, bf16[4,704,128]{2,1,0:T(8,128)(2,1)S(1)}, u32[]{:S(2)}, u32[]{:S(2)}) collective-permute-start(bf16[4,704,128]{2,1,0:T(8,128)(2,1)S(1)} %pad_maximum_fusion.8), channel_id=1, source_target_pairs={{0,2},{2,0},{4,6},{6,4},{8,10},{10,8},{12,14},{14,12},{16,18},{18,... | collective-permute-start | bytes 2162696 | tf_op jit(solution)/shard_map/ppermute | solution.py:673
  362.9 26.3 %collective-permute-start.90 = (bf16[4,704,128]{2,1,0:T(8,128)(2,1)S(1)}, bf16[4,704,128]{2,1,0:T(8,128)(2,1)S(1)}, u32[]{:S(2)}, u32[]{:S(2)}) collective-permute-start(bf16[4,704,128]{2,1,0:T(8,128)(2,1)S(1)} %pad_maximum_fusion.7), channel_id=1, source_target_pairs={{0,8},{2,10},{4,12},{6,14},{8,0},{10,2},{12,4},{14,6},{16,24},{18,... | collective-permute-start | bytes 2162696 | tf_op jit(solution)/shard_map/ppermute | solution.py:673
  364.8 24.5 %collective-permute-start.89 = (bf16[4,704,128]{2,1,0:T(8,128)(2,1)S(1)}, bf16[4,704,128]{2,1,0:T(8,128)(2,1)S(1)}, u32[]{:S(2)}, u32[]{:S(2)}) collective-permute-start(bf16[4,704,128]{2,1,0:T(8,128)(2,1)S(1)} %pad_maximum_fusion.6), channel_id=1, source_target_pairs={{0,4},{2,6},{4,0},{6,2},{8,12},{10,14},{12,8},{14,10},{16,20},{18,... | collective-permute-start | bytes 2162696 | tf_op jit(solution)/shard_map/ppermute | solution.py:673
  365.2 23.5 %collective-permute-start.62 = (bf16[4,368,128]{2,1,0:T(8,128)(2,1)S(1)}, bf16[4,368,128]{2,1,0:T(8,128)(2,1)S(1)}, u32[]{:S(2)}, u32[]{:S(2)}) collective-permute-start(bf16[4,368,128]{2,1,0:T(8,128)(2,1)S(1)} %pad_maximum_fusion.9), channel_id=1, source_target_pairs={{0,2},{2,0},{4,6},{6,4},{8,10},{10,8},{12,14},{14,12},{16,18},{18,... | collective-permute-start | bytes 1130504 | tf_op jit(solution)/shard_map/ppermute | solution.py:673
  372.5 16.2 %collective-permute-start.60 = (bf16[4,352,128]{2,1,0:T(8,128)(2,1)S(1)}, bf16[4,352,128]{2,1,0:T(8,128)(2,1)S(1)}, u32[]{:S(2)}, u32[]{:S(2)}) collective-permute-start(bf16[4,352,128]{2,1,0:T(8,128)(2,1)S(1)} %pad_maximum_fusion.10), channel_id=1, source_target_pairs={{0,4},{2,6},{4,0},{6,2},{8,12},{10,14},{12,8},{14,10},{16,20},{18,... | collective-permute-start | bytes 1081352 | tf_op jit(solution)/shard_map/ppermute | solution.py:673
  388.8 19.1 %collective-permute-start.64 = (bf16[8,352,128]{2,1,0:T(8,128)(2,1)S(1)}, bf16[8,352,128]{2,1,0:T(8,128)(2,1)S(1)}, u32[]{:S(2)}, u32[]{:S(2)}) collective-permute-start(bf16[8,352,128]{2,1,0:T(8,128)(2,1)S(1)} %pad_maximum_fusion.5.o1), channel_id=1, source_target_pairs={{0,4},{2,6},{4,0},{6,2},{8,12},{10,14},{12,8},{14,10},{16,20},{18,... | collective-permute-start | bytes 2162696 | tf_op jit(solution)/shard_map/ppermute | solution.py:673
  390.8 51.8 %collective-permute-start.94 = (bf16[8,704,128]{2,1,0:T(8,128)(2,1)}, bf16[8,704,128]{2,1,0:T(8,128)(2,1)}, u32[]{:S(2)}, u32[]{:S(2)}) collective-permute-start(bf16[8,704,128]{2,1,0:T(8,128)(2,1)} %pad_maximum_fusion.2.own_ref), channel_id=1, source_target_pairs={{0,8},{2,10},{4,12},{6,14},{8,0},{10,2},{12,4},{14,6},{16,24},{18,... | collective-permute-start | bytes 4325384 | tf_op jit(solution)/shard_map/ppermute | solution.py:673
  391.3 51.3 %collective-permute-start.93 = (bf16[8,704,128]{2,1,0:T(8,128)(2,1)S(1)}, bf16[8,704,128]{2,1,0:T(8,128)(2,1)}, u32[]{:S(2)}, u32[]{:S(2)}) collective-permute-start(bf16[8,704,128]{2,1,0:T(8,128)(2,1)S(1)} %pad_maximum_fusion.1.own_ref), channel_id=1, source_target_pairs={{0,4},{2,6},{4,0},{6,2},{8,12},{10,14},{12,8},{14,10},{16,20},{18,... | collective-permute-start | bytes 4325384 | tf_op jit(solution)/shard_map/ppermute | solution.py:673
  392.7 49.8 %collective-permute-start.92 = (bf16[8,704,128]{2,1,0:T(8,128)(2,1)S(1)}, bf16[8,704,128]{2,1,0:T(8,128)(2,1)}, u32[]{:S(2)}, u32[]{:S(2)}) collective-permute-start(bf16[8,704,128]{2,1,0:T(8,128)(2,1)S(1)} %pad_maximum_fusion.own_ref), channel_id=1, source_target_pairs={{0,2},{2,0},{4,6},{6,4},{8,10},{10,8},{12,14},{14,12},{16,18},{18,... | collective-permute-start | bytes 4325384 | tf_op jit(solution)/shard_map/ppermute | solution.py:673
  393.6 44.2 %collective-permute-start.65 = (bf16[8,368,128]{2,1,0:T(8,128)(2,1)S(1)}, bf16[8,368,128]{2,1,0:T(8,128)(2,1)S(1)}, u32[]{:S(2)}, u32[]{:S(2)}) collective-permute-start(bf16[8,368,128]{2,1,0:T(8,128)(2,1)S(1)} %pad_maximum_fusion.3.o2), channel_id=1, source_target_pairs={{0,8},{2,10},{4,12},{6,14},{8,0},{10,2},{12,4},{14,6},{16,24},{18,... | collective-permute-start | bytes 2261000 | tf_op jit(solution)/shard_map/ppermute | solution.py:673
  407.9 29.9 %collective-permute-start.63 = (bf16[8,352,128]{2,1,0:T(8,128)(2,1)S(1)}, bf16[8,352,128]{2,1,0:T(8,128)(2,1)S(1)}, u32[]{:S(2)}, u32[]{:S(2)}) collective-permute-start(bf16[8,352,128]{2,1,0:T(8,128)(2,1)S(1)} %pad_maximum_fusion.4.o0), channel_id=1, source_target_pairs={{0,2},{2,0},{4,6},{6,4},{8,10},{10,8},{12,14},{14,12},{16,18},{18,... | collective-permute-start | bytes 2162696 | tf_op jit(solution)/shard_map/ppermute | solution.py:673
  (83 other events, 1076.5 us)

commit v2 on v1

--- a/solution.py
+++ b/solution.py
@@ -91,7 +91,7 @@
 VMEM = pl.BlockSpec(memory_space=pltpu.VMEM)
 
 
-def call(name, body, idx, inputs, outs, scratch=(), flops=0, limit=32):
+def call(name, body, idx, inputs, outs, scratch=(), flops=0, limit=32, far=0):
     shapes = [jax.ShapeDtypeStruct(s, d) for s, d in outs]
     moved = sum(a.size * a.dtype.itemsize for a in inputs) + sum(
         s.size * s.dtype.itemsize for s in shapes
@@ -100,9 +100,9 @@
         body,
         name=name,
         out_shape=shapes,
-        in_specs=[SMEM] + [VMEM] * len(inputs),
+        in_specs=[SMEM] + [VMEM] * (len(inputs) - far) + [pl.BlockSpec(memory_space=pl.ANY)] * far,
         out_specs=[VMEM] * len(shapes),
-        scratch_shapes=[pltpu.VMEM(s, d) for s, d in scratch],
+        scratch_shapes=[pltpu.VMEM(*s) if isinstance(s, tuple) else s for s in scratch],
         compiler_params=pltpu.CompilerParams(vmem_limit_bytes=limit * MIB),
         cost_estimate=pl.CostEstimate(
             flops=int(flops), bytes_accessed=int(moved), transcendentals=0
@@ -181,24 +181,67 @@
         state[low ^ other] = pieces[other][...]
 
 
-def keys_kernel(dims, idx_ref, x_ref, g1_own, g1_oth, wk_own, wk_oth, wv_own, wv_oth, li_own, li_oth,
-                lo_own, lo_oth, b_own, b_oth, nm_ref, no_ref, k_ref, v_ref, lr_ref, lg_ref, kd_ref, tot_ref,
+def pack_kernel(idx_ref, li_ref, lo_ref, g1_ref, g2_ref, b_ref, hg_ref, out_ref):
+    rank = li_ref.shape[1]
+    high = li_ref.shape[0]
+    out_ref[0:high, :] = jnp.concatenate(
+        [li_ref[...], jnp.zeros((high, 128 - rank), BF16)], axis=1
+    )
+    at = high
+    for tile in range(lo_ref.shape[1] // 128):
+        out_ref[at : at + rank, :] = lo_ref[:, tile * 128 : (tile + 1) * 128]
+        at += rank
+    lines = []
+    for ref in (g1_ref, g2_ref, b_ref, hg_ref):
+        row = ref[...].astype(F32)
+        lines += [row[:, tile * 128 : (tile + 1) * 128] for tile in range(row.shape[1] // 128)]
+    lines.append(jnp.zeros((out_ref.shape[0] - at - len(lines), 128), F32))
+    out_ref[at:, :] = jnp.concatenate(lines, axis=0).astype(BF16)
+
+
+def packed_factors(pack_ref, rank, part):
+    high = pack_ref.shape[0] - 16 - rank * part // 128
+    first = pack_ref[0:high, :][:, 0:rank]
+    second = [pack_ref[high + t * rank : high + (t + 1) * rank, :] for t in range(part // 128)]
+    return first, jnp.concatenate(second, axis=1)
+
+
+def packed_row(pack_ref, first, count):
+    lines = pack_ref[pack_ref.shape[0] - 16 :, :].astype(F32)
+    return jnp.concatenate([lines[t : t + 1, :] for t in range(first, first + count)], axis=1)
+
+
+def packed_places(half, part, gain):
+    g1, b, hg = half // 128, part // 128, gain // 128
+    return (0, g1), (g1, g1), (2 * g1, b), (2 * g1 + b, hg)
+
+
+def keys_kernel(dims, idx_ref, x_ref, cot_ref, g1_own, wk_own, wk_oth, wv_own, wv_oth, li_own, lo_own, b_own, pack_ref,
+                nm_ref, no_ref, k_ref, v_ref, lr_ref, lg_ref, kd_ref, tot_ref, e_ref,
                 m0, m1, m2, m3, state):
     seqs, span = dims
     half = g1_own.shape[1]
+    rank, part = lo_own.shape
+    place_g1, _, place_b, _ = packed_places(half, part, 0)
+    li_oth, lo_oth = packed_factors(pack_ref, rank, part)
+    g1_oth = packed_row(pack_ref, *place_g1)
+    b_oth = packed_row(pack_ref, *place_b)
+    for s in range(seqs):
+        at = slice(s * span, (s + 1) * span)
+        places = lax.broadcasted_iota(jnp.int32, (span, cot_ref.shape[1]), 0) + idx_ref[1] * span
+        e_ref[at, :] = jnp.where(places < idx_ref[2 + s], cot_ref[at, :].astype(F32), 0.0).astype(BF16)
     xm = x_ref[:, mine_at(idx_ref, half)].astype(F32)
     xo = x_ref[:, theirs_at(idx_ref, half)].astype(F32)
     square = jnp.sum(xm * xm, axis=1, keepdims=True) + jnp.sum(xo * xo, axis=1, keepdims=True)
     root = lax.rsqrt(square / (2 * half) + 1e-6)
     nm = (xm * root * g1_own[...].astype(F32)).astype(BF16)
-    no = (xo * root * g1_oth[...].astype(F32)).astype(BF16)
+    no = (xo * root * g1_oth).astype(BF16)
     nm_ref[...] = nm
     no_ref[...] = no
-    lr = (dot(nm, li_own[...]) + dot(no, li_oth[...])).astype(BF16)
+    lr = (dot(nm, li_own[...]) + dot(no, li_oth)).astype(BF16)
     lr_ref[...] = lr
-    part = lo_own.shape[1]
     lg_ref[:, mine_at(idx_ref, part)] = dot(lr, lo_own[...]) + b_own[...].astype(F32)
-    lg_ref[:, theirs_at(idx_ref, part)] = dot(lr, lo_oth[...]) + b_oth[...].astype(F32)
+    lg_ref[:, theirs_at(idx_ref, part)] = dot(lr, lo_oth) + b_oth
     keys = (dot(nm, wk_own[...]) + dot(no, wk_oth[...])).astype(BF16)
     k_ref[...] = keys
     values = (dot(nm, wv_own[...]) + dot(no, wv_oth[...])).astype(BF16)
@@ -264,13 +307,14 @@
             mix_ref[at, vs] = dot(low, v_ref[at, vs])
 
 
-def hidden_kernel(dims, idx_ref, mix_ref, qb_ref, e0, e1, e2, e3, og_ref, hg_own, hg_oth, x_ref, wo_own, wo_oth,
-                  g2_own, g2_oth, mixture_ref, gm_ref, go_ref, hid_ref, sm_ref, so_ref, st_ref,
+def hidden_kernel(dims, idx_ref, mix_ref, qb_ref, e0, e1, e2, e3, og_ref, hg_own, x_ref, wo_own, wo_oth,
+                  g2_own, pack_ref, mixture_ref, gm_ref, go_ref, hid_ref, sm_ref, so_ref, st_ref,
                   gain, gated):
     seqs, span = dims
     load_state(idx_ref, (e0, e1, e2, e3), st_ref)
+    _, place_g2, _, place_hg = packed_places(g2_own.shape[1], qb_ref.shape[1] // 2, hg_own.shape[1])
     gain[:, mine_at(idx_ref, hg_own.shape[1])] = hg_own[...].astype(F32)
-    gain[:, theirs_at(idx_ref, hg_own.shape[1])] = hg_oth[...].astype(F32)
+    gain[:, theirs_at(idx_ref, hg_own.shape[1])] = packed_row(pack_ref, *place_hg)
     wide = qb_ref.shape[1] // HEADS
     tall = mix_ref.shape[1] // HEADS
     factor = wide ** (-0.5)
@@ -302,43 +346,54 @@
     square = jnp.sum(hm * hm, axis=1, keepdims=True) + jnp.sum(ho * ho, axis=1, keepdims=True)
     root = lax.rsqrt(square / (2 * half) + 1e-6)
     sm_ref[...] = (hm * root * g2_own[...].astype(F32)).astype(BF16)
-    so_ref[...] = (ho * root * g2_oth[...].astype(F32)).astype(BF16)
-
-
-def ffn_kernel(dims, idx_ref, sm_ref, so_ref, hid_ref, cot_ref, wg_own, wg_oth, wu_own, wu_oth, wd_own, wd_oth,
-               out_ref, e_ref, am_ref, ao_ref, gg_ref, ug_ref, dm_ref, do_ref):
+    so_ref[...] = (ho * root * packed_row(pack_ref, *place_g2)).astype(BF16)
+
+
+def ffn_kernel(dims, idx_ref, sm_ref, so_ref, hid_ref, e_ref, wg_own, wg_oth, wu_own, wu_oth, wd_own, wd_oth,
+               out_ref, am_ref, ao_ref, g_ref, dm_ref, do_ref, gates_in, ups_in, downs_in, sems):
     seqs, span = dims
     rows, width = hid_ref.shape
-    for s in range(seqs):
-        at = slice(s * span, (s + 1) * span)
-        places = lax.broadcasted_iota(jnp.int32, (span, width), 0) + idx_ref[1] * span
-        valid = places < idx_ref[2 + s]
-        e_ref[at, :] = jnp.where(valid, cot_ref[at, :].astype(F32), 0.0).astype(BF16)
+    half = wd_own.shape[0]
+    spots = (mine_at(idx_ref, half), theirs_at(idx_ref, half))
+    copies = []
+    for step in range(2):
+        now = []
+        for to, sources in ((gates_in, (wg_own, wg_oth)), (ups_in, (wu_own, wu_oth))):
+            for which in range(2):
+                now.append((sources[which].at[:, spots[step]], to.at[step, which]))
+        now.append(((wd_own, wd_oth)[step], downs_in.at[step]))
+        copies.append(
+            [pltpu.make_async_copy(src, dst, sems.at[step, i]) for i, (src, dst) in enumerate(now)]
+        )
+    for step in copies:
+        for one in step:
+            one.start()
     sm, so, cots = sm_ref[...], so_ref[...], e_ref[...]
-    half = wd_own.shape[0]
-    out_ref[...] = hid_ref[...]
     for step in range(2):
-        at = (mine_at, theirs_at)[step](idx_ref, half)
-        down = (wd_own, wd_oth)[step]
+        at = spots[step]
         act_ref = (am_ref, ao_ref)[step]
-        gates = dot(sm, wg_own[:, at]) + dot(so, wg_oth[:, at])
-        ups = dot(sm, wu_own[:, at]) + dot(so, wu_oth[:, at])
+        for one in copies[step]:
+            one.wait()
+        gates = dot(sm, gates_in[step, 0]) + dot(so, gates_in[step, 1])
+        ups = dot(sm, ups_in[step, 0]) + dot(so, ups_in[step, 1])
         sig = sigmoid(gates)
         opened = gates * sig
         act = (opened * ups).astype(BF16)
         act_ref[...] = act
-        grads = dot_t(cots, down[...])
+        grads = dot_t(cots, downs_in[step])
         gate_grad = (grads * ups * sig * (1.0 + gates * (1.0 - sig))).astype(BF16)
         up_grad = (grads * opened).astype(BF16)
-        gg_ref[:, at] = gate_grad
-        ug_ref[:, at] = up_grad
-        out_ref[...] += dot(act, down[...])
-        dm = dot_t(gate_grad, wg_own[:, at]) + dot_t(up_grad, wu_own[:, at])
-        do = dot_t(gate_grad, wg_oth[:, at]) + dot_t(up_grad, wu_oth[:, at])
+        g_ref[:, at] = gate_grad
+        g_ref[:, pl.ds(pl.multiple_of(at.start + 2 * half, 128), half)] = up_grad
+        more = dot(act, downs_in[step])
+        dm = dot_t(gate_grad, gates_in[step, 0]) + dot_t(up_grad, ups_in[step, 0])
+        do = dot_t(gate_grad, gates_in[step, 1]) + dot_t(up_grad, ups_in[step, 1])
         if step == 0:
+            out_ref[...] = hid_ref[...] + more
             dm_ref[...] = dm
             do_ref[...] = do
         else:
+            out_ref[...] += more
             dm_ref[...] += dm
             do_ref[...] += do
     for s in range(seqs):
@@ -347,12 +402,13 @@
         out_ref[at, :] = jnp.where(places < idx_ref[2 + s], out_ref[at, :], 0.0)
 
 
-def gate_back_kernel(dims, idx_ref, hid_ref, dm_ref, do_ref, g2_own, g2_oth, e_ref, wo_own, wo_oth, mixture_ref,
-                     og_ref, hg_own, hg_oth, qb_ref, tot_ref,
+def gate_back_kernel(dims, idx_ref, hid_ref, dm_ref, do_ref, g2_own, e_ref, wo_own, wo_oth, mixture_ref,
+                     og_ref, hg_own, qb_ref, tot_ref, pack_ref,
                      hg_ref, hl_ref, mg_ref, ol_ref, g2m_ref, g2o_ref, hgm_ref, hgo_ref, m0, m1, m2, m3,
                      gain, gated, gain_sum, state):
     seqs, span = dims
     half = g2_own.shape[1]
+    _, place_g2, _, place_hg = packed_places(half, qb_ref.shape[1] // 2, hg_own.shape[1])
     mine, theirs = mine_at(idx_ref, half), theirs_at(idx_ref, half)
     hm, ho = hid_ref[:, mine], hid_ref[:, theirs]
     square = jnp.sum(hm * hm, axis=1, keepdims=True) + jnp.sum(ho * ho, axis=1, keepdims=True)
@@ -361,7 +417,7 @@
     g2m_ref[...] = jnp.sum(dm * hm * root, axis=0, keepdims=True)
     g2o_ref[...] = jnp.sum(do * ho * root, axis=0, keepdims=True)
     dm = dm * g2_own[...].astype(F32)
-    do = do * g2_oth[...].astype(F32)
+    do = do * packed_row(pack_ref, *place_g2)
     along = jnp.sum(dm * hm, axis=1, keepdims=True) + jnp.sum(do * ho, axis=1, keepdims=True)
     along = along * (root * root * root) / (2 * half)
     hg_ref[:, mine] = e_ref[:, mine].astype(F32) + dm * root - hm * along
@@ -372,7 +428,7 @@
     gated[:, mine_at(idx_ref, half)] = dot_t(low, wo_own[...])
     gated[:, theirs_at(idx_ref, half)] = dot_t(low, wo_oth[...])
     gain[:, mine_at(idx_ref, hg_own.shape[1])] = hg_own[...].astype(F32)
-    gain[:, theirs_at(idx_ref, hg_own.shape[1])] = hg_oth[...].astype(F32)
+    gain[:, theirs_at(idx_ref, hg_own.shape[1])] = packed_row(pack_ref, *place_hg)
     head_gain = gain[...]
     wide = qb_ref.shape[1] // HEADS
     tall = mixture_ref.shape[1] // HEADS
@@ -458,11 +514,15 @@
 
 
 def inputs_back_kernel(dims, idx_ref, dq_ref, dk_ref, dv_ref, dc_ref, ol_ref, kd_ref, v_ref, lg_ref, tot_ref, st_ref,
-                       l0, l1, l2, l3, x_ref, hg_ref, g1_own, g1_oth, wq_own, wq_oth, wk_own, wk_oth, wv_own, wv_oth,
-                       wg_own, wg_oth, li_own, li_oth, lo_own, lo_oth,
-                       tg_ref, ga_ref, llm_ref, llo_ref, g1m_ref, g1o_ref, bm_ref, bo_ref,
+                       l0, l1, l2, l3, x_ref, hg_ref, g1_own, wq_own, wq_oth, wk_own, wk_oth, wv_own, wv_oth,
+                       wg_own, wg_oth, li_own, lo_own, pack_ref, g2o_ref, hgo_ref,
+                       tg_ref, ga_ref, llm_ref, g1m_ref, bm_ref, small_ref,
                        leaving, logit, bias):
     seqs, span = dims
+    half = g1_own.shape[1]
+    rank, part = lo_own.shape
+    place_g1, _, _, _ = packed_places(half, part, 0)
+    li_oth, lo_oth = packed_factors(pack_ref, rank, part)
     load_state(idx_ref, (l0, l1, l2, l3), leaving)
     row, col = pair_iota(span)
     later = (col > row).astype(F32).astype(BF16)
@@ -509,32 +569,33 @@
     bias[...] = bias_sum
     part = lo_own.shape[1]
     bm_ref[...] = bias[:, mine_at(idx_ref, part)]
-    bo_ref[...] = bias[:, theirs_at(idx_ref, part)]
+    small_ref[:, 2 * half : 2 * half + part] = bias[:, theirs_at(idx_ref, part)]
+    small_ref[:, half : 2 * half] = g2o_ref[...]
+    small_ref[:, 2 * half + part :] = hgo_ref[...]
     ga_ref[:, 0:keys] = dq_ref[...].astype(BF16)
     ga_ref[:, 2 * keys + vals : 2 * keys + 2 * vals] = ol_ref[...]
     llm, llo = logit[:, mine_at(idx_ref, part)], logit[:, theirs_at(idx_ref, part)]
     llm_ref[...] = llm
-    llo_ref[...] = llo
-    lrg = (dot_t(llm, lo_own[...]) + dot_t(llo, lo_oth[...])).astype(BF16)
-    rank = lrg.shape[1]
+    lrg = (dot_t(llm, lo_own[...]) + dot_t(llo, lo_oth)).astype(BF16)
     rest = jnp.zeros((lrg.shape[0], 128 - rank), BF16)
-    ga_ref[:, 2 * keys + 2 * vals :] = jnp.concatenate([lrg, rest], axis=1)
+    lanes = 2 * keys + 2 * vals + 128
+    ga_ref[:, lanes - 128 : lanes] = jnp.concatenate([lrg, rest], axis=1)
+    ga_ref[:, lanes:] = llo
     qg, kg = ga_ref[:, 0:keys], ga_ref[:, keys : 2 * keys]
     vg = ga_ref[:, 2 * keys : 2 * keys + vals]
     og = ga_ref[:, 2 * keys + vals : 2 * keys + 2 * vals]
     dm = dot_t(qg, wq_own[...]) + dot_t(kg, wk_own[...]) + dot_t(vg, wv_own[...])
     dm = dm + dot_t(og, wg_own[...]) + dot_t(lrg, li_own[...])
     do = dot_t(qg, wq_oth[...]) + dot_t(kg, wk_oth[...]) + dot_t(vg, wv_oth[...])
-    do = do + dot_t(og, wg_oth[...]) + dot_t(lrg, li_oth[...])
-    half = g1_own.shape[1]
+    do = do + dot_t(og, wg_oth[...]) + dot_t(lrg, li_oth)
     mine, theirs = mine_at(idx_ref, half), theirs_at(idx_ref, half)
     xm, xo = x_ref[:, mine].astype(F32), x_ref[:, theirs].astype(F32)
     square = jnp.sum(xm * xm, axis=1, keepdims=True) + jnp.sum(xo * xo, axis=1, keepdims=True)
     root = lax.rsqrt(square / (2 * half) + 1e-6)
     g1m_ref[...] = jnp.sum(dm * xm * root, axis=0, keepdims=True)
-    g1o_ref[...] = jnp.sum(do * xo * root, axis=0, keepdims=True)
+    small_ref[:, 0:half] = jnp.sum(do * xo * root, axis=0, keepdims=True)
     dm = dm * g1_own[...].astype(F32)
-    do = do * g1_oth[...].astype(F32)
+    do = do * packed_row(pack_ref, *place_g1)
     along = jnp.sum(dm * xm, axis=1, keepdims=True) + jnp.sum(do * xo, axis=1, keepdims=True)
     along = along * (root * root * root) / (2 * half)
     tg_ref[:, mine] = hg_ref[:, mine] + dm * root - xm * along
@@ -553,16 +614,19 @@
     return keep_ref.at[position] if position < 8 else send_ref.at[position - 8]
 
 
-def wide_grad_kernel(order, idx_ref, lm_ref, lo_ref, gm_ref, go_ref, keep_ref, send_ref, full):
+def wide_grad_kernel(orders, idx_ref, lm_ref, lo_ref, gm_ref, go_ref, k0, s0, k1, s1, full):
     place = lax.rem(idx_ref[1], 16)
-    full[...] = t_dot(lm_ref[...], gm_ref[...]) + t_dot(lo_ref[...], go_ref[...])
+    width = full.shape[1]
     high = full.shape[0] // 16
-    for position in range(16):
-        block = block_of(position, order) ^ place
-        rows = full[pl.ds(pl.multiple_of(block * high, high), high), :].astype(BF16)
-        to = deal(position, keep_ref, send_ref)
-        for tile in range(full.shape[1] // 128):
-            to[tile * high : (tile + 1) * high, :] = rows[:, tile * 128 : (tile + 1) * 128]
+    for which, refs in enumerate(((k0, s0), (k1, s1))):
+        cols = slice(which * width, (which + 1) * width)
+        full[...] = t_dot(lm_ref[...], gm_ref[:, cols]) + t_dot(lo_ref[...], go_ref[:, cols])
+        for position in range(16):
+            block = block_of(position, orders[which]) ^ place
+            rows = full[pl.ds(pl.multiple_of(block * high, high), high), :].astype(BF16)
+            to = deal(position, *refs)
+            for tile in range(width // 128):
+                to[tile * high : (tile + 1) * high, :] = rows[:, tile * 128 : (tile + 1) * 128]
 
 
 def down_grad_kernel(order, idx_ref, lm_ref, lo_ref, gm_ref, go_ref, keep_ref, send_ref, full):
@@ -577,18 +641,18 @@
 
 
 def attention_grad_kernel(orders, cuts, idx_ref, nm_ref, no_ref, gm_ref, go_ref, am_ref, ao_ref, hm_ref, ho_ref,
-                          lrm_ref, lro_ref, llm_ref, llo_ref, g1_ref, g1o_ref, g2_ref, g2o_ref, b_ref, bo_ref,
-                          hg_ref, hgo_ref, k0, s0, k1, s1, k2, s2, full, outer, small):
+                          lrm_ref, lro_ref, llm_ref, g1_ref, g2_ref, b_ref, hg_ref, small_ref, k0, s0, k1, s1, k2, s2, full, outer, small):
     place = lax.rem(idx_ref[1], 16)
-    full[...] = t_dot(nm_ref[...], gm_ref[...]) + t_dot(no_ref[...], go_ref[...])
+    lanes = full.shape[1]
+    full[...] = t_dot(nm_ref[...], gm_ref[:, 0:lanes]) + t_dot(no_ref[...], go_ref[:, 0:lanes])
     outer[...] = t_dot(am_ref[...], hm_ref[...]) + t_dot(ao_ref[...], ho_ref[...])
-    low_out = t_dot(lrm_ref[...], llm_ref[...]) + t_dot(lro_ref[...], llo_ref[...])
+    low_out = t_dot(lrm_ref[...], llm_ref[...]) + t_dot(lro_ref[...], go_ref[:, lanes:])
     small[...] = jnp.zeros_like(small)
     small[0] = low_out[:, 0:128]
     small[1] = low_out[:, 128:256]
     line = 0
-    for first, second in ((g1_ref, g1o_ref), (g2_ref, g2o_ref), (b_ref, bo_ref), (hg_ref, hgo_ref)):
-        row = first[...] + second[...]
+    for ref in (g1_ref, g2_ref, b_ref, hg_ref):
+        row = ref[...] + small_ref[:, line * 128 : line * 128 + ref.shape[1]]
         for tile in range(row.shape[1] // 128):
             small[2, line : line + 1, :] = row[:, tile * 128 : (tile + 1) * 128]
             line += 1
@@ -682,50 +746,79 @@
     )
 
 
-def together(arrays):
-    return list(lax.optimization_barrier(tuple(arrays)))
-
-
-def reduce_all(parts, orders):
-    count = lax.axis_size("seq")
-    kept = [keep for keep, _ in parts]
-    sent = [send for _, send in parts]
-    for step in range(4):
-        got = together([swap(s, order[step]) for s, order in zip(sent, orders)])
+def fence(*groups):
+    return lax.optimization_barrier(groups)
+
+
+class Portions:
+    def __init__(self, parts, orders):
+        self.kept = [keep for keep, _ in parts]
+        self.sent = [send for _, send in parts]
+        self.orders = orders
+
+    def move(self, arrays, step):
+        if step < 3:
+            return [swap(a, order[step]) for a, order in zip(arrays, self.orders)]
+        return self.move_all(arrays, self.orders[0][3])
+
+    def move_all(self, arrays, bit):
+        got = swap(jnp.concatenate(arrays, axis=1), bit)
+        ends = [0]
+        for a in arrays:
+            ends.append(ends[-1] + a.shape[1])
+        return [got[:, first:last] for first, last in zip(ends[:-1], ends[1:])]
+
+    def reduce_start(self, step):
+        return self.move(self.sent, step)
+
+    def reduce_end(self, step, got):
         for one, more in enumerate(got):
             if step < 3:
                 half = more.shape[0] // 2
-                sent[one] = kept[one][half:] + more[half:]
-                kept[one] = kept[one][:half] + more[:half]
+                self.sent[one] = self.kept[one][half:] + more[half:]
+                self.kept[one] = self.kept[one][:half] + more[:half]
             else:
-                kept[one] = kept[one] + more
-    bit = 16
-    while bit < count:
-        got = together([swap(k, bit) for k in kept])
-        kept = [k + more for k, more in zip(kept, got)]
-        bit *= 2
-    for step in (3, 2, 1, 0):
-        got = together([swap(k, order[step]) for k, order in zip(kept, orders)])
+                self.kept[one] = self.kept[one] + more
+        bit = 16
+        while step == 3 and bit < lax.axis_size("seq"):
+            more = self.move_all(self.kept, bit)
+            self.kept = [k + m for k, m in zip(self.kept, more)]
+            bit *= 2
+
+    def gather_start(self, step):
+        return self.move(self.kept, step)
+
+    def gather_end(self, step, got):
         if step:
-            kept = [jnp.concatenate([k, more], axis=0) for k, more in zip(kept, got)]
-    return list(zip(kept, got))
-
-
-def scan_states(messages, idx, reverse, mid=None):
-    count = lax.axis_size("seq")
+            self.kept = [jnp.concatenate([k, more], axis=0) for k, more in zip(self.kept, got)]
+        else:
+            self.halves = list(zip(self.kept, got))
+
+
+def scan_near(messages):
+    return [messages[0]] + [swap(messages[o], o) for o in (1, 2, 3)]
+
+
+def scan_scratch(messages):
     rows, lanes = messages[0].shape
-    quarter = rows - 16
-    near = [messages[0]] + [swap(messages[o], o) for o in (1, 2, 3)]
-    kept = [((4, quarter, lanes), F32), ((4, 1, lanes), F32)]
-    total = call("group_total", partial(group_total, reverse), idx, near, [((rows, lanes), BF16)], kept)[0]
-    groups = count // 4
+    return [((4, rows - 16, lanes), F32), ((4, 1, lanes), F32)]
+
+
+def scan_total(near, idx, reverse):
+    return call("group_total", partial(group_total, reverse), idx, near, [(near[0].shape, BF16)], scan_scratch(near))[0]
+
+
+def scan_far(total, reverse):
     sign = -4 if reverse else 4
-    far = [ahead(total, sign * step) for step in range(1, groups)]
-    outs = call(
-        "group_entering", partial(group_entering, reverse, len(far)), idx, far + near,
-        [((quarter, lanes), BF16)] * 4, kept + [((4, quarter, lanes), F32)],
-    )
-    return [outs[0]] + [swap(outs[o], o) for o in (1, 2, 3)]
+    return [ahead(total, sign * step) for step in range(1, lax.axis_size("seq") // 4)]
+
+
+def scan_entering(far, near, idx, reverse):
+    rows, lanes = near[0].shape
+    return call(
+        "group_entering", partial(group_entering, reverse, len(far)), idx, list(far) + list(near),
+        [((rows - 16, lanes), BF16)] * 4, scan_scratch(near) + [((4, rows - 16, lanes), F32)],
+    )
 
 
 def shards(
@@ -765,22 +858,31 @@
     first_gain, decay_bias, head_gain, second_gain = (
         a.reshape(1, -1) for a in (first_gain, decay_bias, head_gain, second_gain)
     )
-    wk2, g12, li2, lo2, b2 = (across(a) for a in (key_weight, first_gain, lowrank_in, lowrank_out, decay_bias))
-    wv2, wq2, wg2 = (across(a) for a in (value_weight, query_weight, outgate_weight))
-    hg2, g22, wo2 = (across(a) for a in (head_gain, second_gain, output_weight))
-    wgate2, wup2, wdown2 = (across(a) for a in (gate_weight, up_weight, down_weight))
+    lrank = lowrank_in.shape[1]
+    pack = call(
+        "pack", pack_kernel, idx, [lowrank_in, lowrank_out, first_gain, second_gain, decay_bias, head_gain],
+        [((half + lrank * lowrank_out.shape[1] // 128 + 16, 128), BF16)],
+    )[0]
+    pack2, wk2, wv2, wq2 = (across(a) for a in (pack, key_weight, value_weight, query_weight))
 
     message = ((quarter + 16, keys), BF16)
     state = ((4, quarter, keys), F32)
-    nm, no, k, v, lr, lg, kd, tot, *messages = call(
+    nm, no, k, v, lr, lg, kd, tot, cots, *messages = call(
         "keys", partial(keys_kernel, dims), idx,
-        [x, first_gain, g12, key_weight, wk2, value_weight, wv2, lowrank_in, li2, lowrank_out, lo2, decay_bias, b2],
+        [x, cot, first_gain, key_weight, wk2, value_weight, wv2, lowrank_in, lowrank_out, decay_bias, pack2],
         [((rows, half), BF16), ((rows, half), BF16), ((rows, keys), BF16), ((rows, vals), BF16),
-         ((rows, lowrank_in.shape[1]), BF16), ((rows, keys), F32), ((rows, keys), BF16), ((seqs, keys), F32)]
+         ((rows, lrank), BF16), ((rows, keys), F32), ((rows, keys), BF16), ((seqs, keys), F32), ((rows, width), BF16)]
         + [message] * 4,
         [state], flops=2 * rows * width * (keys + vals) + 4 * rows * span * keys,
     )
-    pieces = scan_states(messages, idx, False)
+    messages, outgate_send = fence(messages, outgate_weight)
+    near = scan_near(messages)
+    wg2, cots2 = across(outgate_send), across(cots)
+    near, gate_send, up_send = fence(near, gate_weight, up_weight)
+    total = scan_total(near, idx, False)
+    total, gate_send, up_send = fence(total, gate_send, up_send)
+    far = scan_far(total, False)
+    wgate2, wup2 = across(gate_send), across(up_send)
     q, og, mix, scores, qb = call(
         "inner", partial(inner_kernel, dims), idx,
         [nm, no, query_weight, wq2, outgate_weight, wg2, k, v, lg],
@@ -788,63 +890,82 @@
          ((rows, keys), BF16)],
         flops=2 * rows * width * (keys + vals) + 60 * rows * span * keys,
     )
+    far, mix = fence(far, mix)
+    pieces = scan_entering(far, near, idx, False)
+    pieces, output_send, down_send = fence(pieces, output_weight, down_weight)
+    pieces = [pieces[0]] + [swap(pieces[o], o) for o in (1, 2, 3)]
+    wo2, wdown2 = across(output_send), across(down_send)
     mixture, gm, go, hid, sm, so, st = call(
         "hidden", partial(hidden_kernel, dims), idx,
-        [mix, qb, *pieces, og, head_gain, hg2, x, output_weight, wo2, second_gain, g22],
+        [mix, qb, *pieces, og, head_gain, x, output_weight, wo2, second_gain, pack2],
         [((rows, vals), F32), ((rows, vals // 2), BF16), ((rows, vals // 2), BF16), ((rows, width), F32),
          ((rows, half), BF16), ((rows, half), BF16), ((4, quarter, keys), BF16)],
         [((1, tall), F32), ((rows, vals), BF16)], flops=2 * rows * vals * width,
     )
-    out, cots, am, ao, gate_grad, up_grad, dm, do = call(
+    so, no_send, lr_send = fence(so, no, lr)
+    so2, no2, go2, lr2 = across(so), across(no_send), across(go), across(lr_send)
+    out, am, ao, gu, dm, do = call(
         "ffn", partial(ffn_kernel, dims), idx,
-        [sm, so, hid, cot, gate_weight, wgate2, up_weight, wup2, down_weight, wdown2],
-        [((rows, width), F32), ((rows, width), BF16), ((rows, ff // 2), BF16), ((rows, ff // 2), BF16),
-         ((rows, ff), BF16), ((rows, ff), BF16), ((rows, half), F32), ((rows, half), F32)],
-        flops=12 * rows * width * ff, limit=52,
-    )
-
-    bits = (1, 2, 4, 8)
-    orders = ((bits[0], bits[1], bits[2], bits[3]), (bits[1], bits[2], bits[0], bits[3]), (bits[2], bits[0], bits[1], bits[3]))
-    cots2, ao2, so2, gate_grad2, up_grad2 = (across(a) for a in (cots, ao, so, gate_grad, up_grad))
+        [sm, so, hid, cots, gate_weight, wgate2, up_weight, wup2, down_weight, wdown2],
+        [((rows, width), F32), ((rows, ff // 2), BF16), ((rows, ff // 2), BF16),
+         ((rows, 2 * ff), BF16), ((rows, half), F32), ((rows, half), F32)],
+        [((2, 2, half, ff // 2), BF16), ((2, 2, half, ff // 2), BF16), ((2, ff // 2, width), BF16),
+         pltpu.SemaphoreType.DMA((2, 5))],
+        flops=12 * rows * width * ff, limit=52, far=6,
+    )
+    so2, no2, go2, lr2, gu, dm, ao = fence(so2, no2, go2, lr2, gu, dm, ao)
+
+    orders = ((1, 2, 4, 8), (2, 4, 1, 8), (4, 1, 2, 8))
+    ao2, gu2 = across(ao), across(gu)
+    hg, hl, mg, ol, g2m, g2o, hgm, hgo, *messages = call(
+        "gate_back", partial(gate_back_kernel, dims), idx,
+        [hid, dm, do, second_gain, cots, output_weight, wo2, mixture, og, head_gain, qb, tot, pack2],
+        [((rows, width), F32), ((rows, width), BF16), ((rows, vals), F32), ((rows, vals), BF16),
+         ((1, half), F32), ((1, half), F32), ((1, tall // 2), F32), ((1, tall // 2), F32)] + [message] * 4,
+        [((1, tall), F32), ((rows, vals), F32), ((1, tall), F32), state],
+        flops=2 * rows * width * vals + 4 * rows * span * keys,
+    )
+    messages, ao2, gu2 = fence(messages, ao2, gu2)
+    near = scan_near(messages)
     portion = ff // 128 * (half // 16)
     flat = [((8, portion, 128), BF16)] * 2
     down_parts = call("down_grad", partial(down_grad_kernel, orders[2]), idx, [am, ao2, cots, cots2], flat,
                       [((ff // 2, width), F32)], flops=2 * rows * ff * width)
-    gate_parts = call("gate_grad", partial(wide_grad_kernel, orders[0]), idx, [sm, so2, gate_grad, gate_grad2], flat,
-                      [((half, ff), F32)], flops=2 * rows * ff * width)
-    up_parts = call("up_grad", partial(wide_grad_kernel, orders[1]), idx, [sm, so2, up_grad, up_grad2], flat,
-                    [((half, ff), F32)], flops=2 * rows * ff * width)
-    gate_halves, up_halves, down_halves = reduce_all([gate_parts, up_parts, down_parts], orders)
-    gate_out = call("gate_open", partial(wide_open_kernel, orders[0]), idx, gate_halves, [((half, ff), F32)])[0]
-    up_out = call("up_open", partial(wide_open_kernel, orders[1]), idx, up_halves, [((half, ff), F32)])[0]
-    down_out = call("down_open", partial(down_open_kernel, orders[2]), idx, down_halves, [((ff // 2, width), F32)])[0]
-
-    hg, hl, mg, ol, g2m, g2o, hgm, hgo, *messages = call(
-        "gate_back", partial(gate_back_kernel, dims), idx,
-        [hid, dm, do, second_gain, g22, cots, output_weight, wo2, mixture, og, head_gain, hg2, qb, tot],
-        [((rows, width), F32), ((rows, width), BF16), ((rows, vals), F32), ((rows, vals), BF16),
-         ((1, half), F32), ((1, half), F32), ((1, tall // 2), F32), ((1, tall // 2), F32)] + [message] * 4,
-        [((1, tall), F32), ((rows, vals), F32), ((1, tall), F32), state],
-        flops=2 * rows * width * vals + 4 * rows * span * keys,
-    )
-    pieces = scan_states(messages, idx, True)
+    wide_parts = call("wide_grad", partial(wide_grad_kernel, orders), idx, [sm, so2, gu, gu2], flat * 2,
+                      [((half, ff), F32)], flops=4 * rows * ff * width, limit=40)
+    near, wide_parts = fence(near, wide_parts)
+    first = Portions([wide_parts[0:2], wide_parts[2:4], down_parts], orders)
+
+    got = first.reduce_start(0)
+    total = scan_total(near, idx, True)
+    far = scan_far(total, True)
     dq, dk, dv, dc = call(
         "inner_back", partial(inner_back_kernel, dims), idx, [q, k, v, lg, scores, mg, qb, st],
         [((rows, keys), F32), ((rows, keys), F32), ((rows, vals), F32), ((rows, keys), F32)],
         flops=100 * rows * span * keys,
     )
+    far, dq = fence(far, dq)
+    pieces = scan_entering(far, near, idx, True)
+    pieces = [pieces[0]] + [swap(pieces[o], o) for o in (1, 2, 3)]
+    got, pieces = fence(got, pieces)
+    first.reduce_end(0, got)
+    first.sent, pieces = fence(first.sent, pieces)
+    got = first.reduce_start(1)
     lanes = 2 * keys + 2 * vals + 128
-    tg, ga, llm, llo, g1m, g1o, bm, bo = call(
+    tg, ga, llm, g1m, bm, small = call(
         "inputs_back", partial(inputs_back_kernel, dims), idx,
-        [dq, dk, dv, dc, ol, kd, v, lg, tot, st, *pieces, x, hg, first_gain, g12, query_weight, wq2, key_weight, wk2,
-         value_weight, wv2, outgate_weight, wg2, lowrank_in, li2, lowrank_out, lo2],
-        [((rows, width), F32), ((rows, lanes), BF16), ((rows, keys // 2), BF16), ((rows, keys // 2), BF16),
-         ((1, half), F32), ((1, half), F32), ((1, keys // 2), F32), ((1, keys // 2), F32)],
+        [dq, dk, dv, dc, ol, kd, v, lg, tot, st, *pieces, x, hg, first_gain, query_weight, wq2, key_weight, wk2,
+         value_weight, wv2, outgate_weight, wg2, lowrank_in, lowrank_out, pack2, g2o, hgo],
+        [((rows, width), F32), ((rows, lanes + keys // 2), BF16), ((rows, keys // 2), BF16),
+         ((1, half), F32), ((1, keys // 2), F32), ((1, 2 * half + keys // 2 + tall // 2), F32)],
         [((4, quarter, keys), BF16), ((rows, keys), BF16), ((1, keys), F32)],
         flops=2 * rows * width * lanes + 8 * rows * span * keys, limit=40,
     )
-    go2, hl2, no2, lr2 = (across(a) for a in (go, hl, no, lr))
-    ga2, llo2, g1o2, g2o2, bo2, hgo2 = (across(a) for a in (ga, llo, g1o, g2o, bo, hgo))
+    ga2, small2 = across(ga), across(small)
+    got, ga2, small2 = fence(got, ga2, small2)
+    first.reduce_end(1, got)
+    got = first.reduce_start(2)
+    hl2 = across(hl)
     tiles = lanes // 128 + width // 128
     cuts = (0, tiles // 3, 2 * tiles // 3, tiles)
     high = half // 16
@@ -854,15 +975,45 @@
         shapes += [((8, size, 128), BF16)] * 2
     parts = call(
         "attention_grad", partial(attention_grad_kernel, orders, cuts), idx,
-        [nm, no2, ga, ga2, gm, go2, hl, hl2, lr, lr2, llm, llo2, g1m, g1o2, g2m, g2o2, bm, bo2, hgm, hgo2],
+        [nm, no2, ga, ga2, gm, go2, hl, hl2, lr, lr2, llm, g1m, g2m, bm, hgm, small2],
         shapes, [((half, lanes), F32), ((vals // 2, width), F32), ((16, 16, 128), F32)],
         flops=2 * 2 * rows * (half * lanes + width * vals // 2),
     )
-    halves = reduce_all([parts[0:2], parts[2:4], parts[4:6]], orders)
+    got, parts = fence(got, parts)
+    first.reduce_end(2, got)
+    second = Portions([parts[0:2], parts[2:4], parts[4:6]], orders)
+    got, more = fence(first.reduce_start(3), second.reduce_start(0))
+    first.reduce_end(3, got)
+    second.reduce_end(0, more)
+    got, more = fence(first.gather_start(3), second.reduce_start(1))
+    first.gather_end(3, got)
+    second.reduce_end(1, more)
+    got, more = fence(first.gather_start(2), second.reduce_start(2))
+    first.gather_end(2, got)
+    second.reduce_end(2, more)
+    got, more = fence(first.gather_start(1), second.reduce_start(3))
+    first.gather_end(1, got)
+    second.reduce_end(3, more)
+    got, more = fence(first.gather_start(0), second.gather_start(3))
+    first.gather_end(0, got)
+    second.gather_end(3, more)
+    gate_halves, up_halves, down_halves = first.halves
+    more = second.gather_start(2)
+    gate_out = call("gate_open", partial(wide_open_kernel, orders[0]), idx, gate_halves, [((half, ff), F32)])[0]
+    more, gate_out = fence(more, gate_out)
+    second.gather_end(2, more)
+    more = second.gather_start(1)
+    up_out = call("up_open", partial(wide_open_kernel, orders[1]), idx, up_halves, [((half, ff), F32)])[0]
+    more, up_out = fence(more, up_out)
+    second.gather_end(1, more)
+    more = second.gather_start(0)
+    down_out = call("down_open", partial(down_open_kernel, orders[2]), idx, down_halves, [((ff // 2, width), F32)])[0]
+    more, down_out = fence(more, down_out)
+    second.gather_end(0, more)
     opened = call(
-        "attention_open", partial(attention_open_kernel, orders, cuts), idx, [a for pair in halves for a in pair],
+        "attention_open", partial(attention_open_kernel, orders, cuts), idx, [a for pair in second.halves for a in pair],
         [((half, keys), F32), ((half, keys), F32), ((half, vals), F32), ((half, vals), F32),
-         ((half, lowrank_in.shape[1]), F32), ((vals // 2, width), F32), ((lowrank_out.shape[0], keys // 2), F32),
+         ((half, lrank), F32), ((vals // 2, width), F32), ((lrank, keys // 2), F32),
          ((1, half), F32), ((1, half), F32), ((1, keys // 2), F32), ((1, tall // 2), F32)],
         [((16, 16, 128), F32)],
     )

time: 460 us -> 384 us (0.83)
  waiting for transfers between devices: 263 us -> 191 us
  starting transfers between devices: 94.7 us -> 79.2 us
  local copies, waits for them, and re-layouts: 14.8 us -> 25.1 us
    ppermute x60 -> x52, waiting for transfers between devices: 215 us -> 162 us  [swap(): lax.ppermute(array, 'seq', tuple(((one, one ^ bit) for one in range(count...]
    ppermute x29 -> x19, waiting for transfers between devices: 27.7 us -> 2.21 us  [across(): return lax.ppermute(array, 'fsdp', ((0, 1), (1, 0)))]
    ppermute x60 -> x52, starting transfers between devices: 76.1 us -> 61.2 us  [swap(): lax.ppermute(array, 'seq', tuple(((one, one ^ bit) for one in range(count...]
    unnamed x106 -> x124, local copies, waits for them, and re-layouts: 13.3 us -> 22.8 us
    ppermute x6, waiting for transfers between devices: 20.4 us -> 25.9 us  [ahead(): lax.ppermute(array, 'seq', tuple(((one, one + step) for one in range(coun...]
  transfers between devices with their start and end apart: 95 -> 77, of which waited for: 47 -> 30; matrix products, arithmetic and copies ran while one was open for 1% -> 1% of each run, Pallas kernels for 8% -> 17%
where the time goes in v2:
time: 384 us; the launch traced here: 381 us
  waiting for transfers between devices  191 us (50%)
  starting transfers between devices  79.2 us (21%)
  Pallas kernels  79 us (21%)
  local copies, waits for them, and re-layouts  25.1 us (7%)
  other arithmetic  4.91 us (1%)
    ppermute x52, waiting for transfers between devices, swap(): lax.ppermute(array, 'seq', tuple(((one, one ^ bit) for one in range(count...  162 us
    pallas_call x19, Pallas kernels, call(): pl.pallas_call(body, name=name, out_shape=shapes, in_specs=[SMEM] + [VMEM...  79 us
    ppermute x52, starting transfers between devices, swap(): lax.ppermute(array, 'seq', tuple(((one, one ^ bit) for one in range(count...  61.2 us
    ppermute x6, waiting for transfers between devices, ahead(): lax.ppermute(array, 'seq', tuple(((one, one + step) for one in range(coun...  25.9 us
    unnamed x124, local copies, waits for them, and re-layouts  22.8 us
    ppermute x6, starting transfers between devices, ahead(): lax.ppermute(array, 'seq', tuple(((one, one + step) for one in range(coun...  13.3 us
  transfers between devices with their start and end apart: 77, of which 30 were waited for; matrix products, arithmetic and copies ran while one was open for 1% of the time, Pallas kernels for 17%

profile of v2, /device:TPU:0, one launch (start us, length us, event | category | flops | bytes accessed | tf_op | source)
XLA Modules:
  0.0 380.6 jit_solution(3662474072757689352)
XLA Ops:
  12.2 3.1 keys.1
  15.9 2.9 collective-permute-start.3
  18.7 1.5 collective-permute-start.4
  20.3 3.1 collective-permute-done.3.refs_1_.refs_4_
  23.4 4.1 %collective-permute-done.4.refs_2_.refs_5_ = bf16[144,512]{1,0:T(8,128)(2,1)S(1)} collective-permute-done((bf16[144,512]{1,0:T(8,128)(2,1)S(1)}, bf16[144,512]{1,0:T(8,128)(2,1)S(1)}, u32[]{:S(2)}, u32[]{:S(2)}) %collective-permute-start.4) | collective-permute-done | bytes 147488 | tf_op jit(solution)/shard_map/ppermute | solution.py:737
  28.3 5.5 %collective-permute-start.8 = (bf16[144,512]{1,0:T(8,128)(2,1)S(1)}, bf16[144,512]{1,0:T(8,128)(2,1)S(1)}, u32[]{:S(2)}, u32[]{:S(2)}) collective-permute-start(bf16[144,512]{1,0:T(8,128)(2,1)S(1)} %group_total.2), channel_id=1, source_target_pairs={{0,24},{2,26},{4,28},{6,30},{1,25},{3,27},{5,29},{7,31}} | collective-permute-start | bytes 442376 | tf_op jit(solution)/shard_map/ppermute | solution.py:742
  35.1 2.6 collective-permute-start.6
  38.4 6.6 %inner.1 = (bf16[256,512]{1,0:T(8,128)(2,1)S(1)}, f32[256,1024]{1,0:T(8,128)S(1)}, f32[256,1024]{1,0:T(8,128)S(1)}, bf16[8,128,128]{2,1,0:T(8,128)(2,1)S(1)}, bf16[256,512]{1,0:T(8,128)(2,1)S(1)}) custom-call(s32[4]{0:T(128)S(1)} %pad_add_fusion.idx_ref, bf16[256,512]{1,0:T(8,128)(2,1)S(1)} %get-tuple-element.237.nm_ref, ...), custom_call_target="tpu_custom_call" | custom-call | flops 1811939328 | bytes 7864320 | tf_op jit(solution)/shard_map/inner/pallas_call | solution.py:99
  47.8 4.3 %collective-permute-done.11.e1 = bf16[128,512]{1,0:T(8,128)(2,1)S(1)} collective-permute-done((bf16[128,512]{1,0:T(8,128)(2,1)S(1)}, bf16[128,512]{1,0:T(8,128)(2,1)S(1)}, u32[]{:S(2)}, u32[]{:S(2)}) %collective-permute-start.11) | collective-permute-done | bytes 131104 | tf_op jit(solution)/shard_map/ppermute | solution.py:737
  52.1 1.5 collective-permute-start.12
  53.6 3.4 collective-permute-done.12.e2
  57.0 1.5 collective-permute-start.13
  58.5 4.4 %collective-permute-done.13.e3 = bf16[128,512]{1,0:T(8,128)(2,1)S(1)} collective-permute-done((bf16[128,512]{1,0:T(8,128)(2,1)S(1)}, bf16[128,512]{1,0:T(8,128)(2,1)S(1)}, u32[]{:S(2)}, u32[]{:S(2)}) %collective-permute-start.13) | collective-permute-done | bytes 131104 | tf_op jit(solution)/shard_map/ppermute | solution.py:737
  62.9 3.0 hidden.1
  70.0 16.9 %ffn.1 = (f32[256,1024]{1,0:T(8,128)}, bf16[256,1408]{1,0:T(8,128)(2,1)}, bf16[256,1408]{1,0:T(8,128)(2,1)}, bf16[256,5632]{1,0:T(8,128)(2,1)}, f32[256,512]{1,0:T(8,128)S(1)}, /*index=5*/f32[256,512]{1,0:T(8,128)S(1)}) custom-call(s32[4]{0:T(128)S(1)} %pad_add_fusion.idx_ref, bf16[256,512]{1,0:T(8,128)(2,1)S(1)} %get-tuple-element.259.sm_ref.lm_ref, ...), custom_call_target="tpu_custom_call" | custom-call | flops 8858370048 | bytes 25821184 | tf_op jit(solution)/shard_map/ffn/pallas_call | solution.py:99
  90.1 4.5 %gate_back.1 = (f32[256,1024]{1,0:T(8,128)S(1)}, bf16[256,1024]{1,0:T(8,128)(2,1)S(1)}, f32[256,1024]{1,0:T(8,128)S(1)}, bf16[256,1024]{1,0:T(8,128)(2,1)S(1)}, ...) custom-call(s32[4]{0:T(128)S(1)} %pad_add_fusion.idx_ref, ...), custom_call_target="tpu_custom_call" | custom-call | flops 603979776 | bytes 10967296 | tf_op jit(solution)/shard_map/gate_back/pallas_call | solution.py:99
  97.5 1.6 copy-done.28
  101.1 1.5 collective-permute-start.26
  102.6 3.7 down_grad.1
  106.3 2.1 collective-permute-start.33
  108.4 1.8 copy-done.27
  110.2 6.0 %wide_grad.1 = (bf16[8,704,128]{2,1,0:T(8,128)(2,1)S(1)}, bf16[8,704,128]{2,1,0:T(8,128)(2,1)}, bf16[8,704,128]{2,1,0:T(8,128)(2,1)S(1)}, bf16[8,704,128]{2,1,0:T(8,128)(2,1)}) custom-call(s32[4]{0:T(128)S(1)} %pad_add_fusion.idx_ref, bf16[256,512]{1,0:T(8,128)(2,1)S(1)} %copy-done.44, bf16[256,512]{1,0:T(8,128)(2,1)} %collective-permute-done.18.lo_ref, ...), custom_call_target="tpu_custom_call" | custom-call | flops 2952790016 | bytes 12058624 | tf_op jit(solution)/shard_map/wide_grad/pallas_call | solution.py:99
  116.2 1.4 collective-permute-start.30
  121.5 25.9 %collective-permute-done.29.refs_2_ = bf16[144,512]{1,0:T(8,128)(2,1)S(1)} collective-permute-done((bf16[144,512]{1,0:T(8,128)(2,1)S(1)}, bf16[144,512]{1,0:T(8,128)(2,1)S(1)}, u32[]{:S(2)}, u32[]{:S(2)}) %collective-permute-start.29) | collective-permute-done | bytes 147488 | tf_op jit(solution)/shard_map/ppermute | solution.py:742
  151.6 5.8 %inner_back.1 = (f32[256,512]{1,0:T(8,128)S(1)}, f32[256,512]{1,0:T(8,128)S(1)}, f32[256,1024]{1,0:T(8,128)S(1)}, f32[256,512]{1,0:T(8,128)S(1)}) custom-call(s32[4]{0:T(128)S(1)} %pad_add_fusion.idx_ref, bf16[256,512]{1,0:T(8,128)(2,1)S(1)} %copy-done.52, bf16[256,512]{1,0:T(8,128)(2,1)S(1)} %copy-done.42, bf16[256,1024]{1,0:T(8,128)(2,1)S(1)} %copy-done.14, ...), custom_call_target="tpu_custom_call" | custom-call | flops 1677721600 | bytes 6291456 | tf_op jit(solution)/shard_map/inner_back/pallas_call | solution.py:99
  158.3 1.4 collective-permute-start.34
  160.3 3.5 collective-permute-done.34.l1
  166.0 3.8 collective-permute-done.36.l3
  169.7 1.5 slice_add_fusion
  173.2 6.4 %inputs_back.1 = (f32[256,1024]{1,0:T(8,128)}, bf16[256,3456]{1,0:T(8,128)(2,1)}, bf16[256,256]{1,0:T(8,128)(2,1)S(1)}, f32[1,512]{1,0:T(1,128)S(1)}, f32[1,256]{1,0:T(1,128)S(1)}, /*index=5*/f32[1,1408]{1,0:T(1,128)S(1)}) custom-call(s32[4]{0:T(128)S(1)} %pad_add_fusion.idx_ref, f32[256,512]{1,0:T(8,128)S(1)} %get-tuple-element.304.dq_ref, ...), custom_call_target="tpu_custom_call" | custom-call | flops 1811939328 | bytes 16502784 | tf_op jit(solution)/shard_map/inputs_back/pallas_call | solution.py:99
  179.6 2.0 collective-permute-start.37
  181.6 2.9 collective-permute-start.38
  185.8 12.8 %collective-permute-done.37 = bf16[4,704,128]{2,1,0:T(8,128)(2,1)S(1)} collective-permute-done((bf16[4,704,128]{2,1,0:T(8,128)(2,1)}, bf16[4,704,128]{2,1,0:T(8,128)(2,1)S(1)}, u32[]{:S(2)}, u32[]{:S(2)}) %collective-permute-start.37) | collective-permute-done | bytes 720928 | tf_op jit(solution)/shard_map/ppermute | solution.py:737
  198.6 2.4 collective-permute-done.38
  201.0 1.5 collective-permute-done.39
  203.1 1.7 collective-permute-start.43
  205.2 4.3 %attention_grad.1 = (bf16[8,352,128]{2,1,0:T(8,128)(2,1)S(1)}, bf16[8,352,128]{2,1,0:T(8,128)(2,1)S(1)}, bf16[8,352,128]{2,1,0:T(8,128)(2,1)S(1)}, bf16[8,352,12...) custom-call(s32[4]{0:T(128)S(1)} %pad_add_fusion.idx_ref, ...), custom_call_target="tpu_custom_call" | custom-call | flops 2214592512 | bytes 10185728 | tf_op jit(solution)/shard_map/attention_grad/pallas_call | solution.py:99
  209.6 2.5 collective-permute-done.44
  216.8 21.6 %collective-permute-done.46 = bf16[1,2112,128]{2,1,0:T(8,128)(2,1)S(1)} collective-permute-done((bf16[1,2112,128]{2,1,0:T(8,128)(2,1)S(1)}, bf16[1,2112,128]{2,1,0:T(8,128)(2,1)S(1)}, u32[]{:S(2)}, u32[]{:S(2)}) %collective-permute-start.46) | collective-permute-done | bytes 540704 | tf_op jit(solution)/shard_map/ppermute | solution.py:737
  238.4 3.6 collective-permute-done.49
  242.5 3.0 collective-permute-start.50
  245.6 1.5 collective-permute-start.53
  248.0 18.2 %collective-permute-done.50 = bf16[1,2112,128]{2,1,0:T(8,128)(2,1)S(1)} collective-permute-done((bf16[1,2112,128]{2,1,0:T(8,128)(2,1)S(1)}, bf16[1,2112,128]{2,1,0:T(8,128)(2,1)S(1)}, u32[]{:S(2)}, u32[]{:S(2)}) %collective-permute-start.50) | collective-permute-done | bytes 540704 | tf_op jit(solution)/shard_map/ppermute | solution.py:737
  266.3 1.5 collective-permute-start.58
  270.8 2.0 collective-permute-done.58
  273.9 11.3 %collective-permute-done.57 = bf16[2,352,128]{2,1,0:T(8,128)(2,1)S(1)} collective-permute-done((bf16[2,352,128]{2,1,0:T(8,128)(2,1)S(1)}, bf16[2,352,128]{2,1,0:T(8,128)(2,1)S(1)}, u32[]{:S(2)}, u32[]{:S(2)}) %collective-permute-start.57) | collective-permute-done | bytes 180256 | tf_op jit(solution)/shard_map/ppermute | solution.py:737
  285.5 1.7 collective-permute-start.62
  287.7 3.1 collective-permute-start.63
  290.9 13.3 %collective-permute-done.63 = bf16[1,1072,128]{2,1,0:T(8,128)(2,1)S(1)} collective-permute-done((bf16[1,1072,128]{2,1,0:T(8,128)(2,1)S(1)}, bf16[1,1072,128]{2,1,0:T(8,128)(2,1)S(1)}, u32[]{:S(2)}, u32[]{:S(2)}) %collective-permute-start.63) | collective-permute-done | bytes 274464 | tf_op jit(solution)/shard_map/ppermute | solution.py:737
  304.2 5.5 %collective-permute-done.61 = bf16[4,704,128]{2,1,0:T(8,128)(2,1)S(1)} collective-permute-done((bf16[4,704,128]{2,1,0:T(8,128)(2,1)S(1)}, bf16[4,704,128]{2,1,0:T(8,128)(2,1)S(1)}, u32[]{:S(2)}, u32[]{:S(2)}) %collective-permute-start.61) | collective-permute-done | bytes 720928 | tf_op jit(solution)/shard_map/ppermute | solution.py:737
  311.1 1.8 collective-permute-start.64
  313.0 1.9 collective-permute-start.67
  314.9 23.4 %collective-permute-done.67 = bf16[1,1072,128]{2,1,0:T(8,128)(2,1)S(1)} collective-permute-done((bf16[1,1072,128]{2,1,0:T(8,128)(2,1)S(1)}, bf16[1,1072,128]{2,1,0:T(8,128)(2,1)S(1)}, u32[]{:S(2)}, u32[]{:S(2)}) %collective-permute-start.67) | collective-permute-done | bytes 274464 | tf_op jit(solution)/shard_map/ppermute | solution.py:737
  338.4 1.8 collective-permute-done.66.got_ref
  340.2 1.7 collective-permute-start.70
  342.7 2.2 collective-permute-start.68
  344.9 3.5 gate_open.1
  349.8 2.1 collective-permute-start.72
  352.5 3.5 up_open.1
  356.0 5.3 %collective-permute-done.72 = bf16[4,352,128]{2,1,0:T(8,128)(2,1)S(1)} collective-permute-done((bf16[4,352,128]{2,1,0:T(8,128)(2,1)S(1)}, bf16[4,352,128]{2,1,0:T(8,128)(2,1)S(1)}, u32[]{:S(2)}, u32[]{:S(2)}) %collective-permute-start.72) | collective-permute-done | bytes 360480 | tf_op jit(solution)/shard_map/ppermute | solution.py:737
  361.3 2.0 collective-permute-done.71
  365.7 3.9 %down_open.1 = f32[1408,1024]{1,0:T(8,128)} custom-call(s32[4]{0:T(128)S(1)} %pad_add_fusion.idx_ref, bf16[8,704,128]{2,1,0:T(8,128)(2,1)S(1)} %pad_maximum_fusion.2.own_ref, bf16[8,704,128]{2,1,0:T(8,128)(2,1)S(1)} %collective-permute-done.66.got_ref), custom_call_target="tpu_custom_call" | custom-call | bytes 8650752 | tf_op jit(solution)/shard_map/down_open/pallas_call | solution.py:99
  369.6 5.4 %collective-permute-done.75.r1 = bf16[8,352,128]{2,1,0:T(8,128)(2,1)S(1)} collective-permute-done((bf16[8,352,128]{2,1,0:T(8,128)(2,1)S(1)}, bf16[8,352,128]{2,1,0:T(8,128)(2,1)S(1)}, u32[]{:S(2)}, u32[]{:S(2)}) %collective-permute-start.75) | collective-permute-done | bytes 720928 | tf_op jit(solution)/shard_map/ppermute | solution.py:737
  375.6 4.0 %attention_open.1 = (f32[512,512]{1,0:T(8,128)}, f32[512,512]{1,0:T(8,128)}, f32[512,1024]{1,0:T(8,128)}, f32[512,1024]{1,0:T(8,128)}, f32[512,16]{1,0:T(8,128)S...) custom-call(s32[4]{0:T(128)S(1)} %pad_add_fusion.idx_ref, ...), custom_call_target="tpu_custom_call" | custom-call | bytes 12834304 | tf_op jit(solution)/shard_map/attention_open/pallas_call | solution.py:99
  (290 shorter events, 64.6 us)
Async XLA Ops:
  15.3 22.5 %collective-permute-start.10 = (bf16[512,1024]{1,0:T(8,128)(2,1)S(1)}, bf16[512,1024]{1,0:T(8,128)(2,1)S(1)}, u32[]{:S(2)}, u32[]{:S(2)}) collective-permute-start(bf16[512,1024]{1,0:T(8,128)(2,1)S(1)} %copy-done.9), channel_id=1, source_target_pairs={{0,1},{1,0},{2,3},{3,2},{4,5},{5,4},{6,7},{7,6},{8,9},{9,8},{10,11... | collective-permute-start | bytes 3145736 | tf_op jit(solution)/shard_map/ppermute | solution.py:732
  15.7 22.0 %collective-permute-start.9 = (bf16[512,512]{1,0:T(8,128)(2,1)S(1)}, bf16[512,512]{1,0:T(8,128)(2,1)S(1)}, u32[]{:S(2)}, u32[]{:S(2)}) collective-permute-start(bf16[512,512]{1,0:T(8,128)(2,1)S(1)} %copy-done.12), channel_id=1, source_target_pairs={{0,1},{1,0},{2,3},{3,2},{4,5},{5,4},{6,7},{7,6},{8,9},{9,8},{10,11... | collective-permute-start | bytes 1572872 | tf_op jit(solution)/shard_map/ppermute | solution.py:732
  15.9 7.5 %collective-permute-start.3 = (bf16[144,512]{1,0:T(8,128)(2,1)S(1)}, bf16[144,512]{1,0:T(8,128)(2,1)S(1)}, u32[]{:S(2)}, u32[]{:S(2)}) collective-permute-start(bf16[144,512]{1,0:T(8,128)(2,1)S(1)} %get-tuple-element.227), channel_id=1, source_target_pairs={{0,2},{2,0},{4,6},{6,4},{8,10},{10,8},{12,14},{14,12},{16,18},{18,... | collective-permute-start | bytes 442376 | tf_op jit(solution)/shard_map/ppermute | solution.py:737
  18.7 8.8 %collective-permute-start.4 = (bf16[144,512]{1,0:T(8,128)(2,1)S(1)}, bf16[144,512]{1,0:T(8,128)(2,1)S(1)}, u32[]{:S(2)}, u32[]{:S(2)}) collective-permute-start(bf16[144,512]{1,0:T(8,128)(2,1)S(1)} %get-tuple-element.228), channel_id=1, source_target_pairs={{0,4},{2,6},{4,0},{6,2},{8,12},{10,14},{12,8},{14,10},{16,20},{18,... | collective-permute-start | bytes 442376 | tf_op jit(solution)/shard_map/ppermute | solution.py:737
  20.3 7.3 %collective-permute-start.5 = (bf16[144,512]{1,0:T(8,128)(2,1)S(1)}, bf16[144,512]{1,0:T(8,128)(2,1)S(1)}, u32[]{:S(2)}, u32[]{:S(2)}) collective-permute-start(bf16[144,512]{1,0:T(8,128)(2,1)S(1)} %get-tuple-element.229), channel_id=1, source_target_pairs={{0,6},{2,4},{4,2},{6,0},{8,14},{10,12},{12,10},{14,8},{16,22},{18,... | collective-permute-start | bytes 442376 | tf_op jit(solution)/shard_map/ppermute | solution.py:737
  28.3 16.8 %collective-permute-start.8 = (bf16[144,512]{1,0:T(8,128)(2,1)S(1)}, bf16[144,512]{1,0:T(8,128)(2,1)S(1)}, u32[]{:S(2)}, u32[]{:S(2)}) collective-permute-start(bf16[144,512]{1,0:T(8,128)(2,1)S(1)} %group_total.2), channel_id=1, source_target_pairs={{0,24},{2,26},{4,28},{6,30},{1,25},{3,27},{5,29},{7,31}} | collective-permute-start | bytes 442376 | tf_op jit(solution)/shard_map/ppermute | solution.py:742
  33.8 11.3 %collective-permute-start.7 = (bf16[144,512]{1,0:T(8,128)(2,1)S(1)}, bf16[144,512]{1,0:T(8,128)(2,1)S(1)}, u32[]{:S(2)}, u32[]{:S(2)}) collective-permute-start(bf16[144,512]{1,0:T(8,128)(2,1)S(1)} %group_total.2), channel_id=1, source_target_pairs={{0,16},{2,18},{4,20},{6,22},{8,24},{10,26},{12,28},{14,30},{1,17},... | collective-permute-start | bytes 442376 | tf_op jit(solution)/shard_map/ppermute | solution.py:742
  35.1 10.0 %collective-permute-start.6 = (bf16[144,512]{1,0:T(8,128)(2,1)S(1)}, bf16[144,512]{1,0:T(8,128)(2,1)S(1)}, u32[]{:S(2)}, u32[]{:S(2)}) collective-permute-start(bf16[144,512]{1,0:T(8,128)(2,1)S(1)} %group_total.2), channel_id=1, source_target_pairs={{0,8},{2,10},{4,12},{6,14},{8,16},{10,18},{12,20},{14,22},{16,24},... | collective-permute-start | bytes 442376 | tf_op jit(solution)/shard_map/ppermute | solution.py:742
  37.8 29.7 %collective-permute-start.15 = (bf16[512,2816]{1,0:T(8,128)(2,1)S(1)}, bf16[512,2816]{1,0:T(8,128)(2,1)S(1)}, u32[]{:S(2)}, u32[]{:S(2)}) collective-permute-start(bf16[512,2816]{1,0:T(8,128)(2,1)S(1)} %copy-done.57), channel_id=1, source_target_pairs={{0,1},{1,0},{2,3},{3,2},{4,5},{5,4},{6,7},{7,6},{8,9},{9,8},{10,11... | collective-permute-start | bytes 8650760 | tf_op jit(solution)/shard_map/ppermute | solution.py:732
  37.9 29.6 %collective-permute-start.16 = (bf16[512,2816]{1,0:T(8,128)(2,1)}, bf16[512,2816]{1,0:T(8,128)(2,1)S(1)}, u32[]{:S(2)}, u32[]{:S(2)}) collective-permute-start(bf16[512,2816]{1,0:T(8,128)(2,1)} %wu_own.1), channel_id=1, source_target_pairs={{0,1},{1,0},{2,3},{3,2},{4,5},{5,4},{6,7},{7,6},{8,9},{9,8},{10,11... | collective-permute-start | bytes 8650760 | tf_op jit(solution)/shard_map/ppermute | solution.py:732
  46.0 22.0 %collective-permute-start.17 = (bf16[1408,1024]{1,0:T(8,128)(2,1)S(1)}, bf16[1408,1024]{1,0:T(8,128)(2,1)}, u32[]{:S(2)}, u32[]{:S(2)}) collective-permute-start(bf16[1408,1024]{1,0:T(8,128)(2,1)S(1)} %copy-done.58), channel_id=1, source_target_pairs={{0,1},{1,0},{2,3},{3,2},{4,5},{5,4},{6,7},{7,6},{8,9},{9,8},{10,11... | collective-permute-start | bytes 8650760 | tf_op jit(solution)/shard_map/ppermute | solution.py:732
  46.1 16.8 %collective-permute-start.14 = (bf16[512,1024]{1,0:T(8,128)(2,1)S(1)}, bf16[512,1024]{1,0:T(8,128)(2,1)S(1)}, u32[]{:S(2)}, u32[]{:S(2)}) collective-permute-start(bf16[512,1024]{1,0:T(8,128)(2,1)S(1)} %copy-done.4), channel_id=1, source_target_pairs={{0,1},{1,0},{2,3},{3,2},{4,5},{5,4},{6,7},{7,6},{8,9},{9,8},{10,11... | collective-permute-start | bytes 3145736 | tf_op jit(solution)/shard_map/ppermute | solution.py:732
  66.9 20.0 %collective-permute-start.21 = (bf16[256,16]{1,0:T(8,128)(2,1)}, bf16[256,16]{1,0:T(8,128)(2,1)S(1)}, u32[]{:S(2)}, u32[]{:S(2)}) collective-permute-start(bf16[256,16]{1,0:T(8,128)(2,1)} %get-tuple-element.271.lrm_ref), channel_id=1, source_target_pairs={{0,1},{1,0},{2,3},{3,2},{4,5},{5,4},{6,7},{7,6},{8,9},{9,8},{10,11... | collective-permute-start | bytes 24584 | tf_op jit(solution)/shard_map/ppermute | solution.py:732
  66.9 20.6 %collective-permute-start.19 = (bf16[256,512]{1,0:T(8,128)(2,1)}, bf16[256,512]{1,0:T(8,128)(2,1)S(1)}, u32[]{:S(2)}, u32[]{:S(2)}) collective-permute-start(bf16[256,512]{1,0:T(8,128)(2,1)} %get-tuple-element.269.no_ref), channel_id=1, source_target_pairs={{0,1},{1,0},{2,3},{3,2},{4,5},{5,4},{6,7},{7,6},{8,9},{9,8},{10,11... | collective-permute-start | bytes 786440 | tf_op jit(solution)/shard_map/ppermute | solution.py:732
  67.4 20.8 %collective-permute-start.18 = (bf16[256,512]{1,0:T(8,128)(2,1)}, bf16[256,512]{1,0:T(8,128)(2,1)}, u32[]{:S(2)}, u32[]{:S(2)}) collective-permute-start(bf16[256,512]{1,0:T(8,128)(2,1)} %get-tuple-element.262.so_ref), channel_id=1, source_target_pairs={{0,1},{1,0},{2,3},{3,2},{4,5},{5,4},{6,7},{7,6},{8,9},{9,8},{10,11... | collective-permute-start | bytes 786440 | tf_op jit(solution)/shard_map/ppermute | solution.py:732
  67.5 20.8 %collective-permute-start.20 = (bf16[256,512]{1,0:T(8,128)(2,1)}, bf16[256,512]{1,0:T(8,128)(2,1)}, u32[]{:S(2)}, u32[]{:S(2)}) collective-permute-start(bf16[256,512]{1,0:T(8,128)(2,1)} %get-tuple-element.270), channel_id=1, source_target_pairs={{0,1},{1,0},{2,3},{3,2},{4,5},{5,4},{6,7},{7,6},{8,9},{9,8},{10,11... | collective-permute-start | bytes 786440 | tf_op jit(solution)/shard_map/ppermute | solution.py:732
  88.3 9.2 %collective-permute-start.23 = (bf16[256,5632]{1,0:T(8,128)(2,1)}, bf16[256,5632]{1,0:T(8,128)(2,1)S(1)}, u32[]{:S(2)}, u32[]{:S(2)}) collective-permute-start(bf16[256,5632]{1,0:T(8,128)(2,1)} %get-tuple-element.284.gm_ref), channel_id=1, source_target_pairs={{0,1},{1,0},{2,3},{3,2},{4,5},{5,4},{6,7},{7,6},{8,9},{9,8},{10,11... | collective-permute-start | bytes 8650760 | tf_op jit(solution)/shard_map/ppermute | solution.py:732
  88.3 9.1 %collective-permute-start.22 = (bf16[256,1408]{1,0:T(8,128)(2,1)}, bf16[256,1408]{1,0:T(8,128)(2,1)S(1)}, u32[]{:S(2)}, u32[]{:S(2)}) collective-permute-start(bf16[256,1408]{1,0:T(8,128)(2,1)} %get-tuple-element.283), channel_id=1, source_target_pairs={{0,1},{1,0},{2,3},{3,2},{4,5},{5,4},{6,7},{7,6},{8,9},{9,8},{10,11... | collective-permute-start | bytes 2162696 | tf_op jit(solution)/shard_map/ppermute | solution.py:732
  88.8 13.8 %collective-permute-start.32 = (bf16[256,1024]{1,0:T(8,128)(2,1)}, bf16[256,1024]{1,0:T(8,128)(2,1)S(1)}, u32[]{:S(2)}, u32[]{:S(2)}) collective-permute-start(bf16[256,1024]{1,0:T(8,128)(2,1)} %get-tuple-element.264.e_ref.gm_ref), channel_id=1, source_target_pairs={{0,1},{1,0},{2,3},{3,2},{4,5},{5,4},{6,7},{7,6},{8,9},{9,8},{10,11... | collective-permute-start | bytes 1572872 | tf_op jit(solution)/shard_map/ppermute | solution.py:732
  99.0 17.2 %collective-permute-start.24 = (bf16[144,512]{1,0:T(8,128)(2,1)}, bf16[144,512]{1,0:T(8,128)(2,1)S(1)}, u32[]{:S(2)}, u32[]{:S(2)}) collective-permute-start(bf16[144,512]{1,0:T(8,128)(2,1)} %get-tuple-element.286), channel_id=1, source_target_pairs={{0,2},{2,0},{4,6},{6,4},{8,10},{10,8},{12,14},{14,12},{16,18},{18,... | collective-permute-start | bytes 442376 | tf_op jit(solution)/shard_map/ppermute | solution.py:737
  100.3 16.0 %collective-permute-start.25 = (bf16[144,512]{1,0:T(8,128)(2,1)}, bf16[144,512]{1,0:T(8,128)(2,1)S(1)}, u32[]{:S(2)}, u32[]{:S(2)}) collective-permute-start(bf16[144,512]{1,0:T(8,128)(2,1)} %get-tuple-element.287), channel_id=1, source_target_pairs={{0,4},{2,6},{4,0},{6,2},{8,12},{10,14},{12,8},{14,10},{16,20},{18,... | collective-permute-start | bytes 442376 | tf_op jit(solution)/shard_map/ppermute | solution.py:737
  101.1 15.2 %collective-permute-start.26 = (bf16[144,512]{1,0:T(8,128)(2,1)}, bf16[144,512]{1,0:T(8,128)(2,1)S(1)}, u32[]{:S(2)}, u32[]{:S(2)}) collective-permute-start(bf16[144,512]{1,0:T(8,128)(2,1)} %get-tuple-element.288), channel_id=1, source_target_pairs={{0,6},{2,4},{4,2},{6,0},{8,14},{10,12},{12,10},{14,8},{16,22},{18,... | collective-permute-start | bytes 442376 | tf_op jit(solution)/shard_map/ppermute | solution.py:737
  106.3 63.5 %collective-permute-start.33 = (bf16[8,704,128]{2,1,0:T(8,128)(2,1)S(1)}, bf16[8,704,128]{2,1,0:T(8,128)(2,1)}, u32[]{:S(2)}, u32[]{:S(2)}) collective-permute-start(bf16[8,704,128]{2,1,0:T(8,128)(2,1)S(1)} %get-tuple-element.315), channel_id=1, source_target_pairs={{0,8},{2,10},{4,12},{6,14},{8,0},{10,2},{12,4},{14,6},{16,24},{18,... | collective-permute-start | bytes 4325384 | tf_op jit(solution)/shard_map/ppermute | solution.py:737
  116.2 53.5 %collective-permute-start.30 = (bf16[8,704,128]{2,1,0:T(8,128)(2,1)}, bf16[8,704,128]{2,1,0:T(8,128)(2,1)S(1)}, u32[]{:S(2)}, u32[]{:S(2)}) collective-permute-start(bf16[8,704,128]{2,1,0:T(8,128)(2,1)} %get-tuple-element.311), channel_id=1, source_target_pairs={{0,2},{2,0},{4,6},{6,4},{8,10},{10,8},{12,14},{14,12},{16,18},{18,... | collective-permute-start | bytes 4325384 | tf_op jit(solution)/shard_map/ppermute | solution.py:737
  117.6 52.1 %collective-permute-start.31 = (bf16[8,704,128]{2,1,0:T(8,128)(2,1)}, bf16[8,704,128]{2,1,0:T(8,128)(2,1)S(1)}, u32[]{:S(2)}, u32[]{:S(2)}) collective-permute-start(bf16[8,704,128]{2,1,0:T(8,128)(2,1)} %get-tuple-element.312), channel_id=1, source_target_pairs={{0,4},{2,6},{4,0},{6,2},{8,12},{10,14},{12,8},{14,10},{16,20},{18,... | collective-permute-start | bytes 4325384 | tf_op jit(solution)/shard_map/ppermute | solution.py:737
  118.9 28.5 %collective-permute-start.29 = (bf16[144,512]{1,0:T(8,128)(2,1)S(1)}, bf16[144,512]{1,0:T(8,128)(2,1)S(1)}, u32[]{:S(2)}, u32[]{:S(2)}) collective-permute-start(bf16[144,512]{1,0:T(8,128)(2,1)S(1)} %group_total.3), channel_id=1, source_target_pairs={{24,0},{26,2},{28,4},{30,6},{25,1},{27,3},{29,5},{31,7}} | collective-permute-start | bytes 442376 | tf_op jit(solution)/shard_map/ppermute | solution.py:742
  120.2 37.2 %collective-permute-start.28 = (bf16[144,512]{1,0:T(8,128)(2,1)S(1)}, bf16[144,512]{1,0:T(8,128)(2,1)S(1)}, u32[]{:S(2)}, u32[]{:S(2)}) collective-permute-start(bf16[144,512]{1,0:T(8,128)(2,1)S(1)} %group_total.3), channel_id=1, source_target_pairs={{16,0},{18,2},{20,4},{22,6},{24,8},{26,10},{28,12},{30,14},{17,1},... | collective-permute-start | bytes 442376 | tf_op jit(solution)/shard_map/ppermute | solution.py:742
  147.4 10.0 %collective-permute-start.27 = (bf16[144,512]{1,0:T(8,128)(2,1)S(1)}, bf16[144,512]{1,0:T(8,128)(2,1)S(1)}, u32[]{:S(2)}, u32[]{:S(2)}) collective-permute-start(bf16[144,512]{1,0:T(8,128)(2,1)S(1)} %group_total.3), channel_id=1, source_target_pairs={{8,0},{10,2},{12,4},{14,6},{16,8},{18,10},{20,12},{22,14},{24,16},... | collective-permute-start | bytes 442376 | tf_op jit(solution)/shard_map/ppermute | solution.py:742
  179.6 22.9 %collective-permute-start.40 = (bf16[256,3456]{1,0:T(8,128)(2,1)}, bf16[256,3456]{1,0:T(8,128)(2,1)S(1)}, u32[]{:S(2)}, u32[]{:S(2)}) collective-permute-start(bf16[256,3456]{1,0:T(8,128)(2,1)} %get-tuple-element.343.gm_ref), channel_id=1, source_target_pairs={{0,1},{1,0},{2,3},{3,2},{4,5},{5,4},{6,7},{7,6},{8,9},{9,8},{10,11... | collective-permute-start | bytes 5308424 | tf_op jit(solution)/shard_map/ppermute | solution.py:732
  179.6 19.0 %collective-permute-start.37 = (bf16[4,704,128]{2,1,0:T(8,128)(2,1)}, bf16[4,704,128]{2,1,0:T(8,128)(2,1)S(1)}, u32[]{:S(2)}, u32[]{:S(2)}) collective-permute-start(bf16[4,704,128]{2,1,0:T(8,128)(2,1)} %get-tuple-element.340), channel_id=1, source_target_pairs={{0,4},{2,6},{4,0},{6,2},{8,12},{10,14},{12,8},{14,10},{16,20},{18,... | collective-permute-start | bytes 2162696 | tf_op jit(solution)/shard_map/ppermute | solution.py:737
  181.6 19.4 %collective-permute-start.38 = (bf16[4,704,128]{2,1,0:T(8,128)(2,1)S(1)}, bf16[4,704,128]{2,1,0:T(8,128)(2,1)S(1)}, u32[]{:S(2)}, u32[]{:S(2)}) collective-permute-start(bf16[4,704,128]{2,1,0:T(8,128)(2,1)S(1)} %get-tuple-element.341), channel_id=1, source_target_pairs={{0,8},{2,10},{4,12},{6,14},{8,0},{10,2},{12,4},{14,6},{16,24},{18,... | collective-permute-start | bytes 2162696 | tf_op jit(solution)/shard_map/ppermute | solution.py:737
  184.5 18.0 %collective-permute-start.39 = (bf16[4,704,128]{2,1,0:T(8,128)(2,1)S(1)}, bf16[4,704,128]{2,1,0:T(8,128)(2,1)S(1)}, u32[]{:S(2)}, u32[]{:S(2)}) collective-permute-start(bf16[4,704,128]{2,1,0:T(8,128)(2,1)S(1)} %get-tuple-element.342), channel_id=1, source_target_pairs={{0,2},{2,0},{4,6},{6,4},{8,10},{10,8},{12,14},{14,12},{16,18},{18,... | collective-permute-start | bytes 2162696 | tf_op jit(solution)/shard_map/ppermute | solution.py:737
  185.7 19.5 %collective-permute-start.45 = (bf16[256,1024]{1,0:T(8,128)(2,1)S(1)}, bf16[256,1024]{1,0:T(8,128)(2,1)S(1)}, u32[]{:S(2)}, u32[]{:S(2)}) collective-permute-start(bf16[256,1024]{1,0:T(8,128)(2,1)S(1)} %copy-done.34), channel_id=1, source_target_pairs={{0,1},{1,0},{2,3},{3,2},{4,5},{5,4},{6,7},{7,6},{8,9},{9,8},{10,11... | collective-permute-start | bytes 1572872 | tf_op jit(solution)/shard_map/ppermute | solution.py:732
  202.6 9.5 %collective-permute-start.44 = (bf16[2,704,128]{2,1,0:T(8,128)(2,1)S(1)}, bf16[2,704,128]{2,1,0:T(8,128)(2,1)S(1)}, u32[]{:S(2)}, u32[]{:S(2)}) collective-permute-start(bf16[2,704,128]{2,1,0:T(8,128)(2,1)S(1)} %get-tuple-element.460), channel_id=1, source_target_pairs={{0,4},{2,6},{4,0},{6,2},{8,12},{10,14},{12,8},{14,10},{16,20},{18,... | collective-permute-start | bytes 1081352 | tf_op jit(solution)/shard_map/ppermute | solution.py:737
  203.1 9.3 %collective-permute-start.43 = (bf16[2,704,128]{2,1,0:T(8,128)(2,1)S(1)}, bf16[2,704,128]{2,1,0:T(8,128)(2,1)S(1)}, u32[]{:S(2)}, u32[]{:S(2)}) collective-permute-start(bf16[2,704,128]{2,1,0:T(8,128)(2,1)S(1)} %get-tuple-element.459), channel_id=1, source_target_pairs={{0,2},{2,0},{4,6},{6,4},{8,10},{10,8},{12,14},{14,12},{16,18},{18,... | collective-permute-start | bytes 1081352 | tf_op jit(solution)/shard_map/ppermute | solution.py:737
  204.8 8.9 %collective-permute-start.42 = (bf16[2,704,128]{2,1,0:T(8,128)(2,1)S(1)}, bf16[2,704,128]{2,1,0:T(8,128)(2,1)S(1)}, u32[]{:S(2)}, u32[]{:S(2)}) collective-permute-start(bf16[2,704,128]{2,1,0:T(8,128)(2,1)S(1)} %get-tuple-element.457), channel_id=1, source_target_pairs={{0,8},{2,10},{4,12},{6,14},{8,0},{10,2},{12,4},{14,6},{16,24},{18,... | collective-permute-start | bytes 1081352 | tf_op jit(solution)/shard_map/ppermute | solution.py:737
  213.9 24.4 %collective-permute-start.46 = (bf16[1,2112,128]{2,1,0:T(8,128)(2,1)S(1)}, bf16[1,2112,128]{2,1,0:T(8,128)(2,1)S(1)}, u32[]{:S(2)}, u32[]{:S(2)}) collective-permute-start(bf16[1,2112,128]{2,1,0:T(8,128)(2,1)S(1)} %pad_maximum_fusion.9), channel_id=1, source_target_pairs={{0,16},{2,18},{4,20},{6,22},{8,24},{10,26},{12,28},{14,30},{16,0},... | collective-permute-start | bytes 1622024 | tf_op jit(solution)/shard_map/ppermute | solution.py:737
  213.9 28.0 %collective-permute-start.49 = (bf16[8,368,128]{2,1,0:T(8,128)(2,1)S(1)}, bf16[8,368,128]{2,1,0:T(8,128)(2,1)S(1)}, u32[]{:S(2)}, u32[]{:S(2)}) collective-permute-start(bf16[8,368,128]{2,1,0:T(8,128)(2,1)S(1)} %get-tuple-element.372), channel_id=1, source_target_pairs={{0,8},{2,10},{4,12},{6,14},{8,0},{10,2},{12,4},{14,6},{16,24},{18,... | collective-permute-start | bytes 2261000 | tf_op jit(solution)/shard_map/ppermute | solution.py:737
  214.6 23.7 %collective-permute-start.47 = (bf16[8,352,128]{2,1,0:T(8,128)(2,1)S(1)}, bf16[8,352,128]{2,1,0:T(8,128)(2,1)S(1)}, u32[]{:S(2)}, u32[]{:S(2)}) collective-permute-start(bf16[8,352,128]{2,1,0:T(8,128)(2,1)S(1)} %get-tuple-element.370), channel_id=1, source_target_pairs={{0,2},{2,0},{4,6},{6,4},{8,10},{10,8},{12,14},{14,12},{16,18},{18,... | collective-permute-start | bytes 2162696 | tf_op jit(solution)/shard_map/ppermute | solution.py:737
  215.6 22.7 %collective-permute-start.48 = (bf16[8,352,128]{2,1,0:T(8,128)(2,1)S(1)}, bf16[8,352,128]{2,1,0:T(8,128)(2,1)S(1)}, u32[]{:S(2)}, u32[]{:S(2)}) collective-permute-start(bf16[8,352,128]{2,1,0:T(8,128)(2,1)S(1)} %get-tuple-element.371), channel_id=1, source_target_pairs={{0,4},{2,6},{4,0},{6,2},{8,12},{10,14},{12,8},{14,10},{16,20},{18,... | collective-permute-start | bytes 2162696 | tf_op jit(solution)/shard_map/ppermute | solution.py:737
  242.1 24.1 %collective-permute-start.52 = (bf16[4,352,128]{2,1,0:T(8,128)(2,1)S(1)}, bf16[4,352,128]{2,1,0:T(8,128)(2,1)S(1)}, u32[]{:S(2)}, u32[]{:S(2)}) collective-permute-start(bf16[4,352,128]{2,1,0:T(8,128)(2,1)S(1)} %get-tuple-element.453), channel_id=1, source_target_pairs={{0,8},{2,10},{4,12},{6,14},{8,0},{10,2},{12,4},{14,6},{16,24},{18,... | collective-permute-start | bytes 1081352 | tf_op jit(solution)/shard_map/ppermute | solution.py:737
  242.5 23.7 %collective-permute-start.50 = (bf16[1,2112,128]{2,1,0:T(8,128)(2,1)S(1)}, bf16[1,2112,128]{2,1,0:T(8,128)(2,1)S(1)}, u32[]{:S(2)}, u32[]{:S(2)}) collective-permute-start(bf16[1,2112,128]{2,1,0:T(8,128)(2,1)S(1)} %pad_maximum_fusion.10), channel_id=1, source_target_pairs={{0,16},{2,18},{4,20},{6,22},{8,24},{10,26},{12,28},{14,30},{16,0},... | collective-permute-start | bytes 1622024 | tf_op jit(solution)/shard_map/ppermute | solution.py:737
  245.6 20.6 %collective-permute-start.53 = (bf16[4,368,128]{2,1,0:T(8,128)(2,1)S(1)}, bf16[4,368,128]{2,1,0:T(8,128)(2,1)S(1)}, u32[]{:S(2)}, u32[]{:S(2)}) collective-permute-start(bf16[4,368,128]{2,1,0:T(8,128)(2,1)S(1)} %get-tuple-element.451), channel_id=1, source_target_pairs={{0,2},{2,0},{4,6},{6,4},{8,10},{10,8},{12,14},{14,12},{16,18},{18,... | collective-permute-start | bytes 1130504 | tf_op jit(solution)/shard_map/ppermute | solution.py:737
  247.2 19.1 %collective-permute-start.51 = (bf16[4,352,128]{2,1,0:T(8,128)(2,1)S(1)}, bf16[4,352,128]{2,1,0:T(8,128)(2,1)S(1)}, u32[]{:S(2)}, u32[]{:S(2)}) collective-permute-start(bf16[4,352,128]{2,1,0:T(8,128)(2,1)S(1)} %get-tuple-element.455), channel_id=1, source_target_pairs={{0,4},{2,6},{4,0},{6,2},{8,12},{10,14},{12,8},{14,10},{16,20},{18,... | collective-permute-start | bytes 1081352 | tf_op jit(solution)/shard_map/ppermute | solution.py:737
  267.8 17.4 %collective-permute-start.59 = (bf16[2,368,128]{2,1,0:T(8,128)(2,1)S(1)}, bf16[2,368,128]{2,1,0:T(8,128)(2,1)S(1)}, u32[]{:S(2)}, u32[]{:S(2)}) collective-permute-start(bf16[2,368,128]{2,1,0:T(8,128)(2,1)S(1)} %get-tuple-element.463), channel_id=1, source_target_pairs={{0,4},{2,6},{4,0},{6,2},{8,12},{10,14},{12,8},{14,10},{16,20},{18,... | collective-permute-start | bytes 565256 | tf_op jit(solution)/shard_map/ppermute | solution.py:737
  268.8 16.4 %collective-permute-start.56 = (bf16[2,704,128]{2,1,0:T(8,128)(2,1)S(1)}, bf16[2,704,128]{2,1,0:T(8,128)(2,1)S(1)}, u32[]{:S(2)}, u32[]{:S(2)}) collective-permute-start(bf16[2,704,128]{2,1,0:T(8,128)(2,1)S(1)} %pad_maximum_fusion.14), channel_id=1, source_target_pairs={{0,4},{2,6},{4,0},{6,2},{8,12},{10,14},{12,8},{14,10},{16,20},{18,... | collective-permute-start | bytes 1081352 | tf_op jit(solution)/shard_map/ppermute | solution.py:737
  270.1 15.1 %collective-permute-start.55 = (bf16[2,704,128]{2,1,0:T(8,128)(2,1)S(1)}, bf16[2,704,128]{2,1,0:T(8,128)(2,1)S(1)}, u32[]{:S(2)}, u32[]{:S(2)}) collective-permute-start(bf16[2,704,128]{2,1,0:T(8,128)(2,1)S(1)} %pad_maximum_fusion.13), channel_id=1, source_target_pairs={{0,2},{2,0},{4,6},{6,4},{8,10},{10,8},{12,14},{14,12},{16,18},{18,... | collective-permute-start | bytes 1081352 | tf_op jit(solution)/shard_map/ppermute | solution.py:737
  270.7 14.5 %collective-permute-start.54 = (bf16[2,704,128]{2,1,0:T(8,128)(2,1)S(1)}, bf16[2,704,128]{2,1,0:T(8,128)(2,1)S(1)}, u32[]{:S(2)}, u32[]{:S(2)}) collective-permute-start(bf16[2,704,128]{2,1,0:T(8,128)(2,1)S(1)} %pad_maximum_fusion.12), channel_id=1, source_target_pairs={{0,8},{2,10},{4,12},{6,14},{8,0},{10,2},{12,4},{14,6},{16,24},{18,... | collective-permute-start | bytes 1081352 | tf_op jit(solution)/shard_map/ppermute | solution.py:737
  272.8 12.4 %collective-permute-start.57 = (bf16[2,352,128]{2,1,0:T(8,128)(2,1)S(1)}, bf16[2,352,128]{2,1,0:T(8,128)(2,1)S(1)}, u32[]{:S(2)}, u32[]{:S(2)}) collective-permute-start(bf16[2,352,128]{2,1,0:T(8,128)(2,1)S(1)} %get-tuple-element.465), channel_id=1, source_target_pairs={{0,8},{2,10},{4,12},{6,14},{8,0},{10,2},{12,4},{14,6},{16,24},{18,... | collective-permute-start | bytes 540680 | tf_op jit(solution)/shard_map/ppermute | solution.py:737
  285.5 18.7 %collective-permute-start.62 = (bf16[4,704,128]{2,1,0:T(8,128)(2,1)S(1)}, bf16[4,704,128]{2,1,0:T(8,128)(2,1)S(1)}, u32[]{:S(2)}, u32[]{:S(2)}) collective-permute-start(bf16[4,704,128]{2,1,0:T(8,128)(2,1)S(1)} %pad_maximum_fusion.6), channel_id=1, source_target_pairs={{0,2},{2,0},{4,6},{6,4},{8,10},{10,8},{12,14},{14,12},{16,18},{18,... | collective-permute-start | bytes 2162696 | tf_op jit(solution)/shard_map/ppermute | solution.py:737
  287.2 22.6 %collective-permute-start.61 = (bf16[4,704,128]{2,1,0:T(8,128)(2,1)S(1)}, bf16[4,704,128]{2,1,0:T(8,128)(2,1)S(1)}, u32[]{:S(2)}, u32[]{:S(2)}) collective-permute-start(bf16[4,704,128]{2,1,0:T(8,128)(2,1)S(1)} %pad_maximum_fusion.5), channel_id=1, source_target_pairs={{0,8},{2,10},{4,12},{6,14},{8,0},{10,2},{12,4},{14,6},{16,24},{18,... | collective-permute-start | bytes 2162696 | tf_op jit(solution)/shard_map/ppermute | solution.py:737
  287.2 22.6 %collective-permute-start.60 = (bf16[4,704,128]{2,1,0:T(8,128)(2,1)S(1)}, bf16[4,704,128]{2,1,0:T(8,128)(2,1)S(1)}, u32[]{:S(2)}, u32[]{:S(2)}) collective-permute-start(bf16[4,704,128]{2,1,0:T(8,128)(2,1)S(1)} %pad_maximum_fusion.4), channel_id=1, source_target_pairs={{0,4},{2,6},{4,0},{6,2},{8,12},{10,14},{12,8},{14,10},{16,20},{18,... | collective-permute-start | bytes 2162696 | tf_op jit(solution)/shard_map/ppermute | solution.py:737
  287.7 16.4 %collective-permute-start.63 = (bf16[1,1072,128]{2,1,0:T(8,128)(2,1)S(1)}, bf16[1,1072,128]{2,1,0:T(8,128)(2,1)S(1)}, u32[]{:S(2)}, u32[]{:S(2)}) collective-permute-start(bf16[1,1072,128]{2,1,0:T(8,128)(2,1)S(1)} %pad_maximum_fusion.17), channel_id=1, source_target_pairs={{0,16},{2,18},{4,20},{6,22},{8,24},{10,26},{12,28},{14,30},{16,0},... | collective-permute-start | bytes 823304 | tf_op jit(solution)/shard_map/ppermute | solution.py:737
  310.2 29.9 %collective-permute-start.66 = (bf16[8,704,128]{2,1,0:T(8,128)(2,1)S(1)}, bf16[8,704,128]{2,1,0:T(8,128)(2,1)S(1)}, u32[]{:S(2)}, u32[]{:S(2)}) collective-permute-start(bf16[8,704,128]{2,1,0:T(8,128)(2,1)S(1)} %pad_maximum_fusion.2.own_ref), channel_id=1, source_target_pairs={{0,8},{2,10},{4,12},{6,14},{8,0},{10,2},{12,4},{14,6},{16,24},{18,... | collective-permute-start | bytes 4325384 | tf_op jit(solution)/shard_map/ppermute | solution.py:737
  310.3 29.8 %collective-permute-start.65 = (bf16[8,704,128]{2,1,0:T(8,128)(2,1)S(1)}, bf16[8,704,128]{2,1,0:T(8,128)(2,1)S(1)}, u32[]{:S(2)}, u32[]{:S(2)}) collective-permute-start(bf16[8,704,128]{2,1,0:T(8,128)(2,1)S(1)} %pad_maximum_fusion.1.own_ref), channel_id=1, source_target_pairs={{0,4},{2,6},{4,0},{6,2},{8,12},{10,14},{12,8},{14,10},{16,20},{18,... | collective-permute-start | bytes 4325384 | tf_op jit(solution)/shard_map/ppermute | solution.py:737
  311.1 29.0 %collective-permute-start.64 = (bf16[8,704,128]{2,1,0:T(8,128)(2,1)S(1)}, bf16[8,704,128]{2,1,0:T(8,128)(2,1)S(1)}, u32[]{:S(2)}, u32[]{:S(2)}) collective-permute-start(bf16[8,704,128]{2,1,0:T(8,128)(2,1)S(1)} %pad_maximum_fusion.own_ref), channel_id=1, source_target_pairs={{0,2},{2,0},{4,6},{6,4},{8,10},{10,8},{12,14},{14,12},{16,18},{18,... | collective-permute-start | bytes 4325384 | tf_op jit(solution)/shard_map/ppermute | solution.py:737
  313.0 25.3 %collective-permute-start.67 = (bf16[1,1072,128]{2,1,0:T(8,128)(2,1)S(1)}, bf16[1,1072,128]{2,1,0:T(8,128)(2,1)S(1)}, u32[]{:S(2)}, u32[]{:S(2)}) collective-permute-start(bf16[1,1072,128]{2,1,0:T(8,128)(2,1)S(1)} %pad_maximum_fusion.18), channel_id=1, source_target_pairs={{0,16},{2,18},{4,20},{6,22},{8,24},{10,26},{12,28},{14,30},{16,0},... | collective-permute-start | bytes 823304 | tf_op jit(solution)/shard_map/ppermute | solution.py:737
  340.2 8.2 %collective-permute-start.70 = (bf16[2,368,128]{2,1,0:T(8,128)(2,1)S(1)}, bf16[2,368,128]{2,1,0:T(8,128)(2,1)S(1)}, u32[]{:S(2)}, u32[]{:S(2)}) collective-permute-start(bf16[2,368,128]{2,1,0:T(8,128)(2,1)S(1)} %pad_maximum_fusion.19), channel_id=1, source_target_pairs={{0,4},{2,6},{4,0},{6,2},{8,12},{10,14},{12,8},{14,10},{16,20},{18,... | collective-permute-start | bytes 565256 | tf_op jit(solution)/shard_map/ppermute | solution.py:737
  348.4 14.8 %collective-permute-start.73 = (bf16[4,368,128]{2,1,0:T(8,128)(2,1)S(1)}, bf16[4,368,128]{2,1,0:T(8,128)(2,1)S(1)}, u32[]{:S(2)}, u32[]{:S(2)}) collective-permute-start(bf16[4,368,128]{2,1,0:T(8,128)(2,1)S(1)} %pad_maximum_fusion.11), channel_id=1, source_target_pairs={{0,2},{2,0},{4,6},{6,4},{8,10},{10,8},{12,14},{14,12},{16,18},{18,... | collective-permute-start | bytes 1130504 | tf_op jit(solution)/shard_map/ppermute | solution.py:737
  349.8 11.4 %collective-permute-start.72 = (bf16[4,352,128]{2,1,0:T(8,128)(2,1)S(1)}, bf16[4,352,128]{2,1,0:T(8,128)(2,1)S(1)}, u32[]{:S(2)}, u32[]{:S(2)}) collective-permute-start(bf16[4,352,128]{2,1,0:T(8,128)(2,1)S(1)} %pad_maximum_fusion.16), channel_id=1, source_target_pairs={{0,8},{2,10},{4,12},{6,14},{8,0},{10,2},{12,4},{14,6},{16,24},{18,... | collective-permute-start | bytes 1081352 | tf_op jit(solution)/shard_map/ppermute | solution.py:737
  351.9 11.4 %collective-permute-start.71 = (bf16[4,352,128]{2,1,0:T(8,128)(2,1)S(1)}, bf16[4,352,128]{2,1,0:T(8,128)(2,1)S(1)}, u32[]{:S(2)}, u32[]{:S(2)}) collective-permute-start(bf16[4,352,128]{2,1,0:T(8,128)(2,1)S(1)} %pad_maximum_fusion.15), channel_id=1, source_target_pairs={{0,4},{2,6},{4,0},{6,2},{8,12},{10,14},{12,8},{14,10},{16,20},{18,... | collective-permute-start | bytes 1081352 | tf_op jit(solution)/shard_map/ppermute | solution.py:737
  363.5 12.2 %collective-permute-start.76 = (bf16[8,368,128]{2,1,0:T(8,128)(2,1)S(1)}, bf16[8,368,128]{2,1,0:T(8,128)(2,1)S(1)}, u32[]{:S(2)}, u32[]{:S(2)}) collective-permute-start(bf16[8,368,128]{2,1,0:T(8,128)(2,1)S(1)} %pad_maximum_fusion.3.o2), channel_id=1, source_target_pairs={{0,8},{2,10},{4,12},{6,14},{8,0},{10,2},{12,4},{14,6},{16,24},{18,... | collective-permute-start | bytes 2261000 | tf_op jit(solution)/shard_map/ppermute | solution.py:737
  363.7 11.4 %collective-permute-start.75 = (bf16[8,352,128]{2,1,0:T(8,128)(2,1)S(1)}, bf16[8,352,128]{2,1,0:T(8,128)(2,1)S(1)}, u32[]{:S(2)}, u32[]{:S(2)}) collective-permute-start(bf16[8,352,128]{2,1,0:T(8,128)(2,1)S(1)} %pad_maximum_fusion.8.o1), channel_id=1, source_target_pairs={{0,4},{2,6},{4,0},{6,2},{8,12},{10,14},{12,8},{14,10},{16,20},{18,... | collective-permute-start | bytes 2162696 | tf_op jit(solution)/shard_map/ppermute | solution.py:737
  364.3 11.3 %collective-permute-start.74 = (bf16[8,352,128]{2,1,0:T(8,128)(2,1)S(1)}, bf16[8,352,128]{2,1,0:T(8,128)(2,1)S(1)}, u32[]{:S(2)}, u32[]{:S(2)}) collective-permute-start(bf16[8,352,128]{2,1,0:T(8,128)(2,1)S(1)} %pad_maximum_fusion.7.o0), channel_id=1, source_target_pairs={{0,2},{2,0},{4,6},{6,4},{8,10},{10,8},{12,14},{14,12},{16,18},{18,... | collective-permute-start | bytes 2162696 | tf_op jit(solution)/shard_map/ppermute | solution.py:737
  (75 other events, 676.1 us)
